TPU v7x, 32 devices: a whole 2x2x4 slice. The times are simulated.
32 devices in a mesh: rep: 2 (over x), shard: 4 (over y, core), tp: 4 (over z).
Axes of the slice: x: 2, y: 2, z: 4, core: 2. Of those that a mesh axis runs over, the one named last changes fastest.
Arguments:
- tokens: bfloat16 [16, 448, 1024], P(('rep', 'shard'), 'tp'), may hold values from -6 to 6
- encoded: bfloat16 [16, 1500, 1024], P(('rep', 'shard')), may hold values from -6 to 6
- cotangent: bfloat16 [16, 448, 1024], P(('rep', 'shard'), 'tp'), may hold values from -6 to 6
- adapter_of: int32 [16], P(('rep', 'shard')), may hold values from 0 to 7
- w_attn_in: bfloat16 [1, 2, 3, 1024, 1024], P(None, None, None, 'shard', 'tp'), may hold values from -0.1875 to 0.1875
- w_attn_out: bfloat16 [1, 2, 1024, 1024], P(None, None, 'tp', 'shard'), may hold values from -0.75 to 0.75
- w_up: bfloat16 [1, 1024, 4096], P(None, 'shard', 'tp'), may hold values from -0.1875 to 0.1875
- w_down: bfloat16 [1, 4096, 1024], P(None, 'tp', 'shard'), may hold values from -0.09375 to 0.09375
- norm_gain: float32 [1, 3, 1024], replicated, may hold values from 0.1 to 1.9
- norm_shift: float32 [1, 3, 1024], replicated, may hold values from -1.2 to 1.2
- down_attn_in: bfloat16 [1, 2, 3, 128, 1024], P(None, None, None, 'shard'), may hold values from -0.1875 to 0.1875
- up_attn_in: bfloat16 [1, 2, 3, 128, 1024], P(None, None, None, 'shard', 'tp'), may hold values from -0.75 to 0.75
- down_feed_in: bfloat16 [1, 128, 1024], P(None, 'shard'), may hold values from -0.1875 to 0.1875
- up_feed_in: bfloat16 [1, 128, 4096], P(None, 'shard', 'tp'), may hold values from -0.75 to 0.75
- down_attn_out: bfloat16 [1, 2, 128, 1024], P(None, None, 'shard', 'tp'), may hold values from -0.1875 to 0.1875
- up_attn_out: bfloat16 [1, 2, 128, 1024], P(None, None, 'shard'), may hold values from -0.75 to 0.75
- down_feed_out: bfloat16 [1, 128, 4096], P(None, 'shard', 'tp'), may hold values from -0.09375 to 0.09375
- up_feed_out: bfloat16 [1, 128, 1024], P(None, 'shard'), may hold values from -0.75 to 0.75
Outputs:
- activations: bfloat16 [16, 448, 1024], P(('rep', 'shard'), 'tp')
- grad_tokens: float32 [16, 448, 1024], P(('rep', 'shard'), 'tp')
- grad_encoded: float32 [16, 1500, 1024], P(('rep', 'shard'), 'tp')
- grad_down_attn_in: float32 [1, 2, 3, 128, 1024], P(None, None, None, ('shard', 'tp'))
- grad_up_attn_in: float32 [1, 2, 3, 128, 1024], P(None, None, None, 'shard', 'tp')
- grad_down_feed_in: float32 [1, 128, 1024], P(None, ('shard', 'tp'))
- grad_up_feed_in: float32 [1, 128, 4096], P(None, 'shard', 'tp')
- grad_down_attn_out: float32 [1, 2, 128, 1024], P(None, None, 'shard', 'tp')
- grad_up_attn_out: float32 [1, 2, 128, 1024], P(None, None, ('shard', 'tp'))
- grad_down_feed_out: float32 [1, 128, 4096], P(None, 'shard', 'tp')
- grad_up_feed_out: float32 [1, 128, 1024], P(None, ('shard', 'tp'))
All inputs are finite; a program needn't handle non-finite values.
Results may differ from a plain program's by a relative error of at most 0.017.
The roundings to bfloat16 on the way count: a program that leaves them out, or rounds other values in their place, can miss the bound.
Values may be sent and summed in bfloat16 or wider, within the bound.
A program may use at most 192 MiB of HBM per device.

v0:
```python
from functools import partial

import jax
import jax.numpy as jnp
from jax import lax
from jax.sharding import PartitionSpec as P

HD = 64
ADAPTERS = 8
RANK = 16
LAYERS = 1


precise = lax.Precision.HIGHEST
epsilon = 1e-05
masked_score = -1e30


def layer_norm(inputs, gain_row, shift_row):
    centered = inputs - jnp.mean(inputs, axis=-1, keepdims=True)
    variance = jnp.mean(centered * centered, axis=-1, keepdims=True)
    return centered * lax.rsqrt(variance + epsilon) * gain_row + shift_row


def pick(rows, chosen):
    return jnp.take(rows.reshape(ADAPTERS, RANK, rows.shape[-1]), chosen, axis=0)


def spread(per_clip, chosen):
    onehot = (jnp.arange(ADAPTERS, dtype=jnp.int32)[None, :] == chosen[:, None]).astype(jnp.float32)
    summed = jnp.einsum("ca,crk->ark", onehot, per_clip, precision=precise)
    return summed.reshape(ADAPTERS * RANK, per_clip.shape[-1])


def down_grad(grad_rank, inputs, chosen):
    return spread(
        jnp.einsum("ctr,ctd->crd", grad_rank, inputs.astype(jnp.float32), precision=precise), chosen
    )


def up_grad(inner_rank, upstream, chosen):
    return spread(
        jnp.einsum("ctr,ctp->crp", inner_rank, upstream.astype(jnp.float32), precision=precise),
        chosen,
    )


def project(inputs, weight, down_rows, up_rows, chosen):
    inner_rank = jnp.einsum(
        "ctd,crd->ctr", inputs, pick(down_rows, chosen), preferred_element_type=jnp.float32
    )
    main_term = jnp.einsum("ctd,dp->ctp", inputs, weight, preferred_element_type=jnp.float32)
    return (
        main_term
        + jnp.einsum(
            "ctr,crp->ctp", inner_rank, pick(up_rows, chosen).astype(jnp.float32), precision=precise
        ),
        inner_rank,
    )


def project_back(weight, down_rows, up_rows, chosen, upstream):
    grad_rank = jnp.einsum(
        "ctp,crp->ctr", upstream, pick(up_rows, chosen), preferred_element_type=jnp.float32
    )
    grad_inputs = jnp.einsum("ctp,dp->ctd", upstream, weight, preferred_element_type=jnp.float32)
    grad_inputs = grad_inputs + jnp.einsum(
        "ctr,crd->ctd", grad_rank, pick(down_rows, chosen).astype(jnp.float32), precision=precise
    )
    return (grad_inputs, grad_rank)


def split_heads(rows):
    return rows.reshape(rows.shape[0], rows.shape[1], rows.shape[2] // HD, HD)


def make_scores(query_heads, key_heads, causal):
    scores = jnp.einsum(
        "cqhe,ckhe->chqk", query_heads, key_heads, preferred_element_type=jnp.float32
    ) * HD ** (-0.5)
    if causal:
        allowed = (
            jnp.arange(query_heads.shape[1])[:, None] >= jnp.arange(key_heads.shape[1])[None, :]
        )
        scores = jnp.where(allowed, scores, masked_score)
    return scores


def attend_forward(queries, keys_in, values_in, causal):
    scores = make_scores(split_heads(queries), split_heads(keys_in), causal)
    highest = jnp.max(scores, axis=-1, keepdims=True)
    expanded = jnp.exp(scores - highest)
    totals = jnp.sum(expanded, axis=-1, keepdims=True)
    attention = (expanded / totals).astype(jnp.bfloat16)
    mixture = jnp.einsum(
        "chqk,ckhe->cqhe", attention, split_heads(values_in), preferred_element_type=jnp.float32
    )
    return (mixture.reshape(queries.shape).astype(jnp.bfloat16), highest + jnp.log(totals))


def attend_backward(queries, keys_in, values_in, log_total, grad_mixture, causal):
    query_heads = split_heads(queries)
    key_heads = split_heads(keys_in)
    value_heads = split_heads(values_in)
    grad_heads = split_heads(grad_mixture)
    attention = jnp.exp(make_scores(query_heads, key_heads, causal) - log_total)
    grad_values = jnp.einsum(
        "chqk,cqhe->ckhe",
        attention.astype(jnp.bfloat16),
        grad_heads,
        preferred_element_type=jnp.float32,
    )
    grad_attention = jnp.einsum(
        "cqhe,ckhe->chqk", grad_heads, value_heads, preferred_element_type=jnp.float32
    )
    grad_scores = attention * (
        grad_attention - jnp.sum(attention * grad_attention, axis=-1, keepdims=True)
    )
    grad_scores = grad_scores.astype(jnp.bfloat16)
    grad_queries = jnp.einsum(
        "chqk,ckhe->cqhe", grad_scores, key_heads, preferred_element_type=jnp.float32
    ) * HD ** (-0.5)
    grad_keys = jnp.einsum(
        "chqk,cqhe->ckhe", grad_scores, query_heads, preferred_element_type=jnp.float32
    ) * HD ** (-0.5)
    return (
        grad_queries.reshape(queries.shape).astype(jnp.bfloat16),
        grad_keys.reshape(keys_in.shape).astype(jnp.bfloat16),
        grad_values.reshape(values_in.shape).astype(jnp.bfloat16),
    )


def gather_rows(rows):
    return lax.all_gather(rows, "tp", axis=1, tiled=True)


def scatter_rows(terms):
    return lax.psum_scatter(terms, "tp", scatter_dimension=1, tiled=True)


def gather_grads(rows):
    return lax.all_gather(rows, "tp", axis=1, tiled=True)


def scatter_grads(terms):
    return lax.psum_scatter(terms, "tp", scatter_dimension=1, tiled=True)


def quarter(rows):
    width = rows.shape[-1] // lax.axis_size("tp")
    return lax.dynamic_slice_in_dim(rows, lax.axis_index("tp") * width, width, rows.ndim - 1)


def adapter_grads(local_in, local_out, rank_list, source_list, out_inner, upstream, chosen):
    summed = lax.psum(tuple(rank_list) + (out_inner,), "tp")
    shared_in = jnp.stack(
        [
            down_grad(summed[position], quarter(source_list[position]), chosen)
            for position in range(len(rank_list))
        ]
    )
    shared_out = up_grad(summed[len(rank_list)], quarter(upstream), chosen)
    parts = (
        lax.psum_scatter(local_in, "shard", scatter_dimension=1, tiled=True),
        lax.psum_scatter(local_out, "shard", scatter_dimension=0, tiled=True),
        lax.psum_scatter(shared_in, "shard", scatter_dimension=1, tiled=True),
        lax.psum_scatter(shared_out[None], "shard", scatter_dimension=1, tiled=True),
    )
    moved = (
        lax.all_to_all(parts[2], "tp", split_axis=1, concat_axis=2, tiled=True),
        lax.all_to_all(parts[3], "tp", split_axis=1, concat_axis=2, tiled=True),
    )
    combined = (parts[0], parts[1], moved[0], moved[1][0])
    combined = tuple(lax.psum((combined[0], combined[1], combined[2], combined[3]), "rep"))
    return combined


def on_device(
    tokens,
    encoded,
    cotangent,
    adapter_of,
    w_attn_in,
    w_attn_out,
    w_up,
    w_down,
    norm_gain,
    norm_shift,
    down_attn_in,
    up_attn_in,
    down_feed_in,
    up_feed_in,
    down_attn_out,
    up_attn_out,
    down_feed_out,
    up_feed_out,
):

    def fetch_attention(layer_index, side_index):
        return (
            lax.all_gather(w_attn_in[layer_index, side_index], "shard", axis=1, tiled=True),
            lax.all_gather(w_attn_out[layer_index, side_index], "shard", axis=1, tiled=True),
            lax.all_gather(down_attn_in[layer_index, side_index], "shard", axis=1, tiled=True),
            lax.all_gather(up_attn_in[layer_index, side_index], "shard", axis=1, tiled=True),
            lax.all_gather(down_attn_out[layer_index, side_index], "shard", axis=0, tiled=True),
            lax.all_gather(up_attn_out[layer_index, side_index], "shard", axis=0, tiled=True),
        )

    def fetch_feed(layer_index):
        return (
            lax.all_gather(w_up[layer_index], "shard", axis=0, tiled=True),
            lax.all_gather(w_down[layer_index], "shard", axis=1, tiled=True),
            lax.all_gather(down_feed_in[layer_index], "shard", axis=0, tiled=True),
            lax.all_gather(up_feed_in[layer_index], "shard", axis=0, tiled=True),
            lax.all_gather(down_feed_out[layer_index], "shard", axis=0, tiled=True),
            lax.all_gather(up_feed_out[layer_index], "shard", axis=0, tiled=True),
        )

    def norm_back(hidden_in, layer_index, which_norm, grad_rows):
        _, pullback = jax.vjp(
            lambda inputs: layer_norm(
                inputs, norm_gain[layer_index, which_norm], norm_shift[layer_index, which_norm]
            ),
            hidden_in,
        )
        return pullback(grad_rows)[0]

    hidden = tokens.astype(jnp.float32)
    kept_state = {}
    layer_index = 0
    for side_index in range(2):
        fetched = fetch_attention(layer_index, side_index)
        w_in, w_out, down_in, up_in, down_out, up_out = fetched
        normed = gather_rows(
            layer_norm(
                hidden, norm_gain[layer_index, side_index], norm_shift[layer_index, side_index]
            ).astype(jnp.bfloat16)
        )
        source = normed if side_index == 0 else encoded
        queries, query_inner = project(normed, w_in[0], down_in[0], up_in[0], adapter_of)
        keys_out, key_inner = project(source, w_in[1], down_in[1], up_in[1], adapter_of)
        values_out, value_inner = project(source, w_in[2], down_in[2], up_in[2], adapter_of)
        projected = (
            queries.astype(jnp.bfloat16),
            keys_out.astype(jnp.bfloat16),
            values_out.astype(jnp.bfloat16),
        )
        mixture, log_total = attend_forward(
            projected[0], projected[1], projected[2], side_index == 0
        )
        branch, out_inner = project(mixture, w_out, down_out, up_out, adapter_of)
        kept_state[layer_index, side_index] = (
            hidden,
            normed,
            (query_inner, key_inner, value_inner),
            projected,
            log_total,
            mixture,
            out_inner,
            None,
        )
        hidden = hidden + scatter_rows(branch)
    fetched = fetch_feed(layer_index)
    w_in, w_out, down_in, up_in, down_out, up_out = fetched
    normed = gather_rows(
        layer_norm(hidden, norm_gain[layer_index, 2], norm_shift[layer_index, 2]).astype(
            jnp.bfloat16
        )
    )
    pre_active, in_inner = project(normed, w_in, down_in, up_in, adapter_of)
    active = jax.nn.gelu(pre_active, approximate=False).astype(jnp.bfloat16)
    branch, out_inner = project(active, w_out, down_out, up_out, adapter_of)
    kept_state[layer_index, 2] = (hidden, normed, in_inner, pre_active, active, out_inner, None)
    hidden = hidden + scatter_rows(branch)
    activations = hidden.astype(jnp.bfloat16)
    grad_hidden = cotangent.astype(jnp.float32)
    grad_memory = jnp.zeros(encoded.shape, jnp.float32)
    results = {}
    for layer_index in reversed(range(LAYERS)):
        hidden_in, normed, in_inner, pre_active, active, out_inner, fetched = kept_state[
            layer_index, 2
        ]
        fetched = fetch_feed(layer_index)
        w_in, w_out, down_in, up_in, down_out, up_out = fetched
        upstream = gather_grads(grad_hidden.astype(jnp.bfloat16))
        grad_active, out_rank = project_back(w_out, down_out, up_out, adapter_of, upstream)
        _, gelu_back = jax.vjp(partial(jax.nn.gelu, approximate=False), pre_active)
        grad_pre = gelu_back(grad_active)[0].astype(jnp.bfloat16)
        grad_normed, in_rank = project_back(w_in, down_in, up_in, adapter_of, grad_pre)
        grad_hidden = grad_hidden + norm_back(hidden_in, layer_index, 2, scatter_grads(grad_normed))
        local_in = up_grad(in_inner, grad_pre, adapter_of)[None]
        local_out = down_grad(out_rank, active, adapter_of)
        results[layer_index, 2] = adapter_grads(
            local_in, local_out, [in_rank], [normed], out_inner, upstream, adapter_of
        )
        for side_index in (1, 0):
            hidden_in, normed, inners, projected, log_total, mixture, out_inner, fetched = (
                kept_state[layer_index, side_index]
            )
            fetched = fetch_attention(layer_index, side_index)
            w_in, w_out, down_in, up_in, down_out, up_out = fetched
            source = normed if side_index == 0 else encoded
            upstream = gather_grads(grad_hidden.astype(jnp.bfloat16))
            grad_mixture, out_rank = project_back(w_out, down_out, up_out, adapter_of, upstream)
            grad_projected = attend_backward(
                projected[0],
                projected[1],
                projected[2],
                log_total,
                grad_mixture.astype(jnp.bfloat16),
                side_index == 0,
            )
            proj_grads = [
                project_back(
                    w_in[proj_index],
                    down_in[proj_index],
                    up_in[proj_index],
                    adapter_of,
                    grad_projected[proj_index],
                )
                for proj_index in range(3)
            ]
            sources = [normed, source, source]
            grad_source = proj_grads[1][0] + proj_grads[2][0]
            if side_index == 0:
                grad_normed = proj_grads[0][0] + grad_source
            else:
                grad_normed = proj_grads[0][0]
                grad_memory = grad_source
            grad_hidden = grad_hidden + norm_back(
                hidden_in, layer_index, side_index, scatter_grads(grad_normed)
            )
            local_in = jnp.stack(
                [
                    up_grad(inners[proj_index], grad_projected[proj_index], adapter_of)
                    for proj_index in range(3)
                ]
            )
            local_out = down_grad(out_rank, mixture, adapter_of)
            results[layer_index, side_index] = adapter_grads(
                local_in,
                local_out,
                [proj_grads[proj_index][1] for proj_index in range(3)],
                sources,
                out_inner,
                upstream,
                adapter_of,
            )
    grad_encoded = lax.psum_scatter(grad_memory, "tp", scatter_dimension=1, tiled=True)
    places = [(layer_index, side_index) for layer_index in range(LAYERS) for side_index in range(3)]
    flattened = tuple((member for entry_key in places for member in results[entry_key]))
    results = {
        entry_key: flattened[4 * position : 4 * position + 4]
        for position, entry_key in enumerate(places)
    }

    def stack_attention(member):
        return jnp.stack([jnp.stack([results[0, side_index][member] for side_index in range(2)])])

    def stack_feed(member):
        return jnp.stack([results[0, 2][member]])

    grad_down_attn_in = stack_attention(2)
    grad_up_attn_in = stack_attention(0)
    grad_down_feed_in = stack_feed(2)[:, 0]
    grad_up_feed_in = stack_feed(0)[:, 0]
    grad_down_attn_out = stack_attention(1)
    grad_up_attn_out = stack_attention(3)
    grad_down_feed_out = stack_feed(1)
    grad_up_feed_out = stack_feed(3)
    return (
        activations,
        grad_hidden,
        grad_encoded,
        grad_down_attn_in,
        grad_up_attn_in,
        grad_down_feed_in,
        grad_up_feed_in,
        grad_down_attn_out,
        grad_up_attn_out,
        grad_down_feed_out,
        grad_up_feed_out,
    )


def solution(mesh):
    placed = (
        P(("rep", "shard"), "tp", None),
        P(("rep", "shard"), None, None),
        P(("rep", "shard"), "tp", None),
        P(("rep", "shard")),
        P(None, None, None, "shard", "tp"),
        P(None, None, "tp", "shard"),
        P(None, "shard", "tp"),
        P(None, "tp", "shard"),
        P(),
        P(),
        P(None, None, None, "shard", None),
        P(None, None, None, "shard", "tp"),
        P(None, "shard", None),
        P(None, "shard", "tp"),
        P(None, None, "shard", "tp"),
        P(None, None, "shard", None),
        P(None, "shard", "tp"),
        P(None, "shard", None),
    )
    return jax.shard_map(
        on_device,
        mesh=mesh,
        in_specs=placed,
        out_specs=(
            P(("rep", "shard"), "tp", None),
            P(("rep", "shard"), "tp", None),
            P(("rep", "shard"), "tp", None),
            P(None, None, None, ("shard", "tp"), None),
            P(None, None, None, "shard", "tp"),
            P(None, ("shard", "tp"), None),
            P(None, "shard", "tp"),
            P(None, None, "shard", "tp"),
            P(None, None, ("shard", "tp"), None),
            P(None, "shard", "tp"),
            P(None, ("shard", "tp"), None),
        ),
        check_vma=False,
    )
```

profile of v0, /device:TPU:1, one launch (start us, length us, event | category | flops | bytes accessed | tf_op | source)
XLA Modules:
  0.0 1804.6 jit_solution(6378411094883966169)
XLA Ops:
  148.2 26.9 %reduce-scatter.19.cloned.1.call-done = f32[2,112,1024]{2,1,0:T(8,128)} async-done(((f32[2,448,1024]{2,1,0:T(8,128)}), f32[2,112,1024]{2,1,0:T(8,128)}) %reduce-scatter.19.cloned.1.call-update) | async-done | bytes 917520 | tf_op jit(solution)/shard_map/reduce_scatter | solution.py:138
  216.1 24.7 %all-gather.31.cloned.1.call-done = bf16[2,448,1024]{2,1,0:T(8,128)(2,1)} async-done(((bf16[2,112,1024]{2,1,0:T(8,128)(2,1)}), bf16[2,448,1024]{2,1,0:T(8,128)(2,1)}) %all-gather.31.cloned.1.call-update) | async-done | bytes 1835024 | tf_op jit(solution)/shard_map/all_gather | solution.py:134
  277.0 65.0 %reduce-scatter.21.cloned.1.call-done = f32[2,112,1024]{2,1,0:T(8,128)} async-done(((f32[2,448,1024]{2,1,0:T(8,128)}), f32[2,112,1024]{2,1,0:T(8,128)}) %reduce-scatter.21.cloned.1.call-update) | async-done | bytes 917520 | tf_op jit(solution)/shard_map/reduce_scatter | solution.py:138
  388.3 20.9 %all-gather.47.cloned.1.call-done = bf16[1,1024,1024]{2,1,0:T(8,128)(2,1)} async-done(((bf16[1,1024,256]{2,1,0:T(8,128)(2,1)}), bf16[1,1024,1024]{2,1,0:T(8,128)(2,1)}) %all-gather.47.cloned.1.call-update) | async-done | bytes 2097168 | tf_op jit(solution)/shard_map/all_gather | solution.py:212
  415.4 18.0 all-gather.45.cloned.1.call-done
  433.4 43.0 %all-gather.33.cloned.1.call-done = bf16[2,448,1024]{2,1,0:T(8,128)(2,1)} async-done(((bf16[2,112,1024]{2,1,0:T(8,128)(2,1)}), bf16[2,448,1024]{2,1,0:T(8,128)(2,1)}) %all-gather.33.cloned.1.call-update) | async-done | bytes 1835024 | tf_op jit(solution)/shard_map/all_gather | solution.py:134
  513.4 57.1 %reduce-scatter.25.cloned.1.call-done = f32[2,112,1024]{2,1,0:T(8,128)} async-done(((f32[2,448,1024]{2,1,0:T(8,128)}), f32[2,112,1024]{2,1,0:T(8,128)}) %reduce-scatter.25.cloned.1.call-update) | async-done | bytes 917520 | tf_op jit(solution)/shard_map/reduce_scatter | solution.py:146
  573.2 68.3 %reduce-scatter.23.cloned.1.call-done = f32[2,112,1024]{2,1,0:T(8,128)} async-done(((f32[2,448,1024]{2,1,0:T(8,128)}), f32[2,112,1024]{2,1,0:T(8,128)}) %reduce-scatter.23.cloned.1.call-update) | async-done | bytes 917520 | tf_op jit(solution)/shard_map/reduce_scatter | solution.py:138
  647.9 40.3 %all-gather.37.cloned.1.call-done = bf16[2,448,1024]{2,1,0:T(8,128)(2,1)} async-done(((bf16[2,112,1024]{2,1,0:T(8,128)(2,1)}), bf16[2,448,1024]{2,1,0:T(8,128)(2,1)}) %all-gather.37.cloned.1.call-update) | async-done | bytes 1835024 | tf_op jit(solution)/shard_map/all_gather | solution.py:142
  696.6 17.5 multiply_reduce_fusion
  747.1 58.7 %reduce-scatter.27.cloned.1.call-done = f32[2,112,1024]{2,1,0:T(8,128)} async-done(((f32[2,448,1024]{2,1,0:T(8,128)}), f32[2,112,1024]{2,1,0:T(8,128)}) %reduce-scatter.27.cloned.1.call-update) | async-done | bytes 917520 | tf_op jit(solution)/shard_map/reduce_scatter | solution.py:146
  895.2 19.7 %add_add_fusion = f32[2,1500,1024]{2,1,0:T(8,128)} fusion(f32[2,1500,1024]{2,1,0:T(8,128)} %fusion.77, f32[2,1500,1024]{2,1,0:T(8,128)} %fusion.81, f32[2,1500,1024]{2,1,0:T(8,128)} %fusion.149, f32[2,1500,16]{1,2,0:T(8,128)S(1)} %fusion.160, bf16[2,16,1024]{2,1,0:T(8,128)(2,1)S(1)} %copy-done.57, pred[2]{0:T(512)(128)(4,1)S(1)} %compare_and_fusion), kind=kOutput, calls=%fused_computation.28 | convolution fusion | flops 599072768 | bytes 49409536 | tf_op jit(solution)/shard_map/ctr,crd->ctd/dot_general | solution.py:67
  914.8 35.8 %copy.155 = f32[2,1500,1024]{2,0,1:T(2,128)} copy(f32[2,1500,1024]{2,1,0:T(8,128)} %add_add_fusion) | data formatting | bytes 24576000 | tf_op jit(solution)/shard_map/add | solution.py:324
  977.1 403.6 %all-reduce.12.cloned.1.call-done = (f32[2,1500,1024]{2,0,1:T(2,128)}, f32[2,1500,16]{1,2,0:T(8,128)}, f32[2,1500,16]{1,2,0:T(8,128)}) async-done(((f32[2,1500,1024]{2,0,1:T(2,128)}, f32[2,1500,16]{1,2,0:T(8,128)}, f32[2,1500,16]{1,2,0:T(8,128)}), (f32[2,1500,1024]{2,0,1:T(2,128)}, f32[2,1500,16]{1,2,0:T(8,128)}, f32[2,1500,16]{1,2,0:T(8,128)})) %all-reduce.12.cloned.1.call-update) | async-done | bytes 12672016
  1407.6 16.8 reduce-scatter.49.cloned.1.call-done
  1474.2 18.2 %reduce-scatter.31.cloned.1.call-done = f32[3,32,256]{2,1,0:T(8,128)} async-done(((f32[3,128,256]{2,1,0:T(8,128)}), f32[3,32,256]{2,1,0:T(8,128)}) %reduce-scatter.31.cloned.1.call-update) | async-done | bytes 98320 | tf_op jit(solution)/shard_map/reduce_scatter | solution.py:166
  1514.2 21.9 %reduce-scatter.43.cloned.1.call-done = f32[32,256]{1,0:T(8,128)} async-done(((f32[128,256]{1,0:T(8,128)}), f32[32,256]{1,0:T(8,128)}) %reduce-scatter.43.cloned.1.call-update) | async-done | bytes 32784 | tf_op jit(solution)/shard_map/reduce_scatter | solution.py:165
  1536.2 23.9 %reduce-scatter.33.cloned.1.call-done = f32[3,32,256]{2,1,0:T(8,128)} async-done(((f32[3,128,256]{2,1,0:T(8,128)}), f32[3,32,256]{2,1,0:T(8,128)}) %reduce-scatter.33.cloned.1.call-update) | async-done | bytes 98320 | tf_op jit(solution)/shard_map/reduce_scatter | solution.py:166
  1584.3 24.6 %reduce-scatter.51.cloned.1.call-done = f32[32,1024]{1,0:T(8,128)} async-done(((f32[128,1024]{1,0:T(8,128)}), f32[32,1024]{1,0:T(8,128)}) %reduce-scatter.51.cloned.1.call-update) | async-done | bytes 131088 | tf_op jit(solution)/shard_map/reduce_scatter | solution.py:165
  1608.9 23.5 %reduce-scatter.37.cloned.1.call-done = f32[3,32,256]{2,1,0:T(8,128)} async-done(((f32[3,128,256]{2,1,0:T(8,128)}), f32[3,32,256]{2,1,0:T(8,128)}) %reduce-scatter.37.cloned.1.call-update) | async-done | bytes 98320 | tf_op jit(solution)/shard_map/reduce_scatter | solution.py:164
  1632.4 23.5 %reduce-scatter.35.cloned.1.call-done = f32[3,32,256]{2,1,0:T(8,128)} async-done(((f32[3,128,256]{2,1,0:T(8,128)}), f32[3,32,256]{2,1,0:T(8,128)}) %reduce-scatter.35.cloned.1.call-update) | async-done | bytes 98320 | tf_op jit(solution)/shard_map/reduce_scatter | solution.py:164
  1657.9 24.4 %all-reduce.14.cloned.1.call-done = (f32[1,8,1024]{2,1,0:T(8,128)}, f32[1,32,256]{2,1,0:T(8,128)}, f32[1,32,256]{2,1,0:T(8,128)}, f32[1,8,1024]{2,1,0:T(8,128)},...) async-done(((f32[1,8,1024]{2,1,0:T(8,128)}, f32[1,32,256]{2,1,0:T(8,128)}, f32[1,32,256]{2,1,0:T(8,128)}, f32[1,8,1024]{2,1,0:T(8,128)}, f32[1,8,1024]{2,1,0:T(8,128)}, ...) | async-done | bytes 196624 | tf_op jit(solution)/shard_map/psum | solution.py:174
  1689.8 29.4 %all-reduce.16.cloned.1.call-done = (f32[1,3,8,1024]{3,2,1,0:T(8,128)}, f32[1,3,8,1024]{3,2,1,0:T(8,128)}, f32[1,3,32,256]{3,2,1,0:T(8,128)}, f32[1,3,32,256]{3,...) async-done(((f32[1,3,8,1024]{3,2,1,0:T(8,128)}, f32[1,3,8,1024]{3,2,1,0:T(8,128)}, f32[1,3,32,256]{3,2,1,0:T(8,128)}, f32[1,3,32,256]{3,2,1,0:T(8,128)}, ...) | async-done | bytes 655376 | tf_op jit(solution)/shard_map/psum | solution.py:174
  1722.5 67.3 %reduce-scatter.29.cloned.1.call-done = f32[2,112,1024]{2,1,0:T(8,128)} async-done(((f32[2,448,1024]{2,1,0:T(8,128)}), f32[2,112,1024]{2,1,0:T(8,128)}) %reduce-scatter.29.cloned.1.call-update) | async-done | bytes 917520 | tf_op jit(solution)/shard_map/reduce_scatter | solution.py:146
  (660 shorter events, 614.2 us)
Async XLA Ops:
  16.6 158.5 %reduce-scatter.19.cloned.1.call-start = ((), (), s32[]{:S(2)}) async-start(), calls=%async_computation.25 | async-start | bytes 4587520 | tf_op jit(solution)/shard_map/reduce_scatter | solution.py:138
  177.8 164.2 %reduce-scatter.21.cloned.1.call-start = ((), (), s32[]{:S(2)}) async-start(), calls=%async_computation.27 | async-start | bytes 4587520 | tf_op jit(solution)/shard_map/reduce_scatter | solution.py:138
  276.2 157.2 %all-gather.45.cloned.1.call-start = ((), (), s32[]{:S(2)}) async-start(), calls=%async_computation.50 | async-start | bytes 2621440 | tf_op jit(solution)/shard_map/all_gather | solution.py:211
  276.9 199.5 %all-gather.33.cloned.1.call-start = ((), (), s32[]{:S(2)}) async-start(), calls=%async_computation.28 | async-start | bytes 2293760 | tf_op jit(solution)/shard_map/all_gather | solution.py:134
  346.5 224.1 %reduce-scatter.25.cloned.1.call-start = ((), (), s32[]{:S(2)}) async-start(), calls=%async_computation.31 | async-start | bytes 4587520 | tf_op jit(solution)/shard_map/reduce_scatter | solution.py:146
  503.3 138.2 %reduce-scatter.23.cloned.1.call-start = ((), (), s32[]{:S(2)}) async-start(), calls=%async_computation.29 | async-start | bytes 4587520 | tf_op jit(solution)/shard_map/reduce_scatter | solution.py:138
  513.4 174.8 %all-gather.37.cloned.1.call-start = ((), (), s32[]{:S(2)}) async-start(), calls=%async_computation.32 | async-start | bytes 2293760 | tf_op jit(solution)/shard_map/all_gather | solution.py:142
  646.1 159.7 %reduce-scatter.27.cloned.1.call-start = ((), (), s32[]{:S(2)}) async-start(), calls=%async_computation.33 | async-start | bytes 4587520 | tf_op jit(solution)/shard_map/reduce_scatter | solution.py:146
  895.1 485.6 %all-reduce.12.cloned.1.call-start = ((), (), s32[]{:S(2)}) async-start(), calls=%async_computation.53 | async-start | bytes 25362432
  950.7 451.8 %reduce-scatter.39.cloned.1.call-start = ((), (), s32[]{:S(2)}) async-start(), calls=%async_computation.40 | async-start | bytes 163840 | tf_op jit(solution)/shard_map/reduce_scatter | solution.py:166
  956.5 467.9 %reduce-scatter.49.cloned.1.call-start = ((), (), s32[]{:S(2)}) async-start(), calls=%async_computation.45 | async-start | bytes 163840 | tf_op jit(solution)/shard_map/reduce_scatter | solution.py:167
  959.1 487.4 %reduce-scatter.47.cloned.1.call-start = ((), (), s32[]{:S(2)}) async-start(), calls=%async_computation.44 | async-start | bytes 163840 | tf_op jit(solution)/shard_map/reduce_scatter | solution.py:167
  960.5 508.0 %reduce-scatter.53.cloned.1.call-start = ((), (), s32[]{:S(2)}) async-start(), calls=%async_computation.47 | async-start | bytes 163840 | tf_op jit(solution)/shard_map/reduce_scatter | solution.py:167
  963.0 529.5 %reduce-scatter.31.cloned.1.call-start = ((), (), s32[]{:S(2)}) async-start(), calls=%async_computation.36 | async-start | bytes 491520 | tf_op jit(solution)/shard_map/reduce_scatter | solution.py:166
  964.6 549.6 %reduce-scatter.45.cloned.1.call-start = ((), (), s32[]{:S(2)}) async-start(), calls=%async_computation.43 | async-start | bytes 163840 | tf_op jit(solution)/shard_map/reduce_scatter | solution.py:165
  973.5 562.6 %reduce-scatter.43.cloned.1.call-start = ((), (), s32[]{:S(2)}) async-start(), calls=%async_computation.42 | async-start | bytes 163840 | tf_op jit(solution)/shard_map/reduce_scatter | solution.py:165
  975.2 584.9 %reduce-scatter.33.cloned.1.call-start = ((), (), s32[]{:S(2)}) async-start(), calls=%async_computation.37 | async-start | bytes 491520 | tf_op jit(solution)/shard_map/reduce_scatter | solution.py:166
  1386.8 197.5 %reduce-scatter.41.cloned.1.call-start = ((), (), s32[]{:S(2)}) async-start(), calls=%async_computation.41 | async-start | bytes 655360 | tf_op jit(solution)/shard_map/reduce_scatter | solution.py:164
  1389.4 219.5 %reduce-scatter.51.cloned.1.call-start = ((), (), s32[]{:S(2)}) async-start(), calls=%async_computation.46 | async-start | bytes 655360 | tf_op jit(solution)/shard_map/reduce_scatter | solution.py:165
  1393.6 238.8 %reduce-scatter.37.cloned.1.call-start = ((), (), s32[]{:S(2)}) async-start(), calls=%async_computation.39 | async-start | bytes 491520 | tf_op jit(solution)/shard_map/reduce_scatter | solution.py:164
  1398.8 257.0 %reduce-scatter.35.cloned.1.call-start = ((), (), s32[]{:S(2)}) async-start(), calls=%async_computation.38 | async-start | bytes 491520 | tf_op jit(solution)/shard_map/reduce_scatter | solution.py:164
  1498.4 183.9 %all-reduce.14.cloned.1.call-start = ((), (), s32[]{:S(2)}) async-start(), calls=%async_computation.54 | async-start | bytes 393216 | tf_op jit(solution)/shard_map/psum | solution.py:174
  1566.0 153.2 %all-reduce.16.cloned.1.call-start = ((), (), s32[]{:S(2)}) async-start(), calls=%async_computation.55 | async-start | bytes 1310720 | tf_op jit(solution)/shard_map/psum | solution.py:174
  1655.9 133.9 %reduce-scatter.29.cloned.1.call-start = ((), (), s32[]{:S(2)}) async-start(), calls=%async_computation.35 | async-start | bytes 4587520 | tf_op jit(solution)/shard_map/reduce_scatter | solution.py:146
  (174 other events, 5244.2 us)
Sparse Core Ops, SparseCore 0:
  10.2 26.0 all-gather.40
  38.5 41.2 all-gather.28
  108.0 67.0 reduce-scatter.18
  199.7 40.9 all-gather.30
  274.8 67.0 reduce-scatter.20
  343.5 41.9 all-gather.34
  387.1 22.1 all-gather.46
  410.8 22.5 all-gather.44
  435.4 40.9 all-gather.32
  503.4 67.0 reduce-scatter.24
  572.7 68.7 reduce-scatter.22
  646.2 41.9 all-gather.36
  738.6 67.0 reduce-scatter.26
  810.6 41.9 all-gather.38
  899.1 38.4 all-reduce.9
  950.8 429.8 all-reduce.11
  1471.2 21.2 reduce-scatter.30
  1538.8 21.2 reduce-scatter.32
  1562.6 21.6 reduce-scatter.40
  1587.2 21.6 reduce-scatter.50
  1635.0 20.8 reduce-scatter.34
  1659.6 22.6 all-reduce.13
  1686.3 32.8 all-reduce.15
  1721.5 68.2 reduce-scatter.28
  (8 shorter events, 156.5 us)
where the time goes:
time: 1810 us; the launch traced here: 1800 us
  waiting for transfers between devices  1200 us (66%)
  matrix products  259 us (14%)
  local copies, waits for them, and re-layouts  122 us (7%)
  blocking collectives  101 us (6%)
  other arithmetic  74.9 us (4%)
  starting transfers between devices  27.5 us (2%)
    unnamed x33, waiting for transfers between devices  408 us
    reduce_scatter x3, waiting for transfers between devices, scatter_grads(): return lax.psum_scatter(terms, 'tp', scatter_dimension=1, tiled=True)  183 us
    reduce_scatter x3, waiting for transfers between devices, scatter_rows(): return lax.psum_scatter(terms, 'tp', scatter_dimension=1, tiled=True)  160 us
    all_gather x3, waiting for transfers between devices, gather_rows(): return lax.all_gather(rows, 'tp', axis=1, tiled=True)  82 us
    reduce_scatter x3, waiting for transfers between devices, adapter_grads(): lax.psum_scatter(local_out, 'shard', scatter_dimension=0, tiled=True)  59.9 us
    reduce_scatter x3, waiting for transfers between devices, adapter_grads(): lax.psum_scatter(local_in, 'shard', scatter_dimension=1, tiled=True)  59.8 us
    psum x2, waiting for transfers between devices, adapter_grads(): lax.psum((combined[0], combined[1], combined[2], combined[3]), 'rep')  53.8 us
    dot_general x10, matrix products, project_back(): jnp.einsum('ctr,crd->ctd', grad_rank, pick(down_rows, chosen).astype(jnp....  53.7 us
  transfers between devices with their start and end apart: 38, of which 30 were waited for; matrix products, arithmetic and copies ran while one was open for 14% of the time, Pallas kernels for 0%

commit v1 on v0

v1 whole, which is shorter than its diff:
```python
from functools import partial

import jax
import jax.numpy as jnp
from jax import lax
from jax.sharding import Mesh, PartitionSpec as P

HD = 64
RANK = 16
epsilon = 1e-05
masked_score = -1e30
f32, bf16 = jnp.float32, jnp.bfloat16
SWAP = ((0, 1), (1, 0))


def dot(a, b, dims):
    return lax.dot_general(a, b, (dims, ((), ())), preferred_element_type=f32)


def mm(a, b):
    return dot(a, b, ((1,), (0,)))


def mm_t(a, b):
    return dot(a, b, ((1,), (1,)))


def t_mm(a, b):
    return dot(a, b, ((0,), (0,)))


def layer_norm(inputs, gain_row, shift_row):
    centered = inputs - jnp.mean(inputs, axis=-1, keepdims=True)
    variance = jnp.mean(centered * centered, axis=-1, keepdims=True)
    return centered * lax.rsqrt(variance + epsilon) * gain_row + shift_row


def norm_back(hidden, gain_row, shift_row, grad):
    return jax.vjp(lambda rows: layer_norm(rows, gain_row, shift_row), hidden)[1](grad)[0]


def heads_of(rows):
    return rows.reshape(rows.shape[0], rows.shape[1] // HD, HD)


def make_scores(queries, keys, causal):
    scores = jnp.einsum("qhe,khe->hqk", queries, keys, preferred_element_type=f32) * HD**-0.5
    if causal:
        allowed = jnp.arange(queries.shape[0])[:, None] >= jnp.arange(keys.shape[0])[None, :]
        scores = jnp.where(allowed, scores, masked_score)
    return scores


def attend_forward(queries, keys, values, causal):
    scores = make_scores(heads_of(queries), heads_of(keys), causal)
    highest = jnp.max(scores, axis=-1, keepdims=True)
    expanded = jnp.exp(scores - highest)
    totals = jnp.sum(expanded, axis=-1, keepdims=True)
    probs = (expanded / totals).astype(bf16)
    mixture = jnp.einsum("hqk,khe->qhe", probs, heads_of(values), preferred_element_type=f32)
    return mixture.reshape(queries.shape).astype(bf16), highest + jnp.log(totals)


def attend_backward(queries, keys, values, log_total, grad, causal):
    qh, kh, vh, gh = (heads_of(rows) for rows in (queries, keys, values, grad))
    probs = jnp.exp(make_scores(qh, kh, causal) - log_total)
    grad_values = jnp.einsum("hqk,qhe->khe", probs.astype(bf16), gh, preferred_element_type=f32)
    grad_probs = jnp.einsum("qhe,khe->hqk", gh, vh, preferred_element_type=f32)
    grad_scores = probs * (grad_probs - jnp.sum(probs * grad_probs, axis=-1, keepdims=True))
    grad_scores = grad_scores.astype(bf16)
    grad_queries = jnp.einsum("hqk,khe->qhe", grad_scores, kh, preferred_element_type=f32) * HD**-0.5
    grad_keys = jnp.einsum("hqk,qhe->khe", grad_scores, qh, preferred_element_type=f32) * HD**-0.5
    return (
        grad_queries.reshape(queries.shape).astype(bf16),
        grad_keys.reshape(keys.shape).astype(bf16),
        grad_values.reshape(values.shape).astype(bf16),
    )


def swap_core(rows):
    return lax.ppermute(rows, "core", SWAP)


def core_sum(part):
    return part + swap_core(part)


def own_and_other(stacked):
    core = lax.axis_index("core")
    keep = lax.dynamic_index_in_dim(stacked, core, 0, keepdims=False)
    send = lax.dynamic_index_in_dim(stacked, 1 - core, 0, keepdims=False)
    return keep, swap_core(send)


def in_core_order(own, other):
    first = lax.axis_index("core") == 0
    return jnp.stack([jnp.where(first, own, other), jnp.where(first, other, own)])


def scatter_sh(stacked):
    n = lax.axis_size("sh")
    if n == 2:
        me = lax.axis_index("sh")
        keep = lax.dynamic_index_in_dim(stacked, me, 0, keepdims=False)
        send = lax.dynamic_index_in_dim(stacked, 1 - me, 0, keepdims=False)
        return keep + lax.ppermute(send, "sh", SWAP)
    return lax.psum_scatter(stacked, "sh", scatter_dimension=0, tiled=False)


def over_z(stacked):
    return lax.all_to_all(stacked, "tp", 0, 0, tiled=True)


def half_columns(rows):
    width = rows.shape[-1] // 2
    return lax.dynamic_slice_in_dim(rows, lax.axis_index("core") * width, width, rows.ndim - 1)


def rows_home(half):
    tp = lax.axis_size("tp")
    moved = over_z(half.reshape(tp, half.shape[0] // tp, half.shape[1]))
    own, other = own_and_other(moved.reshape(2, tp // 2, *moved.shape[1:]))
    both = in_core_order(own, other)
    return jnp.moveaxis(both, 0, 2).reshape(both.shape[1], both.shape[2], 2 * half.shape[1])


def rows_here(rows):
    tp = lax.axis_size("tp")
    both = in_core_order(rows, swap_core(rows)).reshape(4, *rows.shape[1:])
    moved = over_z(half_columns(both))
    moved = moved.reshape(tp * rows.shape[1], rows.shape[2] // 2)
    pair = in_core_order(moved, swap_core(moved))
    return jnp.concatenate([pair[0], pair[1]], axis=-1)


def gather_weights(w_attn_in, w_attn_out, w_up, w_down):
    def over_shard(block, axis):
        return lax.all_gather(block, ("sh", "core"), axis=axis, tiled=True)

    def over_tp(block, axis):
        return lax.all_gather(block, "tp", axis=axis, tiled=True)

    core = lax.axis_index("core")

    def half(block, axis):
        width = block.shape[axis] // 2
        return lax.dynamic_slice_in_dim(block, core * width, width, axis)

    w_in = over_tp(half(over_shard(w_attn_in.reshape(6, *w_attn_in.shape[3:]), 1), 2), 2)
    w_out = over_tp(half(over_shard(w_attn_out[0], 2), 1), 1)
    w_first = over_tp(half(over_shard(w_up[0], 0), 1), 1)
    w_second = over_tp(half(over_shard(w_down[0], 1), 0), 0)
    return w_in, w_out, w_first, w_second


def on_device(
    tokens,
    encoded,
    cotangent,
    adapter_of,
    w_attn_in,
    w_attn_out,
    w_up,
    w_down,
    norm_gain,
    norm_shift,
    down_attn_in,
    up_attn_in,
    down_feed_in,
    up_feed_in,
    down_attn_out,
    up_attn_out,
    down_feed_out,
    up_feed_out,
):
    n, tp = lax.axis_size("sh"), lax.axis_size("tp")
    sh, core, z = lax.axis_index("sh"), lax.axis_index("core"), lax.axis_index("tp")
    width = w_attn_in.shape[3] * 2 * n
    held_rows = down_feed_in.shape[1]
    quarter = width // tp
    piece = quarter // 2

    ids = lax.all_gather(adapter_of, ("sh", "core"), tiled=True)

    row_ids = (sh * 2 + core) * held_rows + jnp.arange(held_rows)
    wanted = ids.reshape(n, tp)[:, :, None] * RANK + jnp.arange(RANK)
    picks = (wanted[..., None] == row_ids).astype(bf16)
    whole = jnp.concatenate(
        [
            down_attn_in.reshape(6, held_rows, width),
            down_feed_in,
            up_attn_out[0],
            up_feed_out,
        ]
    )
    def in_quarters(rows):
        return jnp.moveaxis(rows.reshape(held_rows, tp, quarter), 1, 0)

    split = jnp.concatenate(
        [
            up_attn_in.reshape(6, held_rows, quarter),
            in_quarters(up_feed_in[0]),
            down_attn_out[0],
            in_quarters(down_feed_out[0]),
        ]
    )
    picks_z = lax.dynamic_index_in_dim(picks, z, 1, keepdims=False)
    chosen_whole = jnp.einsum("srk,mkd->smrd", picks_z, whole, preferred_element_type=f32).astype(bf16)
    chosen_split = jnp.einsum("szrk,mkd->szmrd", picks, split, preferred_element_type=f32).astype(bf16)
    chosen_whole = core_sum(scatter_sh(chosen_whole))
    chosen_split = over_z(core_sum(scatter_sh(chosen_split)))

    def columns(first, count):
        mine = half_columns(chosen_split[:, first : first + count])
        return jnp.moveaxis(mine, 0, 2).reshape(count, RANK, tp * piece)

    def wide_columns(first):
        mine = lax.dynamic_slice_in_dim(chosen_split[:, first : first + tp], core * 2, 2, 1)
        return jnp.moveaxis(mine, 2, 0).reshape(RANK, tp * 2 * quarter)

    a_in, a_up, b_out, b_down = chosen_whole[:6], chosen_whole[6], chosen_whole[7:9], chosen_whole[9]
    b_in, b_up, a_out, a_down = columns(0, 6), wide_columns(6), columns(6 + tp, 2), wide_columns(8 + tp)

    w_in, w_out, w_first, w_second = gather_weights(w_attn_in, w_attn_out, w_up, w_down)

    def merge(weight, down_rows, up_rows):
        return (weight.astype(f32) + t_mm(down_rows, up_rows)).astype(bf16)

    w_in = [merge(w_in[i], a_in[i], b_in[i]) for i in range(6)]
    w_out = [merge(w_out[i], a_out[i], b_out[i]) for i in range(2)]
    w_first = merge(w_first, a_up, b_up)
    w_second = merge(w_second, a_down, b_down)

    hidden = rows_here(tokens).astype(f32)
    upstream = rows_here(cotangent)
    mine = lax.dynamic_index_in_dim(encoded, z % 2, 0, keepdims=False)
    memory = jnp.where(core == z // 2, mine, swap_core(mine))

    kept = []
    for side in range(2):
        normed = layer_norm(hidden, norm_gain[0, side], norm_shift[0, side]).astype(bf16)
        source = normed if side == 0 else memory
        queries = mm(normed, w_in[3 * side]).astype(bf16)
        keys = mm(source, w_in[3 * side + 1]).astype(bf16)
        values = mm(source, w_in[3 * side + 2]).astype(bf16)
        mixture, log_total = attend_forward(queries, keys, values, side == 0)
        kept.append((hidden, normed, source, queries, keys, values, mixture, log_total))
        hidden = hidden + core_sum(mm(mixture, w_out[side]))
    normed = layer_norm(hidden, norm_gain[0, 2], norm_shift[0, 2]).astype(bf16)
    pre_active = mm(normed, w_first)
    active = jax.nn.gelu(pre_active, approximate=False).astype(bf16)
    result = (hidden + core_sum(mm(active, w_second))).astype(bf16)
    activations = rows_home(half_columns(result))

    grad_hidden = upstream.astype(f32)
    grad_active = mm_t(upstream, w_second)
    _, gelu_back = jax.vjp(partial(jax.nn.gelu, approximate=False), pre_active)
    grad_pre = gelu_back(grad_active)[0].astype(bf16)
    grad_hidden = grad_hidden + norm_back(
        hidden, norm_gain[0, 2], norm_shift[0, 2], core_sum(mm_t(grad_pre, w_first))
    )

    def rank_grads(inputs, grad, down_rows, up_rows):
        inner = mm_t(inputs, down_rows).astype(bf16)
        back = mm_t(grad, up_rows).astype(bf16)
        return t_mm(back, inputs), t_mm(inner, grad)

    split_grads, whole_grads = [None] * 4, [None] * 4
    whole_grads[1], split_grads[1] = rank_grads(normed, grad_pre, a_up, b_up)
    split_grads[3], whole_grads[3] = rank_grads(active, upstream, a_down, b_down)
    in_whole, in_split, out_whole, out_split = [None] * 6, [None] * 6, [None] * 2, [None] * 2
    for side in (1, 0):
        hidden, normed, source, queries, keys, values, mixture, log_total = kept[side]
        upstream = grad_hidden.astype(bf16)
        grad_mixture = mm_t(upstream, w_out[side]).astype(bf16)
        out_split[side], out_whole[side] = rank_grads(mixture, upstream, a_out[side], b_out[side])
        grads = attend_backward(queries, keys, values, log_total, grad_mixture, side == 0)
        terms = [mm_t(grads[i], w_in[3 * side + i]) for i in range(3)]
        for i in range(3):
            inputs = normed if i == 0 else source
            in_whole[3 * side + i], in_split[3 * side + i] = rank_grads(
                inputs, grads[i], a_in[3 * side + i], b_in[3 * side + i]
            )
        if side == 1:
            part = (terms[1] + terms[2]).astype(bf16)
            own, other = own_and_other(jnp.moveaxis(part.reshape(part.shape[0], 2, -1), 1, 0))
            grad_encoded = rows_home((own.astype(f32) + other.astype(f32)).astype(bf16)).astype(f32)
            term = terms[0]
        else:
            term = terms[0] + terms[1] + terms[2]
        grad_hidden = grad_hidden + norm_back(
            hidden, norm_gain[0, side], norm_shift[0, side], core_sum(term)
        )
    grad_tokens = rows_home(half_columns(grad_hidden).astype(bf16)).astype(f32)

    def in_pieces(rows):
        return jnp.moveaxis(rows.reshape(RANK, tp, piece), 1, 0)[:, None]

    def in_wide_pieces(rows):
        return jnp.moveaxis(rows.reshape(RANK, tp, tp, piece), 0, 2)

    partial_whole = jnp.stack(in_whole + [whole_grads[1]] + out_whole + [whole_grads[3]]).astype(bf16)
    partial_whole = jnp.moveaxis(partial_whole.reshape(-1, RANK, tp, 2, piece), (3, 2), (0, 1))
    own, other = own_and_other(jnp.moveaxis(partial_whole, 2, 2))
    compact = jnp.concatenate(
        [in_pieces(rows) for rows in in_split]
        + [in_wide_pieces(split_grads[1])]
        + [in_pieces(rows) for rows in out_split]
        + [in_wide_pieces(split_grads[3])],
        axis=1,
    ).astype(bf16)
    compact = jnp.concatenate([compact, own + other], axis=1)
    compact = over_z(compact)
    here = ids.reshape(n, tp)[sh]
    rows = jnp.arange(2 * n * held_rows)
    place = (here[:, None] * RANK + jnp.arange(RANK))[None] == rows[:, None, None]
    dense = jnp.einsum("gkr,kmrp->gmp", place.astype(bf16), compact, preferred_element_type=f32)
    dense = dense.astype(bf16).reshape(n, 2, held_rows, *dense.shape[1:])
    dense = scatter_sh(dense)
    dense = dense + lax.ppermute(dense, "rep", SWAP)
    both = in_core_order(*own_and_other(dense))
    done = jnp.moveaxis(both, 0, 2)
    count = 8 + 2 * tp
    sums = done[:, :count].astype(f32)

    def narrow(first, number):
        block = sums[:, first : first + number].reshape(held_rows, number, quarter)
        return jnp.moveaxis(block, 1, 0)

    def wide(first):
        block = sums[:, first : first + tp].reshape(held_rows, 2, tp // 2, 2, piece)
        return block

    def wide_of(first):
        block = jnp.moveaxis(sums[:, first : first + tp], 2, 1)
        return block.reshape(held_rows, 2 * tp * piece)

    grad_up_attn_in = narrow(0, 6).reshape(1, 2, 3, held_rows, quarter)
    grad_up_feed_in = wide_of(6)[None]
    grad_down_attn_out = narrow(6 + tp, 2)[None]
    grad_down_feed_out = wide_of(8 + tp)[None]
    rest = done[:, count:].reshape(tp, held_rows // tp, 10, quarter)
    rest = jnp.moveaxis(over_z(rest), 0, 2)
    rest = jnp.moveaxis(rest.reshape(held_rows // tp, 10, width), 1, 0).astype(f32)
    return (
        activations,
        grad_tokens,
        grad_encoded,
        rest[:6].reshape(1, 2, 3, held_rows // tp, width),
        grad_up_attn_in,
        rest[6:7],
        grad_up_feed_in,
        grad_down_attn_out,
        rest[7:9][None],
        grad_down_feed_out,
        rest[9:10],
    )


def solution(mesh):
    rep, shard, tp = (mesh.shape[name] for name in ("rep", "shard", "tp"))
    fine = Mesh(mesh.devices.reshape(rep, shard // 2, 2, tp), ("rep", "sh", "core", "tp"))
    shard = ("sh", "core")
    clips = ("rep", "sh", "core")
    both = ("sh", "core", "tp")
    placed = (
        P(clips, "tp", None),
        P(clips, None, None),
        P(clips, "tp", None),
        P(clips),
        P(None, None, None, shard, "tp"),
        P(None, None, "tp", shard),
        P(None, shard, "tp"),
        P(None, "tp", shard),
        P(),
        P(),
        P(None, None, None, shard, None),
        P(None, None, None, shard, "tp"),
        P(None, shard, None),
        P(None, shard, "tp"),
        P(None, None, shard, "tp"),
        P(None, None, shard, None),
        P(None, shard, "tp"),
        P(None, shard, None),
    )
    return jax.shard_map(
        on_device,
        mesh=fine,
        in_specs=placed,
        out_specs=(
            P(clips, "tp", None),
            P(clips, "tp", None),
            P(clips, "tp", None),
            P(None, None, None, both, None),
            P(None, None, None, shard, "tp"),
            P(None, both, None),
            P(None, shard, "tp"),
            P(None, None, shard, "tp"),
            P(None, None, both, None),
            P(None, shard, "tp"),
            P(None, both, None),
        ),
        check_vma=False,
    )
```

time: 1810 us -> 801 us (0.44)
  waiting for transfers between devices: 1200 us -> 328 us
  blocking collectives: 101 us -> 3.12 us
  matrix products: 259 us -> 193 us
  starting transfers between devices: 27.5 us -> 53.9 us
    reduce_scatter x18 -> x0, waiting for transfers between devices: 555 us -> none  [the longest x3 183 us: scatter_grads(): return lax.psum_scatter(terms, 'tp', scatter_dimension=1, tiled=True)]
    unnamed x33 -> x8, waiting for transfers between devices: 408 us -> 2.65 us
    all_gather x14 -> x0, blocking collectives: 101 us -> none  [the longest x2 23.2 us: fetch_attention(): lax.all_gather(down_attn_in[layer_index, side_index], 'shard', axis=1, ti...]
    all_to_all x6 -> x8, waiting for transfers between devices: 4.16 us -> 76.6 us  [over_z(): return lax.all_to_all(stacked, 'tp', 0, 0, tiled=True)]
    dot_general x112 -> x65, matrix products: 259 us -> 193 us  [the longest x50 123 us: dot(): return lax.dot_general(a, b, (dims, ((), ())), preferred_element_type=f32)]
    all_gather x10 -> x8, waiting for transfers between devices: 182 us -> 240 us  [the longest x4 172 us: over_tp(): return lax.all_gather(block, 'tp', axis=axis, tiled=True)]
    psum x3 -> x0, waiting for transfers between devices: 53.8 us -> none  [the longest x2 53.8 us: adapter_grads(): lax.psum((combined[0], combined[1], combined[2], combined[3]), 'rep')]
    add x1, local copies, waits for them, and re-layouts: 35.8 us -> 0.84 us  [core_sum(): return part + swap_core(part)]
  transfers between devices with their start and end apart: 38 -> 39, of which waited for: 30 -> 15; matrix products, arithmetic and copies ran while one was open for 14% -> 43% of each run, Pallas kernels for 0% -> 0%
where the time goes in v1:
time: 801 us; the launch traced here: 793 us
  waiting for transfers between devices  328 us (41%)
  matrix products  193 us (24%)
  local copies, waits for them, and re-layouts  121 us (15%)
  other arithmetic  77.7 us (10%)
  starting transfers between devices  53.9 us (7%)
  between operations  17 us (2%)
    all_gather x4, waiting for transfers between devices, over_tp(): return lax.all_gather(block, 'tp', axis=axis, tiled=True)  172 us
    dot_general x50, matrix products, dot(): return lax.dot_general(a, b, (dims, ((), ())), preferred_element_type=f32)  123 us
    all_to_all x8, waiting for transfers between devices, over_z(): return lax.all_to_all(stacked, 'tp', 0, 0, tiled=True)  76.6 us
    all_gather x4, waiting for transfers between devices, over_shard(): return lax.all_gather(block, ('sh', 'core'), axis=axis, tiled=True)  67.6 us
    unnamed x314, local copies, waits for them, and re-layouts  31.6 us
    all_to_all x8, starting transfers between devices, over_z(): return lax.all_to_all(stacked, 'tp', 0, 0, tiled=True)  31.4 us
    dot_general x2, matrix products, attend_backward(): grad_probs = jnp.einsum('qhe,khe->hqk', gh, vh, preferred_element_type=f32)  22.5 us
    convert_element_type x2, other arithmetic, attend_backward(): grad_scores = grad_scores.astype(bf16)  20.3 us
  transfers between devices with their start and end apart: 39, of which 15 were waited for; matrix products, arithmetic and copies ran while one was open for 43% of the time, Pallas kernels for 0%

profile of v1, /device:TPU:1, one launch (start us, length us, event | category | flops | bytes accessed | tf_op | source)
XLA Modules:
  0.0 793.0 jit_solution(9697595662378190981)
XLA Ops:
  10.0 18.9 %all-gather.19.cloned.1.call-done = bf16[1,2,256,1024]{3,2,1,0:T(8,128)(2,1)} async-done(((bf16[1,2,256,256]{3,2,1,0:T(8,128)(2,1)}), bf16[1,2,256,1024]{3,2,1,0:T(8,128)(2,1)}) %all-gather.19.cloned.1.call-update) | async-done | bytes 1048592 | tf_op jit(solution)/shard_map/all_gather | solution.py:138
  31.0 28.1 %all-gather.15.cloned.1.call-done = bf16[6,1024,256]{2,1,0:T(8,128)(2,1)} async-done(((bf16[6,256,256]{2,1,0:T(8,128)(2,1)}), bf16[6,1024,256]{2,1,0:T(8,128)(2,1)}) %all-gather.15.cloned.1.call-update) | async-done | bytes 3145744 | tf_op jit(solution)/shard_map/all_gather | solution.py:138
  69.7 20.6 %all-gather.21.cloned.1.call-done = bf16[1,1024,1024]{2,1,0:T(8,128)(2,1)} async-done(((bf16[1,256,1024]{2,1,0:T(8,128)(2,1)}), bf16[1,1024,1024]{2,1,0:T(8,128)(2,1)}) %all-gather.21.cloned.1.call-update) | async-done | bytes 2097168 | tf_op jit(solution)/shard_map/all_gather | solution.py:138
  93.3 7.6 constant_dynamic-slice_fusion.9
  115.4 10.1 %all-to-all-done = bf16[4,112,512]{2,1,0:T(8,128)(2,1)S(1)} async-done(((bf16[4,112,512]{2,1,0:T(8,128)(2,1)}), bf16[4,112,512]{2,1,0:T(8,128)(2,1)S(1)}, u32[]{:S(2)}, u32[]{:S(2)}) %all-to-all-start) | async-done | bytes 458784 | tf_op jit(solution)/shard_map/all_to_all | solution.py:111
  135.5 19.5 %all-to-all-done.3 = bf16[4,112,512]{2,1,0:T(8,128)(2,1)} async-done(((bf16[4,112,512]{2,1,0:T(8,128)(2,1)}), bf16[4,112,512]{2,1,0:T(8,128)(2,1)}, u32[]{:S(2)}, u32[]{:S(2)}) %all-to-all-start.3) | async-done | bytes 458784 | tf_op jit(solution)/shard_map/all_to_all | solution.py:111
  163.6 20.9 %all-to-all-done.1 = bf16[4,16,16,256]{3,2,1,0:T(8,128)(2,1)S(1)} async-done(((bf16[4,16,16,256]{3,2,1,0:T(8,128)(2,1)}), bf16[4,16,16,256]{3,2,1,0:T(8,128)(2,1)S(1)}, u32[]{:S(2)}, u32[]{:S(2)}) %all-to-all-start.1) | async-done | bytes 524320 | tf_op jit(solution)/shard_map/all_to_all | solution.py:111
  199.8 104.4 %all-gather.17.cloned.1.call-done = bf16[6,1024,512]{2,1,0:T(8,128)(2,1)} async-done(((bf16[6,1024,128]{2,1,0:T(8,128)(2,1)}), bf16[6,1024,512]{2,1,0:T(8,128)(2,1)}) %all-gather.17.cloned.1.call-update) | async-done | bytes 6291472 | tf_op jit(solution)/shard_map/all_gather | solution.py:141
  366.3 5.7 fusion
  374.1 9.8 %fusion.51 = bf16[8,64,448]{2,1,0:T(8,128)(2,1)S(1)} fusion(bf16[1500,8,64]{0,2,1:T(8,128)(2,1)S(1)} %bitcast.690, f32[8,448,1500]{2,1,0:T(8,128)} %copy-done, f32[8,448]{1,0:T(8,128)S(1)} %fusion, f32[8,448]{1,0:T(8,128)S(1)} %get-tuple-element.109), kind=kOutput, calls=%fused_computation.119 | convolution fusion | flops 704485376 | bytes 23527424 | tf_op jit(solution)/shard_map/hqk,khe->qhe/dot_general | solution.py:60
  391.5 5.9 fusion.7
  397.4 68.0 %all-gather.29.cloned.1.call-done = bf16[1,2048,1024]{2,1,0:T(8,128)(2,1)} async-done(((bf16[1,512,1024]{2,1,0:T(8,128)(2,1)}), bf16[1,2048,1024]{2,1,0:T(8,128)(2,1)}) %all-gather.29.cloned.1.call-update) | async-done | bytes 4194320 | tf_op jit(solution)/shard_map/all_gather | solution.py:141
  465.4 5.5 fusion.6
  479.6 10.8 %multiply_convert_fusion.2 = (bf16[448,2048]{1,0:T(8,128)(2,1)}, f32[448,2048]{1,0:T(8,128)S(1)}, f32[448,2048]{1,0:T(8,128)S(1)}) fusion(bf16[448,1024]{1,0:T(8,128)(2,1)S(1)} %add_convert_fusion.2, bf16[1024,2048]{1,0:T(8,128)(2,1)S(1)} %copy-done.61), kind=kOutput, calls=%fused_computation.29 | convolution fusion | flops 1938685952 | bytes 14286848 | tf_op jit(solution)/shard_map/dot_general | solution.py:17
  513.5 6.1 fusion.194
  529.8 14.4 %multiply_reduce_fusion = (f32[8,448]{1,0:T(8,128)S(1)}, f32[8,448,1500]{2,1,0:T(8,128)}) fusion(f32[8,448,1500]{2,1,0:T(8,128)} %copy-done, f32[8,448]{1,0:T(8,128)S(1)} %log_add_fusion.1, bf16[448,8,64]{0,2,1:T(8,128)(2,1)S(1)} %bitcast.693, bf16[1500,8,64]{0,2,1:T(8,128)(2,1)} %bitcast.689), kind=kOutput, calls=%fused_computation.1 | convolution fusion | flops 704252416 | bytes 45031424 | tf_op jit(solution)/shard_map/qhe,khe->hqk/dot_general | solution.py:68
  544.2 15.1 %multiply_convert_fusion = bf16[8,448,1500]{2,1,0:T(8,128)(2,1)S(1)} fusion(f32[8,448,1500]{2,1,0:T(8,128)} %get-tuple-element.113, f32[8,448,1500]{2,1,0:T(8,128)} %copy-done, f32[8,448]{1,0:T(8,128)S(1)} %get-tuple-element.112, f32[8,448]{1,0:T(8,128)S(1)} %log_add_fusion.1), kind=kLoop, calls=%fused_computation | loop fusion | flops 21504000 | bytes 53788672 | tf_op jit(solution)/shard_map/convert_element_type | solution.py:70
  566.4 7.3 fusion.24
  573.8 10.5 %fusion.21 = bf16[8,64,1500]{2,1,0:T(8,128)(2,1)} fusion(bf16[448,8,64]{0,2,1:T(8,128)(2,1)S(1)} %bitcast.694, f32[8,448,1500]{2,1,0:T(8,128)} %copy-done, f32[8,448]{1,0:T(8,128)S(1)} %log_add_fusion.1), kind=kOutput, calls=%fused_computation.50 | convolution fusion | flops 699648000 | bytes 23513088 | tf_op jit(solution)/shard_map/hqk,qhe->khe/dot_general | solution.py:67
  607.8 7.0 reshape.414
  614.7 7.4 constant_dynamic-slice_fusion.5
  640.4 8.1 %multiply_reduce_fusion.1 = (f32[8,448]{1,0:T(8,128)S(1)}, f32[8,448,448]{1,2,0:T(8,128)}) fusion(f32[8,448,448]{1,2,0:T(8,128)} %copy-done.1, f32[8,448]{1,0:T(8,128)S(1)} %copy-done.81, bf16[448,8,64]{0,2,1:T(8,128)(2,1)} %bitcast.700, bf16[448,8,64]{0,2,1:T(8,128)(2,1)} %bitcast.708), kind=kOutput, calls=%fused_computation.16 | convolution fusion | flops 210334208 | bytes 13791232 | tf_op jit(solution)/shard_map/qhe,khe->hqk/dot_general | solution.py:68
  718.8 5.8 collective-permute-done.21
  734.6 13.5 %all-to-all-done.5 = bf16[4,375,512]{2,1,0:T(8,128)(2,1)S(1)} async-done(((bf16[4,375,512]{2,1,0:T(8,128)(2,1)}), bf16[4,375,512]{2,1,0:T(8,128)(2,1)S(1)}, u32[]{:S(2)}, u32[]{:S(2)}) %all-to-all-start.5) | async-done | bytes 1536032 | tf_op jit(solution)/shard_map/all_to_all | solution.py:111
  (604 shorter events, 344.9 us)
Async XLA Ops:
  7.2 21.8 %all-gather.19.cloned.1.call-start = ((), (), s32[]{:S(2)}) async-start(), calls=%async_computation.10 | async-start | bytes 1310720 | tf_op jit(solution)/shard_map/all_gather | solution.py:138
  7.9 51.1 %all-gather.15.cloned.1.call-start = ((), (), s32[]{:S(2)}) async-start(), calls=%async_computation.8 | async-start | bytes 3932160 | tf_op jit(solution)/shard_map/all_gather | solution.py:138
  8.7 81.6 %all-gather.21.cloned.1.call-start = ((), (), s32[]{:S(2)}) async-start(), calls=%async_computation.11 | async-start | bytes 2621440 | tf_op jit(solution)/shard_map/all_gather | solution.py:138
  9.4 184.4 %all-gather.23.cloned.1.call-start = ((), (), s32[]{:S(2)}) async-start(), calls=%async_computation.12 | async-start | bytes 2621440 | tf_op jit(solution)/shard_map/all_gather | solution.py:138
  10.0 186.9 %all-gather.25.cloned.1.call-start = ((), (), s32[]{:S(2)}) async-start(), calls=%async_computation.13 | async-start | bytes 2621440 | tf_op jit(solution)/shard_map/all_gather | solution.py:141
  30.9 273.2 %all-gather.17.cloned.1.call-start = ((), (), s32[]{:S(2)}) async-start(), calls=%async_computation.9 | async-start | bytes 7864320 | tf_op jit(solution)/shard_map/all_gather | solution.py:141
  61.7 329.7 %all-gather.27.cloned.1.call-start = ((), (), s32[]{:S(2)}) async-start(), calls=%async_computation.14 | async-start | bytes 5242880 | tf_op jit(solution)/shard_map/all_gather | solution.py:141
  61.8 44.2 %collective-permute-start = (bf16[2,112,1024]{2,1,0:T(8,128)(2,1)S(1)}, bf16[2,112,1024]{2,1,0:T(8,128)(2,1)}, u32[]{:S(2)}, u32[]{:S(2)}) collective-permute-start(bf16[2,112,1024]{2,1,0:T(8,128)(2,1)S(1)} %copy-done.77), channel_id=1, source_target_pairs={{0,4},{4,0},{1,5},{5,1},{2,6},{6,2},{3,7},{7,3},{8,12},{12,8},{9,1... | collective-permute-start | bytes 1376264 | tf_op jit(solution)/shard_map/ppermute | solution.py:81
  63.6 49.6 %collective-permute-start.11 = (bf16[2,112,1024]{2,1,0:T(8,128)(2,1)}, bf16[2,112,1024]{2,1,0:T(8,128)(2,1)}, u32[]{:S(2)}, u32[]{:S(2)}) collective-permute-start(bf16[2,112,1024]{2,1,0:T(8,128)(2,1)} %param.20), channel_id=1, source_target_pairs={{0,4},{4,0},{1,5},{5,1},{2,6},{6,2},{3,7},{7,3},{8,12},{12,8},{9,1... | collective-permute-start | bytes 1376264 | tf_op jit(solution)/shard_map/ppermute | solution.py:81
  68.4 62.6 %collective-permute-start.2 = (bf16[10,16,1024]{2,1,0:T(8,128)(2,1)}, bf16[10,16,1024]{2,1,0:T(8,128)(2,1)S(1)}, u32[]{:S(2)}, u32[]{:S(2)}) collective-permute-start(bf16[10,16,1024]{2,1,0:T(8,128)(2,1)} %dynamic-slice_bitcast_fusion.1), channel_id=1, source_target_pairs={{0,8},{8,0},{1,9},{9,1},{2,10},{10,2},{3,11},{11,3},{4,12},{12,4},... | collective-permute-start | bytes 983048 | tf_op jit(solution)/shard_map/ppermute | solution.py:106
  93.2 36.5 %collective-permute-start.4 = (bf16[4,16,16,256]{3,2,0,1:T(8,128)(2,1)S(1)}, bf16[4,16,16,256]{3,2,0,1:T(8,128)(2,1)S(1)}, u32[]{:S(2)}, u32[]{:S(2)}) collective-permute-start(bf16[4,16,16,256]{3,2,0,1:T(8,128)(2,1)S(1)} %dynamic-slice_bitcast_fusion), channel_id=1, source_target_pairs={{0,8},{8,0},{1,9},{9,1},{2,10},{10,2},{3,11},{11,3},{4,12},{12,4},... | collective-permute-start | bytes 1572872 | tf_op jit(solution)/shard_map/ppermute | solution.py:106
  104.4 84.6 %collective-permute-start.7 = (bf16[1500,1024]{1,0:T(8,128)(2,1)}, bf16[1500,1024]{1,0:T(8,128)(2,1)}, u32[]{:S(2)}, u32[]{:S(2)}) collective-permute-start(bf16[1500,1024]{1,0:T(8,128)(2,1)} %bitcast.660), channel_id=1, source_target_pairs={{0,4},{4,0},{1,5},{5,1},{2,6},{6,2},{3,7},{7,3},{8,12},{12,8},{9,1... | collective-permute-start | bytes 9216008 | tf_op jit(solution)/shard_map/ppermute | solution.py:81
  125.6 29.4 %all-to-all-start.3 = ((bf16[4,112,512]{2,1,0:T(8,128)(2,1)}), bf16[4,112,512]{2,1,0:T(8,128)(2,1)}, u32[]{:S(2)}, u32[]{:S(2)}) async-start(bf16[4,112,512]{2,1,0:T(8,128)(2,1)} %constant_dynamic-slice_fusion.6), calls=%async_computation.3 | async-start | bytes 917504 | tf_op jit(solution)/shard_map/all_to_all | solution.py:111
  130.9 30.0 %collective-permute-start.1 = (bf16[448,512]{1,0:T(8,128)(2,1)S(1)}, bf16[448,512]{1,0:T(8,128)(2,1)S(1)}, u32[]{:S(2)}, u32[]{:S(2)}) collective-permute-start(bf16[448,512]{1,0:T(8,128)(2,1)S(1)} %bitcast.714), channel_id=1, source_target_pairs={{0,4},{4,0},{1,5},{5,1},{2,6},{6,2},{3,7},{7,3},{8,12},{12,8},{9,1... | collective-permute-start | bytes 1376264 | tf_op jit(solution)/shard_map/ppermute | solution.py:81
  155.0 29.5 %all-to-all-start.1 = ((bf16[4,16,16,256]{3,2,1,0:T(8,128)(2,1)}), bf16[4,16,16,256]{3,2,1,0:T(8,128)(2,1)S(1)}, u32[]{:S(2)}, u32[]{:S(2)}) async-start(bf16[4,16,16,256]{3,2,1,0:T(8,128)(2,1)} %copy.343), calls=%async_computation.1 | async-start | bytes 1048576 | tf_op jit(solution)/shard_map/all_to_all | solution.py:111
  158.4 307.0 %all-gather.29.cloned.1.call-start = ((), (), s32[]{:S(2)}) async-start(), calls=%async_computation.15 | async-start | bytes 5242880 | tf_op jit(solution)/shard_map/all_gather | solution.py:141
  158.7 227.5 %collective-permute-start.12 = (bf16[448,512]{1,0:T(8,128)(2,1)}, bf16[448,512]{1,0:T(8,128)(2,1)}, u32[]{:S(2)}, u32[]{:S(2)}) collective-permute-start(bf16[448,512]{1,0:T(8,128)(2,1)} %bitcast.78), channel_id=1, source_target_pairs={{0,4},{4,0},{1,5},{5,1},{2,6},{6,2},{3,7},{7,3},{8,12},{12,8},{9,1... | collective-permute-start | bytes 1376264 | tf_op jit(solution)/shard_map/ppermute | solution.py:81
  385.9 88.4 %collective-permute-start.8 = (f32[448,1024]{1,0:T(8,128)}, f32[448,1024]{1,0:T(8,128)}, u32[]{:S(2)}, u32[]{:S(2)}) collective-permute-start(f32[448,1024]{1,0:T(8,128)} %fusion.193), channel_id=1, source_target_pairs={{0,4},{4,0},{1,5},{5,1},{2,6},{6,2},{3,7},{7,3},{8,12},{12,8},{9,1... | collective-permute-start | bytes 5505032 | tf_op jit(solution)/shard_map/ppermute | solution.py:81
  519.7 64.6 %collective-permute-start.9 = (f32[448,1024]{1,0:T(8,128)}, f32[448,1024]{1,0:T(8,128)}, u32[]{:S(2)}, u32[]{:S(2)}) collective-permute-start(f32[448,1024]{1,0:T(8,128)} %fusion.194), channel_id=1, source_target_pairs={{0,4},{4,0},{1,5},{5,1},{2,6},{6,2},{3,7},{7,3},{8,12},{12,8},{9,1... | collective-permute-start | bytes 5505032 | tf_op jit(solution)/shard_map/ppermute | solution.py:81
  586.9 97.0 %all-to-all-start.2 = ((bf16[4,112,512]{2,1,0:T(8,128)(2,1)}), bf16[4,112,512]{2,1,0:T(8,128)(2,1)}, u32[]{:S(2)}, u32[]{:S(2)}) async-start(bf16[4,112,512]{2,1,0:T(8,128)(2,1)} %bitcast.68), calls=%async_computation.2 | async-start | bytes 917504 | tf_op jit(solution)/shard_map/all_to_all | solution.py:111
  595.4 28.4 %collective-permute-start.14 = (f32[448,1024]{1,0:T(8,128)}, f32[448,1024]{1,0:T(8,128)}, u32[]{:S(2)}, u32[]{:S(2)}) collective-permute-start(f32[448,1024]{1,0:T(8,128)} %fusion.196), channel_id=1, source_target_pairs={{0,4},{4,0},{1,5},{5,1},{2,6},{6,2},{3,7},{7,3},{8,12},{12,8},{9,1... | collective-permute-start | bytes 5505032 | tf_op jit(solution)/shard_map/ppermute | solution.py:81
  623.8 81.5 %collective-permute-start.17 = (bf16[1500,512]{1,0:T(8,128)(2,1)}, bf16[1500,512]{1,0:T(8,128)(2,1)}, u32[]{:S(2)}, u32[]{:S(2)}) collective-permute-start(bf16[1500,512]{1,0:T(8,128)(2,1)} %bitcast.661), channel_id=1, source_target_pairs={{0,4},{4,0},{1,5},{5,1},{2,6},{6,2},{3,7},{7,3},{8,12},{12,8},{9,1... | collective-permute-start | bytes 4608008 | tf_op jit(solution)/shard_map/ppermute | solution.py:81
  693.2 34.8 %collective-permute-start.15 = (f32[448,1024]{1,0:T(8,128)S(1)}, f32[448,1024]{1,0:T(8,128)}, u32[]{:S(2)}, u32[]{:S(2)}) collective-permute-start(f32[448,1024]{1,0:T(8,128)S(1)} %add_add_fusion.3), channel_id=1, source_target_pairs={{0,4},{4,0},{1,5},{5,1},{2,6},{6,2},{3,7},{7,3},{8,12},{12,8},{9,1... | collective-permute-start | bytes 5505032 | tf_op jit(solution)/shard_map/ppermute | solution.py:81
  708.9 39.3 %all-to-all-start.5 = ((bf16[4,375,512]{2,1,0:T(8,128)(2,1)}), bf16[4,375,512]{2,1,0:T(8,128)(2,1)S(1)}, u32[]{:S(2)}, u32[]{:S(2)}) async-start(bf16[4,375,512]{2,1,0:T(8,128)(2,1)} %reshape.415), calls=%async_computation.5 | async-start | bytes 3080192 | tf_op jit(solution)/shard_map/all_to_all | solution.py:111
  (163 other events, 1708.1 us)
Sparse Core Ops, SparseCore 0:
  9.6 19.3 all-gather.18
  30.5 28.5 all-gather.14
  60.6 29.5 all-gather.20
  91.7 28.6 all-gather.22
  121.8 66.5 all-gather.24
  190.4 113.7 all-gather.16
  305.7 78.7 all-gather.26
  386.1 79.2 all-gather.28

commit v2 on v1

--- a/solution.py
+++ b/solution.py
@@ -1,8 +1,11 @@
+import functools
 from functools import partial
 
 import jax
 import jax.numpy as jnp
 from jax import lax
+from jax.experimental import pallas as pl
+from jax.experimental.pallas import tpu as pltpu
 from jax.sharding import Mesh, PartitionSpec as P
 
 HD = 64
@@ -11,6 +14,220 @@
 masked_score = -1e30
 f32, bf16 = jnp.float32, jnp.bfloat16
 SWAP = ((0, 1), (1, 0))
+MESH = pl.DeviceIdType.MESH
+
+
+class Unit:
+    def __init__(self, kind, index):
+        self.kind, self.index = kind, index
+        self.rows = 512 if kind in ("in", "up") else 128
+        self.most = self.rows * 3 // 4
+        self.via_y = 304 if self.rows == 512 else 80
+
+
+UNITS = (
+    [Unit("in", i) for i in (0, 1, 2)]
+    + [Unit("out", 0)]
+    + [Unit("in", i) for i in (3, 4, 5)]
+    + [Unit("out", 1)]
+    + [Unit(kind, j) for j in range(4) for kind in ("up", "down")]
+)
+
+
+def gather_kernel(tok, enc, cot, w_in, w_out, w_up, w_down, g_tok, g_enc, g_cot, g_in, g_out, g_up, g_down, sems, semr, loc):
+    x, y, c, z = (lax.axis_index(a) for a in ("rep", "sh", "core", "tp"))
+    count = [0]
+    waits = []
+
+    def when(cond, fn):
+        if cond is None:
+            fn()
+        else:
+            pl.when(cond)(fn)
+
+    def block(u, yy, zz, first, size):
+        def al(v, m):
+            return pl.multiple_of(v, m)
+        if u.kind == "in":
+            return g_in.at[u.index, pl.ds(al(yy * 512 + first, 16), size), pl.ds(al(zz * 128, 128), 128)]
+        if u.kind == "up":
+            return g_up.at[pl.ds(al(yy * 512 + first, 16), size), pl.ds(al(zz * 512 + u.index * 128, 128), 128)]
+        if u.kind == "out":
+            return g_out.at[u.index, pl.ds(al(zz * 128 + first, 16), size), pl.ds(al(yy * 512, 512), 512)]
+        return g_down.at[pl.ds(al(zz * 512 + u.index * 128 + first, 16), size), pl.ds(al(yy * 512, 512), 512)]
+
+    def half_src(u, cc):
+        if u.kind == "in":
+            return w_in.at[u.index, :, pl.ds(pl.multiple_of(cc * 128, 128), 128)]
+        if u.kind == "up":
+            return w_up.at[:, pl.ds(pl.multiple_of(cc * 512 + u.index * 128, 128), 128)]
+        if u.kind == "out":
+            return w_out.at[u.index, pl.ds(pl.multiple_of(cc * 128, 128), 128), :]
+        return w_down.at[pl.ds(pl.multiple_of(cc * 512 + u.index * 128, 128), 128), :]
+
+    def half_dst(u, cc):
+        if u.kind == "in":
+            return block(u, y, z, cc * 256, 256)
+        if u.kind == "up":
+            return block(u, y, z, cc * 256, 256)
+        al = pl.multiple_of
+        if u.kind == "out":
+            return g_out.at[u.index, pl.ds(al(z * 128, 128), 128), pl.ds(al(y * 512 + cc * 256, 256), 256)]
+        return g_down.at[pl.ds(al(z * 512 + u.index * 128, 128), 128), pl.ds(al(y * 512 + cc * 256, 256), 256)]
+
+    def remote(src, dst, s, r, dev):
+        return pltpu.make_async_remote_copy(src_ref=src, dst_ref=dst, send_sem=s, recv_sem=r, device_id=dev, device_id_type=MESH)
+
+    def send(cond, src, dst, s, r, dev):
+        when(cond, lambda: remote(src, dst, s, r, dev).start())
+        waits.append((cond, lambda: remote(src, dst, s, r, dev).wait_send()))
+
+    def got(dst, s, r, dev):
+        remote(dst, dst, s, r, dev).wait_recv()
+
+    bar = pltpu.get_barrier_semaphore()
+    peers = [{"rep": 1 - x}, {"sh": 1 - y}, {"core": 1 - c}] + [{"tp": lax.rem(z + k, 4)} for k in (1, 2, 3)]
+    for dev in peers:
+        pl.semaphore_signal(bar, inc=1, device_id=dev, device_id_type=MESH)
+    pl.semaphore_wait(bar, 6)
+    X, Y, C = peers[:3]
+    UP, DOWN = {"tp": z + 1}, {"tp": z - 1}
+    NU = len(UNITS)
+    def S(kind, u, j):
+        return sems.at[kind, u, j]
+    def R(kind, u, j):
+        return semr.at[kind, u, j]
+    def core_exchange(i):
+        u = UNITS[i]
+        send(None, half_src(u, 1 - c), half_dst(u, c), S(0, i, 0), R(0, i, 0), C)
+        pltpu.make_async_copy(half_src(u, c), half_dst(u, c), loc.at[i]).start()
+
+    def own(i):
+        u = UNITS[i]
+        got(half_dst(u, 1 - c), S(0, i, 0), R(0, i, 0), C)
+        pltpu.make_async_copy(half_src(u, c), half_dst(u, c), loc.at[i]).wait()
+        zb = block(u, y, z, x * (u.rows - u.most), u.most)
+        send(z < 3, zb, zb, S(1, i, z), R(1, i, z), UP)
+        send(z > 0, zb, zb, S(2, i, z), R(1, i, z), DOWN)
+        yb = block(u, y, z, x * (u.rows - u.via_y), u.via_y)
+        send(None, yb, yb, S(3, i, z), R(3, i, z), Y)
+
+    def hop(i, k):
+        u = UNITS[i]
+        for ok, j, more, dev, kind in (((z >= k), z - k, (z >= k) & (z < 3), UP, 1), ((z + k <= 3), z + k, (z + k <= 3) & (z > 0), DOWN, 2)):
+            zb = block(u, y, j, x * (u.rows - u.most), u.most)
+            when(ok, functools.partial(got, zb, S(1, i, j), R(1, i, j), X))
+            send(more, zb, zb, S(kind, i, j), R(1, i, j), dev)
+            yb = block(u, y, j, x * (u.rows - u.via_y), u.via_y)
+            send(ok, yb, yb, S(3, i, j), R(3, i, j), Y)
+            xb = block(u, y, j, x * u.most, u.rows - u.most)
+            send(ok, xb, xb, S(4, i, j), R(4, i, j), X)
+
+    def cross(i, k):
+        u = UNITS[i]
+        for ok, j in ((z >= k, z - k), (z + k <= 3, z + k)) if k else ((None, z),):
+            yb = block(u, 1 - y, j, x * (u.rows - u.via_y), u.via_y)
+            when(ok, functools.partial(got, yb, S(3, i, j), R(3, i, j), X))
+            xb = block(u, 1 - y, j, x * u.via_y, u.rows - u.via_y)
+            send(ok, xb, xb, S(5, i, j), R(5, i, j), X)
+
+    def last(i, k):
+        u = UNITS[i]
+        for ok, j in ((z >= k, z - k), (z + k <= 3, z + k)) if k else ((None, z),):
+            if k:
+                xb = block(u, y, j, (1 - x) * u.most, u.rows - u.most)
+                when(ok, functools.partial(got, xb, S(4, i, j), R(4, i, j), X))
+            xb = block(u, 1 - y, j, (1 - x) * u.via_y, u.rows - u.via_y)
+            when(ok, functools.partial(got, xb, S(5, i, j), R(5, i, j), X))
+
+    NM = 0
+    def rows_out(src, dst, slot):
+        for i in (0, 1):
+            zd = 2 * c + i
+            d = dst.at[pl.ds(pl.multiple_of(z * 112, 16), 112)]
+            send(zd != z, src.at[i], d, S(0, slot * 2 + i, 1), R(0, slot * 4 + z, 2), {"tp": zd})
+            def local(i=i, d=d):
+                cp = pltpu.make_async_copy(src.at[i], d, loc.at[NU + slot])
+                cp.start()
+                cp.wait()
+            when(zd == z, local)
+
+    def rows_in(dst, slot):
+        mine = c == z // 2
+        def wait3():
+            for k in (1, 2, 3):
+                j = lax.rem(z + k, 4)
+                d = dst.at[pl.ds(pl.multiple_of(j * 112, 16), 112)]
+                got(d, S(0, 0, 1), R(0, slot * 4 + j, 2), X)
+        when(mine, wait3)
+        send(mine, dst, dst, S(0, 8 + slot, 3), R(0, 8 + slot, 3), C)
+
+    def rows_have(dst, slot):
+        when(c != z // 2, lambda: got(dst, S(0, 8 + slot, 3), R(0, 8 + slot, 3), C))
+
+    for i in range(NU):
+        core_exchange(i)
+    rows_out(tok, g_tok, 0)
+    mine = c == z // 2
+    enc_parts = []
+
+    def enc_src(part):
+        return enc.at[lax.rem(z, 2), part]
+
+    def enc_local(part, slot):
+        return pltpu.make_async_copy(enc_src(part), g_enc.at[part], loc.at[NU + 2 + slot])
+
+    def enc_start(part, slot):
+        enc_local(part, slot).start()
+
+    for t in range(NU + 6):
+        if t < NU:
+            own(t)
+        for k in (1, 2, 3):
+            if 0 <= t - k < NU:
+                hop(t - k, k)
+        for k in (0, 1, 2, 3):
+            if 0 <= t - k - 1 < NU:
+                cross(t - k - 1, k)
+        if t == 5:
+            rows_in(g_tok, 0)
+        if t == 10:
+            rows_out(cot, g_cot, 1)
+        if t == 17:
+            rows_in(g_cot, 1)
+        if t in (6, 8, 10):
+            part = slice((t - 6) * 256, (t - 4) * 256 if t < 10 else 1500)
+            enc_parts.append((part, (t - 6) // 2))
+            send(mine, enc_src(part), g_enc.at[part], S(0, (t - 6) // 2, 3), R(0, 4 + (t - 6) // 2, 3), C)
+            when(mine, functools.partial(enc_start, part, (t - 6) // 2))
+        for k in (0, 1, 2, 3):
+            if 0 <= t - k - 2 < NU:
+                last(t - k - 2, k)
+    rows_have(g_tok, 0)
+    rows_have(g_cot, 1)
+    for part, slot in enc_parts:
+        when(mine, lambda: enc_local(part, slot).wait())
+        when(c != z // 2, lambda: got(g_enc.at[part], S(0, 0, 3), R(0, 4 + slot, 3), C))
+    for cond, fn in waits:
+        when(cond, fn)
+
+
+def gather(tok, enc, cot, w_in, w_out, w_up, w_down):
+    any_ = pl.BlockSpec(memory_space=pl.ANY)
+    NU = len(UNITS)
+    shapes = [(448, 1024), (1500, 1024), (448, 1024), (6, 1024, 512), (2, 512, 1024), (1024, 2048), (2048, 1024)]
+    return pl.pallas_call(
+        gather_kernel,
+        out_shape=[jax.ShapeDtypeStruct(s, bf16) for s in shapes],
+        in_specs=[any_] * 7,
+        out_specs=[any_] * 7,
+        scratch_shapes=[
+            pltpu.SemaphoreType.DMA((6, NU, 4)),
+            pltpu.SemaphoreType.DMA((6, NU, 4)),
+            pltpu.SemaphoreType.DMA((NU + 5,)),
+        ],
+        compiler_params=pltpu.CompilerParams(collective_id=1, has_side_effects=True),
+    )(tok, enc, cot, w_in, w_out, w_up, w_down)
 
 
 def dot(a, b, dims):
@@ -221,7 +438,22 @@
     a_in, a_up, b_out, b_down = chosen_whole[:6], chosen_whole[6], chosen_whole[7:9], chosen_whole[9]
     b_in, b_up, a_out, a_down = columns(0, 6), wide_columns(6), columns(6 + tp, 2), wide_columns(8 + tp)
 
-    w_in, w_out, w_first, w_second = gather_weights(w_attn_in, w_attn_out, w_up, w_down)
+    if n == 2:
+        taken, memory, upstream, w_in, w_out, w_first, w_second = gather(
+            tokens,
+            encoded,
+            cotangent,
+            w_attn_in.reshape(6, *w_attn_in.shape[3:]),
+            w_attn_out[0],
+            w_up[0],
+            w_down[0],
+        )
+    else:
+        w_in, w_out, w_first, w_second = gather_weights(w_attn_in, w_attn_out, w_up, w_down)
+        taken = rows_here(tokens)
+        upstream = rows_here(cotangent)
+        mine = lax.dynamic_index_in_dim(encoded, z % 2, 0, keepdims=False)
+        memory = jnp.where(core == z // 2, mine, swap_core(mine))
 
     def merge(weight, down_rows, up_rows):
         return (weight.astype(f32) + t_mm(down_rows, up_rows)).astype(bf16)
@@ -231,10 +463,7 @@
     w_first = merge(w_first, a_up, b_up)
     w_second = merge(w_second, a_down, b_down)
 
-    hidden = rows_here(tokens).astype(f32)
-    upstream = rows_here(cotangent)
-    mine = lax.dynamic_index_in_dim(encoded, z % 2, 0, keepdims=False)
-    memory = jnp.where(core == z // 2, mine, swap_core(mine))
+    hidden = taken.astype(f32)
 
     kept = []
     for side in range(2):

time: 801 us -> 685 us (0.86)
  waiting for transfers between devices: 328 us -> 44.2 us
  Pallas kernels: 0 us -> 202 us
  local copies, waits for them, and re-layouts: 121 us -> 107 us
  between operations: 17 us -> 3.8 us
    all_gather x8 -> x0, waiting for transfers between devices: 240 us -> none  [the longest x4 172 us: over_tp(): return lax.all_gather(block, 'tp', axis=axis, tiled=True)]
    pallas_call x0 -> x1, Pallas kernels: none -> 202 us  [gather(): pl.pallas_call(gather_kernel, out_shape=[jax.ShapeDtypeStruct(s, bf16) fo...]
    all_to_all x8 -> x6, waiting for transfers between devices: 76.6 us -> 34.2 us  [over_z(): return lax.all_to_all(stacked, 'tp', 0, 0, tiled=True)]
    dynamic_slice x7 -> x0, local copies, waits for them, and re-layouts: 19.1 us -> none  [the longest x4 9.86 us: half(): return lax.dynamic_slice_in_dim(block, core * width, width, axis)]
    all_to_all x8 -> x6, starting transfers between devices: 31.4 us -> 23.3 us  [over_z(): return lax.all_to_all(stacked, 'tp', 0, 0, tiled=True)]
    unnamed x314 -> x284, local copies, waits for them, and re-layouts: 31.6 us -> 36 us
    ppermute x19 -> x14, starting transfers between devices: 18.1 us -> 19.4 us  [swap_core(): return lax.ppermute(rows, 'core', SWAP)]
  transfers between devices with their start and end apart: 39 -> 24, of which waited for: 15 -> 8; matrix products, arithmetic and copies ran while one was open for 43% -> 40% of each run, Pallas kernels for 0% -> 30%
where the time goes in v2:
time: 685 us; the launch traced here: 673 us
  Pallas kernels  202 us (29%)
  matrix products  191 us (28%)
  local copies, waits for them, and re-layouts  107 us (16%)
  other arithmetic  73.4 us (11%)
  starting transfers between devices  45.9 us (7%)
  waiting for transfers between devices  44.2 us (6%)
    pallas_call x1, Pallas kernels, gather(): pl.pallas_call(gather_kernel, out_shape=[jax.ShapeDtypeStruct(s, bf16) fo...  202 us
    dot_general x50, matrix products, dot(): return lax.dot_general(a, b, (dims, ((), ())), preferred_element_type=f32)  122 us
    unnamed x284, local copies, waits for them, and re-layouts  36 us
    all_to_all x6, waiting for transfers between devices, over_z(): return lax.all_to_all(stacked, 'tp', 0, 0, tiled=True)  34.2 us
    all_to_all x6, starting transfers between devices, over_z(): return lax.all_to_all(stacked, 'tp', 0, 0, tiled=True)  23.3 us
    dot_general x2, matrix products, attend_backward(): grad_probs = jnp.einsum('qhe,khe->hqk', gh, vh, preferred_element_type=f32)  23.3 us
    convert_element_type x2, other arithmetic, attend_backward(): grad_scores = grad_scores.astype(bf16)  20.1 us
    ppermute x14, starting transfers between devices, swap_core(): return lax.ppermute(rows, 'core', SWAP)  19.4 us
  transfers between devices with their start and end apart: 24, of which 8 were waited for; matrix products, arithmetic and copies ran while one was open for 40% of the time, Pallas kernels for 30%

profile of v2, /device:TPU:1, one launch (start us, length us, event | category | flops | bytes accessed | tf_op | source)
XLA Modules:
  0.0 672.8 jit_solution(18186126533398770831)
XLA Ops:
  3.6 5.1 all-reduce
  15.5 7.3 %copy.340.enc = bf16[2,1500,1024]{2,1,0:T(8,128)(2,1)} copy(bf16[2,1500,1024]{2,0,1:T(2,128)(2,1)} %param.19) | data formatting | bytes 12288000 | tf_op args[1]
  22.9 201.8 %shard_map.257 = (bf16[448,1024]{1,0:T(8,128)(2,1)}, bf16[1500,1024]{1,0:T(8,128)(2,1)}, bf16[448,1024]{1,0:T(8,128)(2,1)}, bf16[6,1024,512]{2,1,0:T(8,128)(2,1)...) custom-call(bf16[2,112,1024]{2,1,0:T(8,128)(2,1)} %tok.1, ...), custom_call_target="tpu_custom_call" | custom-call | tf_op jit(solution)/shard_map/pallas_call | solution.py:219
  226.2 5.8 collective-permute-start.3
  241.8 10.7 %all-to-all-done = bf16[4,16,16,256]{3,2,1,0:T(8,128)(2,1)S(1)} async-done(((bf16[4,16,16,256]{3,2,1,0:T(8,128)(2,1)}), bf16[4,16,16,256]{3,2,1,0:T(8,128)(2,1)S(1)}, u32[]{:S(2)}, u32[]{:S(2)}) %all-to-all-start) | async-done | bytes 524320 | tf_op jit(solution)/shard_map/all_to_all | solution.py:328
  310.0 5.7 fusion
  317.8 9.6 %fusion.49 = bf16[8,64,448]{2,1,0:T(8,128)(2,1)S(1)} fusion(bf16[1500,8,64]{0,2,1:T(8,128)(2,1)S(1)} %bitcast.653, f32[8,448,1500]{2,1,0:T(8,128)} %copy-done, f32[8,448]{1,0:T(8,128)S(1)} %fusion, f32[8,448]{1,0:T(8,128)S(1)} %get-tuple-element.115), kind=kOutput, calls=%fused_computation.115 | convolution fusion | flops 704485376 | bytes 23527424 | tf_op jit(solution)/shard_map/hqk,khe->qhe/dot_general | solution.py:277
  338.3 5.6 add_convert_fusion.1
  358.8 10.9 %add_convert_fusion.3 = (bf16[448,2048]{1,0:T(8,128)(2,1)S(1)}, f32[448,2048]{1,0:T(8,128)S(1)}) fusion(f32[448,2048]{1,0:T(8,128)S(1)} %fusion.191, bf16[448,1024]{1,0:T(8,128)(2,1)S(1)} %copy-done.20, bf16[2048,1024]{1,0:T(8,128)(2,1)S(1)} %copy-done.52), kind=kOutput, calls=%fused_computation.26 | convolution fusion | flops 1945108480 | bytes 14286848 | tf_op jit(solution)/shard_map/dot_general | solution.py:234
  391.6 6.2 fusion.192
  409.3 15.3 %multiply_reduce_fusion = (f32[8,448]{1,0:T(8,128)S(1)}, f32[8,448,1500]{2,1,0:T(8,128)}) fusion(f32[8,448,1500]{2,1,0:T(8,128)} %copy-done, f32[8,448]{1,0:T(8,128)S(1)} %log_add_fusion.1, bf16[448,8,64]{0,2,1:T(8,128)(2,1)} %bitcast.656, bf16[1500,8,64]{0,2,1:T(8,128)(2,1)} %bitcast.652), kind=kOutput, calls=%fused_computation.1 | convolution fusion | flops 704252416 | bytes 45031424 | tf_op jit(solution)/shard_map/qhe,khe->hqk/dot_general | solution.py:285
  424.5 14.9 %multiply_convert_fusion = bf16[8,448,1500]{2,1,0:T(8,128)(2,1)S(1)} fusion(f32[8,448,1500]{2,1,0:T(8,128)} %get-tuple-element.118, f32[8,448,1500]{2,1,0:T(8,128)} %copy-done, f32[8,448]{1,0:T(8,128)S(1)} %get-tuple-element.117, f32[8,448]{1,0:T(8,128)S(1)} %log_add_fusion.1), kind=kLoop, calls=%fused_computation | loop fusion | flops 21504000 | bytes 53788672 | tf_op jit(solution)/shard_map/convert_element_type | solution.py:287
  448.4 7.4 %fusion.22 = bf16[8,64,1500]{2,1,0:T(8,128)(2,1)} fusion(bf16[448,8,64]{0,2,1:T(8,128)(2,1)S(1)} %bitcast.639, bf16[8,448,1500]{2,1,0:T(8,128)(2,1)} %copy-done.2), kind=kOutput, calls=%fused_computation.47 | convolution fusion | flops 689664000 | bytes 12746752 | tf_op jit(solution)/shard_map/hqk,qhe->khe/dot_general | solution.py:289
  455.8 9.3 %fusion.19 = bf16[8,64,1500]{2,1,0:T(8,128)(2,1)S(1)} fusion(bf16[448,8,64]{0,2,1:T(8,128)(2,1)S(1)} %bitcast.657, f32[8,448,1500]{2,1,0:T(8,128)} %copy-done, f32[8,448]{1,0:T(8,128)S(1)} %log_add_fusion.1), kind=kOutput, calls=%fused_computation.46 | convolution fusion | flops 699648000 | bytes 23513088 | tf_op jit(solution)/shard_map/hqk,qhe->khe/dot_general | solution.py:284
  468.2 4.6 all-to-all-start.1
  491.8 8.2 %reshape.398 = bf16[1500,2,512]{2,1,0:T(2,128)(2,1)} reshape(bf16[1500,1024]{1,0:T(8,128)(2,1)} %add_convert_fusion.2) | data formatting | bytes 6144000 | tf_op jit(solution)/shard_map/reshape | solution.py:515
  499.9 9.7 %constant_dynamic-slice_fusion.5 = (bf16[1500,1,512]{2,1,0:T(2,128)(2,1)}, bf16[1500,1,512]{2,1,0:T(2,128)(2,1)S(1)}) fusion(bf16[1500,2,512]{2,1,0:T(2,128)(2,1)} %reshape.398, s32[]{:T(128)S(6)} %select_n.108, s32[]{:T(128)S(6)} %select_n.109), kind=kLoop, calls=%fused_computation.328 | loop fusion | bytes 6144008 | tf_op jit(solution)/shard_map/dynamic-slice
  527.0 8.1 %multiply_reduce_fusion.1 = (f32[8,448]{1,0:T(8,128)S(1)}, f32[8,448,448]{1,2,0:T(8,128)}) fusion(f32[8,448,448]{1,2,0:T(8,128)} %copy-done.1, f32[8,448]{1,0:T(8,128)S(1)} %copy-done.72, bf16[448,8,64]{0,2,1:T(8,128)(2,1)} %bitcast.663, bf16[448,8,64]{0,2,1:T(8,128)(2,1)} %bitcast.672), kind=kOutput, calls=%fused_computation.14 | convolution fusion | flops 210334208 | bytes 13791232 | tf_op jit(solution)/shard_map/qhe,khe->hqk/dot_general | solution.py:285
  535.1 5.2 multiply_convert_fusion.1
  570.8 4.9 all-to-all-start.4
  582.4 5.6 all-to-all-done.4
  606.8 6.4 collective-permute-done.16
  624.2 10.6 %all-to-all-done.3 = bf16[4,375,512]{2,1,0:T(8,128)(2,1)S(1)} async-done(((bf16[4,375,512]{2,1,0:T(8,128)(2,1)}), bf16[4,375,512]{2,1,0:T(8,128)(2,1)S(1)}, u32[]{:S(2)}, u32[]{:S(2)}) %all-to-all-start.3) | async-done | bytes 1536032 | tf_op jit(solution)/shard_map/all_to_all | solution.py:328
  638.2 4.8 all-to-all-done.5
  (524 shorter events, 285.5 us)
Async XLA Ops:
  12.8 213.3 %collective-permute-start.2 = (bf16[4,16,16,256]{3,2,0,1:T(8,128)(2,1)}, bf16[4,16,16,256]{3,2,0,1:T(8,128)(2,1)S(1)}, u32[]{:S(2)}, u32[]{:S(2)}) collective-permute-start(bf16[4,16,16,256]{3,2,0,1:T(8,128)(2,1)} %dynamic-slice_bitcast_fusion), channel_id=1, source_target_pairs={{0,8},{8,0},{1,9},{9,1},{2,10},{10,2},{3,11},{11,3},{4,12},{12,4},... | collective-permute-start | bytes 1572872 | tf_op jit(solution)/shard_map/ppermute | solution.py:323
  14.2 224.8 %collective-permute-start = (bf16[10,16,1024]{2,1,0:T(8,128)(2,1)}, bf16[10,16,1024]{2,1,0:T(8,128)(2,1)}, u32[]{:S(2)}, u32[]{:S(2)}) collective-permute-start(bf16[10,16,1024]{2,1,0:T(8,128)(2,1)} %dynamic-slice_bitcast_fusion.1), channel_id=1, source_target_pairs={{0,8},{8,0},{1,9},{9,1},{2,10},{10,2},{3,11},{11,3},{4,12},{12,4},... | collective-permute-start | bytes 983048 | tf_op jit(solution)/shard_map/ppermute | solution.py:323
  226.2 7.4 %collective-permute-start.3 = (bf16[4,16,16,256]{3,2,0,1:T(8,128)(2,1)S(1)}, bf16[4,16,16,256]{3,2,0,1:T(8,128)(2,1)S(1)}, u32[]{:S(2)}, u32[]{:S(2)}) collective-permute-start(bf16[4,16,16,256]{3,2,0,1:T(8,128)(2,1)S(1)} %bitcast_add_fusion), channel_id=1, source_target_pairs={{0,4},{4,0},{1,5},{5,1},{2,6},{6,2},{3,7},{7,3},{8,12},{12,8},{9,1... | collective-permute-start | bytes 1572872 | tf_op jit(solution)/shard_map/ppermute | solution.py:298
  234.7 17.8 %all-to-all-start = ((bf16[4,16,16,256]{3,2,1,0:T(8,128)(2,1)}), bf16[4,16,16,256]{3,2,1,0:T(8,128)(2,1)S(1)}, u32[]{:S(2)}, u32[]{:S(2)}) async-start(bf16[4,16,16,256]{3,2,1,0:T(8,128)(2,1)} %copy.345), calls=%async_computation | async-start | bytes 1048576 | tf_op jit(solution)/shard_map/all_to_all | solution.py:328
  240.0 1.7 collective-permute-start.1
  276.3 21.5 %collective-permute-start.4 = (f32[448,1024]{1,0:T(8,128)}, f32[448,1024]{1,0:T(8,128)}, u32[]{:S(2)}, u32[]{:S(2)}) collective-permute-start(f32[448,1024]{1,0:T(8,128)} %fusion.189), channel_id=1, source_target_pairs={{0,4},{4,0},{1,5},{5,1},{2,6},{6,2},{3,7},{7,3},{8,12},{12,8},{9,1... | collective-permute-start | bytes 5505032 | tf_op jit(solution)/shard_map/ppermute | solution.py:298
  330.1 20.7 %collective-permute-start.5 = (f32[448,1024]{1,0:T(8,128)}, f32[448,1024]{1,0:T(8,128)}, u32[]{:S(2)}, u32[]{:S(2)}) collective-permute-start(f32[448,1024]{1,0:T(8,128)} %fusion.190), channel_id=1, source_target_pairs={{0,4},{4,0},{1,5},{5,1},{2,6},{6,2},{3,7},{7,3},{8,12},{12,8},{9,1... | collective-permute-start | bytes 5505032 | tf_op jit(solution)/shard_map/ppermute | solution.py:298
  373.1 24.6 %collective-permute-start.8 = (f32[448,1024]{1,0:T(8,128)}, f32[448,1024]{1,0:T(8,128)}, u32[]{:S(2)}, u32[]{:S(2)}) collective-permute-start(f32[448,1024]{1,0:T(8,128)} %fusion.193), channel_id=1, source_target_pairs={{0,4},{4,0},{1,5},{5,1},{2,6},{6,2},{3,7},{7,3},{8,12},{12,8},{9,1... | collective-permute-start | bytes 5505032 | tf_op jit(solution)/shard_map/ppermute | solution.py:298
  397.8 67.4 %collective-permute-start.6 = (f32[448,1024]{1,0:T(8,128)}, f32[448,1024]{1,0:T(8,128)}, u32[]{:S(2)}, u32[]{:S(2)}) collective-permute-start(f32[448,1024]{1,0:T(8,128)} %fusion.192), channel_id=1, source_target_pairs={{0,4},{4,0},{1,5},{5,1},{2,6},{6,2},{3,7},{7,3},{8,12},{12,8},{9,1... | collective-permute-start | bytes 5505032 | tf_op jit(solution)/shard_map/ppermute | solution.py:298
  468.2 102.6 %all-to-all-start.1 = ((bf16[4,112,512]{2,1,0:T(8,128)(2,1)}), bf16[4,112,512]{2,1,0:T(8,128)(2,1)}, u32[]{:S(2)}, u32[]{:S(2)}) async-start(bf16[4,112,512]{2,1,0:T(8,128)(2,1)} %bitcast.675), calls=%async_computation.1 | async-start | bytes 917504 | tf_op jit(solution)/shard_map/all_to_all | solution.py:328
  478.5 32.8 %collective-permute-start.9 = (f32[448,1024]{1,0:T(8,128)}, f32[448,1024]{1,0:T(8,128)}, u32[]{:S(2)}, u32[]{:S(2)}) collective-permute-start(f32[448,1024]{1,0:T(8,128)} %fusion.194), channel_id=1, source_target_pairs={{0,4},{4,0},{1,5},{5,1},{2,6},{6,2},{3,7},{7,3},{8,12},{12,8},{9,1... | collective-permute-start | bytes 5505032 | tf_op jit(solution)/shard_map/ppermute | solution.py:298
  511.3 80.6 %collective-permute-start.12 = (bf16[1500,512]{1,0:T(8,128)(2,1)}, bf16[1500,512]{1,0:T(8,128)(2,1)}, u32[]{:S(2)}, u32[]{:S(2)}) collective-permute-start(bf16[1500,512]{1,0:T(8,128)(2,1)} %bitcast.624), channel_id=1, source_target_pairs={{0,4},{4,0},{1,5},{5,1},{2,6},{6,2},{3,7},{7,3},{8,12},{12,8},{9,1... | collective-permute-start | bytes 4608008 | tf_op jit(solution)/shard_map/ppermute | solution.py:298
  547.8 21.4 %collective-permute-start.14 = (bf16[4,10,16,128]{3,2,1,0:T(8,128)(2,1)}, bf16[4,10,16,128]{3,2,1,0:T(8,128)(2,1)}, u32[]{:S(2)}, u32[]{:S(2)}) collective-permute-start(bf16[4,10,16,128]{3,2,1,0:T(8,128)(2,1)} %dynamic-slice_bitcast_fusion.5), channel_id=1, source_target_pairs={{0,4},{4,0},{1,5},{5,1},{2,6},{6,2},{3,7},{7,3},{8,12},{12,8},{9,1... | collective-permute-start | bytes 491528 | tf_op jit(solution)/shard_map/ppermute | solution.py:298
  570.8 17.2 %all-to-all-start.4 = ((bf16[4,26,16,128]{3,2,1,0:T(8,128)(2,1)}), bf16[4,26,16,128]{3,2,1,0:T(8,128)(2,1)}, u32[]{:S(2)}, u32[]{:S(2)}) async-start(bf16[4,26,16,128]{3,2,1,0:T(8,128)(2,1)} %fusion.108), calls=%async_computation.4 | async-start | bytes 851968 | tf_op jit(solution)/shard_map/all_to_all | solution.py:328
  580.2 37.4 %collective-permute-start.10 = (f32[448,1024]{1,0:T(8,128)S(1)}, f32[448,1024]{1,0:T(8,128)}, u32[]{:S(2)}, u32[]{:S(2)}) collective-permute-start(f32[448,1024]{1,0:T(8,128)S(1)} %add_add_fusion.3), channel_id=1, source_target_pairs={{0,4},{4,0},{1,5},{5,1},{2,6},{6,2},{3,7},{7,3},{8,12},{12,8},{9,1... | collective-permute-start | bytes 5505032 | tf_op jit(solution)/shard_map/ppermute | solution.py:298
  582.3 22.5 %collective-permute-start.7 = (bf16[2,112,512]{2,1,0:T(8,128)(2,1)}, bf16[2,112,512]{2,1,0:T(8,128)(2,1)}, u32[]{:S(2)}, u32[]{:S(2)}) collective-permute-start(bf16[2,112,512]{2,1,0:T(8,128)(2,1)} %dynamic-slice_bitcast_fusion.3), channel_id=1, source_target_pairs={{0,4},{4,0},{1,5},{5,1},{2,6},{6,2},{3,7},{7,3},{8,12},{12,8},{9,1... | collective-permute-start | bytes 688136 | tf_op jit(solution)/shard_map/ppermute | solution.py:298
  591.3 10.5 %collective-permute-start.15 = (bf16[2,32,26,128]{3,1,2,0:T(8,128)(2,1)}, bf16[2,32,26,128]{3,1,2,0:T(8,128)(2,1)}, u32[]{:S(2)}, u32[]{:S(2)}) collective-permute-start(bf16[2,32,26,128]{3,1,2,0:T(8,128)(2,1)} %bitcast.626), channel_id=1, source_target_pairs={{0,8},{8,0},{1,9},{9,1},{2,10},{10,2},{3,11},{11,3},{4,12},{12,4},... | collective-permute-start | bytes 1277960 | tf_op jit(solution)/shard_map/ppermute | solution.py:323
  595.5 39.3 %all-to-all-start.3 = ((bf16[4,375,512]{2,1,0:T(8,128)(2,1)}), bf16[4,375,512]{2,1,0:T(8,128)(2,1)S(1)}, u32[]{:S(2)}, u32[]{:S(2)}) async-start(bf16[4,375,512]{2,1,0:T(8,128)(2,1)} %reshape.399), calls=%async_computation.3 | async-start | bytes 3080192 | tf_op jit(solution)/shard_map/all_to_all | solution.py:328
  603.7 9.5 %collective-permute-start.16 = (bf16[2,32,26,128]{3,1,2,0:T(8,128)(2,1)}, bf16[2,32,26,128]{3,1,2,0:T(8,128)(2,1)}, u32[]{:S(2)}, u32[]{:S(2)}) collective-permute-start(bf16[2,32,26,128]{3,1,2,0:T(8,128)(2,1)} %fusion.95), channel_id=1, source_target_pairs={{0,16},{16,0},{1,17},{17,1},{2,18},{18,2},{3,19},{19,3},{4,20},{20... | collective-permute-start | bytes 1277960 | tf_op jit(solution)/shard_map/ppermute | solution.py:549
  614.5 8.5 %collective-permute-start.17 = (bf16[32,26,128]{2,0,1:T(8,128)(2,1)S(1)}, bf16[32,26,128]{2,0,1:T(8,128)(2,1)S(1)}, u32[]{:S(2)}, u32[]{:S(2)}) collective-permute-start(bf16[32,26,128]{2,0,1:T(8,128)(2,1)S(1)} %dynamic-slice_bitcast_fusion.4), channel_id=1, source_target_pairs={{0,4},{4,0},{1,5},{5,1},{2,6},{6,2},{3,7},{7,3},{8,12},{12,8},{9,1... | collective-permute-start | bytes 638984 | tf_op jit(solution)/shard_map/ppermute | solution.py:298
  634.7 8.2 %all-to-all-start.5 = ((bf16[4,8,10,256]{3,1,2,0:T(8,128)(2,1)}), bf16[4,8,10,256]{3,1,2,0:T(8,128)(2,1)S(1)}, u32[]{:S(2)}, u32[]{:S(2)}) async-start(bf16[4,8,10,256]{3,1,2,0:T(8,128)(2,1)} %copy.414), calls=%async_computation.5 | async-start | bytes 327680 | tf_op jit(solution)/shard_map/all_to_all | solution.py:328
  642.9 13.4 %all-to-all-start.2 = ((bf16[4,112,512]{2,1,0:T(8,128)(2,1)}), bf16[4,112,512]{2,1,0:T(8,128)(2,1)S(1)}, u32[]{:S(2)}, u32[]{:S(2)}) async-start(bf16[4,112,512]{2,1,0:T(8,128)(2,1)} %bitcast.81), calls=%async_computation.2 | async-start | bytes 917504 | tf_op jit(solution)/shard_map/all_to_all | solution.py:328
  650.9 12.7 %collective-permute-start.13 = (bf16[2,375,512]{2,0,1:T(2,128)(2,1)}, bf16[2,375,512]{2,0,1:T(2,128)(2,1)}, u32[]{:S(2)}, u32[]{:S(2)}) collective-permute-start(bf16[2,375,512]{2,0,1:T(2,128)(2,1)} %bitcast.625), channel_id=1, source_target_pairs={{0,4},{4,0},{1,5},{5,1},{2,6},{6,2},{3,7},{7,3},{8,12},{12,8},{9,1... | collective-permute-start | bytes 2304008 | tf_op jit(solution)/shard_map/ppermute | solution.py:298
  656.4 6.1 collective-permute-start.11
  (133 other events, 811.4 us)

commit v3 on v1

v3 whole, which is shorter than its diff:
```python
import functools

import jax
import jax.numpy as jnp
from jax import lax
from jax.experimental import pallas as pl
from jax.experimental.pallas import tpu as pltpu
from jax.sharding import Mesh, PartitionSpec as P

HD = 64
RANK = 16
epsilon = 1e-05
masked_score = -1e30
f32, bf16 = jnp.float32, jnp.bfloat16
SWAP = ((0, 1), (1, 0))
MESH = pl.DeviceIdType.MESH


def dot(a, b, dims):
    return lax.dot_general(a, b, (dims, ((), ())), preferred_element_type=f32)


def mm(a, b):
    return dot(a, b, ((1,), (0,)))


def mm_t(a, b):
    return dot(a, b, ((1,), (1,)))


def t_mm(a, b):
    return dot(a, b, ((0,), (0,)))


HIDE = -1e30
SCALE = HD**-0.5
EPS = 1e-05
VM = pl.BlockSpec(memory_space=pltpu.VMEM)


def nn(a, b):
    return lax.dot_general(a, b, (((1,), (0,)), ((), ())), preferred_element_type=f32)


def nt(a, b):
    return lax.dot_general(a, b, (((1,), (1,)), ((), ())), preferred_element_type=f32)


def normalize(rows):
    centered = rows - jnp.mean(rows, axis=-1, keepdims=True)
    variance = jnp.mean(centered * centered, axis=-1, keepdims=True)
    inverse = lax.rsqrt(variance + EPS)
    return centered * inverse, inverse


def norm_back(rows, gain, grad):
    unit, inverse = normalize(rows)
    scaled = grad * gain
    first = jnp.mean(scaled, axis=-1, keepdims=True)
    second = jnp.mean(scaled * unit, axis=-1, keepdims=True)
    return (scaled - first - unit * second) * inverse


def pair_lanes(p):
    return pl.ds(pl.multiple_of(p * 128, 128), 128)


def scores_t(keys, queries, frames, causal):
    s = nt(keys, queries) * SCALE
    if causal:
        key = lax.broadcasted_iota(jnp.int32, s.shape, 0)
        query = lax.broadcasted_iota(jnp.int32, s.shape, 1)
        s = jnp.where(query >= key, s, HIDE)
    elif frames < s.shape[0]:
        full = frames // 128 * 128
        key = full + lax.broadcasted_iota(jnp.int32, (s.shape[0] - full, s.shape[1]), 0)
        s = jnp.concatenate([s[:full], jnp.where(key < frames, s[full:], HIDE)])
    return s


def attend_forward(q, k, v, mix, lse, frames, causal, start=0, number=None):
    def pair(p, carry):
        lanes = pair_lanes(p)
        qp, kp = q[:, lanes], k[:, lanes]
        vt = v[:, lanes].T
        first = lax.broadcasted_iota(jnp.int32, qp.shape, 1) < HD
        outs, logs = [], []
        for h in (0, 1):
            s = scores_t(kp, jnp.where(first == (h == 0), qp, 0), frames, causal)
            top = jnp.max(s, axis=0, keepdims=True)
            e = jnp.exp(s - top)
            total = jnp.sum(e, axis=0, keepdims=True)
            probs = (e * (1.0 / total)).astype(bf16)
            outs.append(nn(vt, probs)[h * HD : (h + 1) * HD])
            logs.append(top + jnp.log(total))
        mix[:, lanes] = jnp.concatenate(outs).T.astype(bf16)
        lse[p] = jnp.concatenate(logs)
        return carry

    lax.fori_loop(start, start + (number or q.shape[1] // 128), pair, 0)


def attend_backward(q, k, v, do, lse, dq, dk, dv, frames, causal):
    def pair(p, carry):
        lanes = pair_lanes(p)
        qp, kp, vp, dop = q[:, lanes], k[:, lanes], v[:, lanes], do[:, lanes]
        kt = kp.T
        logs = lse[p]
        first = lax.broadcasted_iota(jnp.int32, qp.shape, 1) < HD
        dqs, dks, dvs = [], [], []
        for h in (0, 1):
            mine = first == (h == 0)
            s = scores_t(kp, jnp.where(mine, qp, 0), frames, causal)
            probs = jnp.exp(s - logs[h : h + 1])
            dvs.append(nn(probs.astype(bf16), dop))
            dp = nt(vp, jnp.where(mine, dop, 0))
            t = probs * dp
            ds = (t - probs * jnp.sum(t, axis=0, keepdims=True)).astype(bf16)
            dks.append(nn(ds, qp))
            dqs.append(nn(kt, ds)[h * HD : (h + 1) * HD])
        first_k = lax.broadcasted_iota(jnp.int32, kp.shape, 1) < HD
        dv[:, lanes] = jnp.where(first_k, dvs[0], dvs[1]).astype(bf16)
        dk[:, lanes] = (jnp.where(first_k, dks[0], dks[1]) * SCALE).astype(bf16)
        dq[:, lanes] = (jnp.concatenate(dqs).T * SCALE).astype(bf16)
        return carry

    lax.fori_loop(0, q.shape[1] // 128, pair, 0)


def params():
    return pltpu.CompilerParams(vmem_limit_bytes=60 * 1024 * 1024)


def sds(shape, dtype):
    return jax.ShapeDtypeStruct(shape, dtype)


def self_forward(tok, gain, shift, wi, wo):
    def kernel(tok, gain, shift, wi, wo, normed, q, k, v, lse, mix, part):
        unit, _ = normalize(tok[...].astype(f32))
        normed[...] = (unit * gain[...] + shift[...]).astype(bf16)
        for i, out in enumerate((q, k, v)):
            out[...] = nn(normed[...], wi[i]).astype(bf16)
        attend_forward(q, k, v, mix, lse, tok.shape[0], True)
        part[...] = nn(mix[...], wo[...])

    r, d = tok.shape
    w = wi.shape[2]
    return pl.pallas_call(kernel, out_shape=[sds((r, d), bf16)] + [sds((r, w), bf16)] * 3 + [sds((w // 128, 2, r), f32), sds((r, w), bf16), sds((r, d), f32)],
        in_specs=[VM] * 5, out_specs=[VM] * 7, compiler_params=params(), name="self_forward")(tok, gain, shift, wi, wo)


def memory_project(enc, wi):
    def kernel(enc, wi, k, v):
        frames = enc.shape[0]
        for i, out in enumerate((k, v)):
            out[:frames] = nn(enc[...], wi[i]).astype(bf16)
            out[frames:] = jnp.zeros((out.shape[0] - frames, out.shape[1]), bf16)
    frames = -(-enc.shape[0] // 128) * 128
    return pl.pallas_call(kernel, out_shape=[sds((frames, wi.shape[2]), bf16)] * 2, in_specs=[VM] * 2, out_specs=[VM] * 2, compiler_params=params(), name="memory_project")(enc, wi)


def cross_forward(hid, part, other, gain, shift, wq, k, v, wo, frames):
    def kernel(hid, part, other, gain, shift, wq, k, v, wo, hidden, normed, q, lse, mix, out):
        hidden[...] = hid[...].astype(f32) + part[...] + other[...]
        unit, _ = normalize(hidden[...])
        normed[...] = (unit * gain[...] + shift[...]).astype(bf16)
        q[...] = nn(normed[...], wq[...]).astype(bf16)
        attend_forward(q, k, v, mix, lse, frames, False)
        out[...] = nn(mix[...], wo[...])

    r, d = hid.shape
    w = wq.shape[1]
    return pl.pallas_call(kernel, out_shape=[sds((r, d), f32), sds((r, d), bf16), sds((r, w), bf16), sds((w // 128, 2, r), f32), sds((r, w), bf16), sds((r, d), f32)],
        in_specs=[VM] * 9, out_specs=[VM] * 6, compiler_params=params(), name="cross_forward")(hid, part, other, gain, shift, wq, k, v, wo)


def rank_t(rows16, inputs):
    return nt(rows16, inputs).astype(bf16)


def feed(hid, part, other, gain, shift, up, down, e, a_up, b_up, a_down, b_down):
    CH = 512

    def kernel(hid, part, other, gain, shift, up, down, e, a_up, b_up, a_down, b_down, hidden, out, back, g_aup, g_bup, g_adown, g_bdown, normed):
        hidden[...] = hid[...] + part[...] + other[...]
        unit, _ = normalize(hidden[...])
        normed[...] = (unit * gain[...] + shift[...]).astype(bf16)
        t_in = rank_t(a_up[...], normed[...])
        r_out = rank_t(b_down[...], e[...])
        r_in = jnp.zeros((16, hid.shape[0]), f32)
        t_out = jnp.zeros((16, hid.shape[0]), f32)
        for j in range(up.shape[1] // CH):
            cols = slice(j * CH, (j + 1) * CH)
            pre = nn(normed[...], up[:, cols])
            cdf = 0.5 * (1.0 + lax.erf(pre * (2**-0.5)))
            active = (pre * cdf).astype(bf16)
            slope = cdf + pre * jnp.exp(-0.5 * pre * pre) * 0.3989422804014327
            grad = (nt(e[...], down[cols]) * slope).astype(bf16)
            term, term_b = nn(active, down[cols]), nt(grad, up[:, cols])
            if j == 0:
                out[...], back[...] = term, term_b
            else:
                out[...] += term
                back[...] += term_b
            g_bup[:, cols] = nn(t_in, grad)
            g_adown[:, cols] = nn(r_out, active)
            r_in += nt(b_up[:, cols], grad)
            t_out += nt(a_down[:, cols], active)
        g_aup[...] = nn(r_in.astype(bf16), normed[...])
        g_bdown[...] = nn(t_out.astype(bf16), e[...])

    r, d = hid.shape
    w = up.shape[1]
    return pl.pallas_call(kernel, out_shape=[sds((r, d), f32)] * 3 + [sds((16, d), f32), sds((16, w), f32), sds((16, w), f32), sds((16, d), f32)],
        in_specs=[VM] * 12, out_specs=[VM] * 7, scratch_shapes=[pltpu.VMEM((r, d), bf16)], compiler_params=params(), name="feed")(
            hid, part, other, gain, shift, up, down, e, a_up, b_up, a_down, b_down)


def cross_backward(hid3, gain3, g, part, other, wo, wq, q, k, v, lse, frames):
    def kernel(hid3, gain3, g, part, other, wo, wq, q, k, v, lse, g_out, e, dq, dk, dv, back, do):
        g_out[...] = g[...].astype(f32) + norm_back(hid3[...], gain3[...], part[...] + other[...])
        e[...] = g_out[...].astype(bf16)
        do[...] = nt(e[...], wo[...]).astype(bf16)
        attend_backward(q, k, v, do, lse, dq, dk, dv, frames, False)
        back[...] = nt(dq[...], wq[...])

    r, d = hid3.shape
    w, f = q.shape[1], k.shape[0]
    return pl.pallas_call(kernel, out_shape=[sds((r, d), f32), sds((r, d), bf16), sds((r, w), bf16), sds((f, w), bf16), sds((f, w), bf16), sds((r, d), f32)],
        in_specs=[VM] * 11, out_specs=[VM] * 6, scratch_shapes=[pltpu.VMEM((r, w), bf16)], compiler_params=params(), name="cross_backward")(
            hid3, gain3, g, part, other, wo, wq, q, k, v, lse)


def self_backward(hid2, gain2, g, part, other, wo, wi, q, k, v, lse):
    def kernel(hid2, gain2, g, part, other, wo, wi, q, k, v, lse, g_out, e, dq, dk, dv, back, do):
        g_out[...] = g[...] + norm_back(hid2[...], gain2[...], part[...] + other[...])
        e[...] = g_out[...].astype(bf16)
        do[...] = nt(e[...], wo[...]).astype(bf16)
        attend_backward(q, k, v, do, lse, dq, dk, dv, q.shape[0], True)
        back[...] = nt(dq[...], wi[0])
        back[...] += nt(dk[...], wi[1])
        back[...] += nt(dv[...], wi[2])

    r, d = hid2.shape
    w = q.shape[1]
    return pl.pallas_call(kernel, out_shape=[sds((r, d), f32), sds((r, d), bf16)] + [sds((r, w), bf16)] * 3 + [sds((r, d), f32)],
        in_specs=[VM] * 11, out_specs=[VM] * 6, scratch_shapes=[pltpu.VMEM((r, w), bf16)], compiler_params=params(), name="self_backward")(
            hid2, gain2, g, part, other, wo, wi, q, k, v, lse)


def final_norm(hid, gain, g, part, other):
    def kernel(hid, gain, g, part, other, out):
        out[...] = (g[...] + norm_back(hid[...].astype(f32), gain[...], part[...] + other[...])).astype(bf16)

    return pl.pallas_call(kernel, out_shape=sds(hid.shape, bf16), in_specs=[VM] * 5, out_specs=VM, compiler_params=params(), name="final_norm")(hid, gain, g, part, other)


def memory_backward(dk, dv, wi, frames):
    def kernel(dk, dv, wi, out):
        out[...] = (nt(dk[:frames], wi[0]) + nt(dv[:frames], wi[1])).astype(bf16)
    d = wi.shape[1]
    return pl.pallas_call(kernel, out_shape=sds((frames, d), bf16), in_specs=[VM] * 3, out_specs=VM, compiler_params=params(), name="memory_backward")(dk, dv, wi)


def attention_ranks(normed, source, mix, dq, dk, dv, e, a_in, b_in, a_out, b_out):
    def kernel(*refs):
        operands, results = refs[:-4], refs[-4:]
        given = operands[:7] if source is not None else operands[:1] + operands[:1] + operands[1:6]
        normed, source_, mix, dq, dk, dv, e = given
        a_in, b_in, a_out, b_out = operands[-4:]
        ga_in, gb_in, ga_out, gb_out = results
        for i, (u, g) in enumerate(((normed, dq), (source_, dk), (source_, dv))):
            rows = u.shape[0]
            inner = rank_t(a_in[i], u[...])
            back = rank_t(b_in[i], g[:rows])
            gb_in[i] = nn(inner, g[:rows]).astype(bf16)
            ga_in[i] = nn(back, u[...]).astype(bf16)
        ga_out[...] = nn(rank_t(b_out[...], e[...]), mix[...]).astype(bf16)
        gb_out[...] = nn(rank_t(a_out[...], mix[...]), e[...]).astype(bf16)

    args = [normed] + ([source] if source is not None else []) + [mix, dq, dk, dv, e, a_in, b_in, a_out, b_out]
    return pl.pallas_call(kernel, out_shape=[sds(t.shape, bf16) for t in (a_in, b_in, a_out, b_out)],
        in_specs=[VM] * len(args), out_specs=[VM] * 4, compiler_params=params(), name="attention_ranks")(*args)


OFFS = (2, 3, 4, 6, 8)


class Unit:
    def __init__(self, place, kind, index):
        self.place, self.tall, self.index = place, kind == "a", index
        self.rows = 512 if self.tall else 128
        late = place >= 10
        if self.tall:
            self.most, self.via_y = (496, 400) if late else (400, 304)
        else:
            self.most, self.via_y = (112, 96) if late else (96, 80)


def make_units():
    order = [("a", 0), ("a", 1), ("a", 2), ("b", 0), ("a", 3), ("a", 4), ("a", 5), ("b", 1)]
    for j in range(4):
        order += [("a", 6 + j), ("b", 2 + j)]
    return [Unit(i, kind, index) for i, (kind, index) in enumerate(order)]


def layer_kernel(
    tok, enc, cot, w_in, w_out, w_up, w_down, ids, gain, shift,
    d_ai, u_ai, d_fi, u_fi, d_ao, u_ao, d_fo, u_fo,
    result, g_rows, g_memory, gsplit, gwhole,
    ga, gb, rows, grads, memory, normed, q0, k0, v0, mix, q1, k1, v1, lse, hidden, g_now, do, dq, dkv,
    outbox, inbox, idbuf, cs, cw, rs, rw, ys, yw, fz, fw, r_in, t_out, r_up,
    core_s, core_r, up_s, dn_s, z_r, y_s, y_r, x_s, x_r, row_s, row_r, loc, ad_s, ad_r, ex_s, ex_r,
):
    units = make_units()
    count = len(units)
    frames = enc.shape[1]
    x, y, c, z = (lax.axis_index(a) for a in ("rep", "sh", "core", "tp"))
    al = pl.multiple_of
    sent = {}

    def when(cond, fn):
        fn() if cond is None else pl.when(cond)(fn)

    def remote(src, dst, s, r, dev):
        return pltpu.make_async_remote_copy(
            src_ref=src, dst_ref=dst, send_sem=s, recv_sem=r, device_id=dev, device_id_type=MESH
        )

    def send(key, cond, src, dst, s, r, dev):
        when(cond, lambda: remote(src, dst, s, r, dev).start())
        sent.setdefault(key, []).append((cond, lambda: remote(src, dst, s, r, dev).wait_send()))

    def settle(key):
        for cond, fn in sent.pop(key, []):
            when(cond, fn)

    X, Y, C = {"rep": 1 - x}, {"sh": 1 - y}, {"core": 1 - c}
    YC = {"sh": 1 - y, "core": 1 - c}
    UP, DOWN = {"tp": z + 1}, {"tp": z - 1}
    others = [lax.rem(z + k, 4) for k in (1, 2, 3)]

    def got(dst, r):
        remote(dst, dst, r, r, X).wait_recv()

    bar = pltpu.get_barrier_semaphore()
    for dev in [X, Y, C, YC] + [{"tp": j} for j in others]:
        pl.semaphore_signal(bar, inc=1, device_id=dev, device_id_type=MESH)
    pl.semaphore_wait(bar, 7)

    def block(u, yy, zz, first, size):
        if u.tall:
            return ga.at[pl.ds(al(u.index * 1024 + yy * 512 + first, 16), size), pl.ds(al(zz * 128, 128), 128)]
        return gb.at[u.index, zz, pl.ds(al(first, 16), size), pl.ds(al(yy * 512, 512), 512)]

    def across(u, yy, first, size):
        if u.tall:
            return ga.at[pl.ds(al(u.index * 1024 + yy * 512 + first, 16), size)]
        return gb.at[u.index, :, pl.ds(al(first, 16), size), pl.ds(al(yy * 512, 512), 512)]

    def three(u, first, size):
        if u.tall:
            return ga.at[pl.ds(al(u.index * 1024 + y * 512 + first, 16), size), 0:384]
        return gb.at[u.index, 0:3, pl.ds(al(first, 16), size), pl.ds(al(y * 512, 512), 512)]

    def half_src(u, cc):
        m = u.index
        if u.tall:
            if m < 6:
                return w_in.at[m, :, pl.ds(al(cc * 128, 128), 128)]
            return w_up.at[:, pl.ds(al(cc * 512 + (m - 6) * 128, 128), 128)]
        if m < 2:
            return w_out.at[m, pl.ds(al(cc * 128, 128), 128)]
        return w_down.at[pl.ds(al(cc * 512 + (m - 2) * 128, 128), 128)]

    def half_dst(u, cc):
        if u.tall:
            return block(u, y, z, cc * 256, 256)
        return gb.at[u.index, z, :, pl.ds(al(y * 512 + cc * 256, 256), 256)]

    def core_exchange(u):
        i = u.place
        send("core", None, half_src(u, 1 - c), half_dst(u, c), core_s.at[i], core_r.at[i], C)
        pltpu.make_async_copy(half_src(u, c), half_dst(u, c), loc.at[i]).start()

    def to_y(u, j):
        b = block(u, y, j, x * (u.rows - u.via_y), u.via_y)
        remote(b, b, y_s.at[u.place], y_r.at[u.place], Y).start()

    def own(u):
        i = u.place
        got(half_dst(u, 1 - c), core_r.at[i])
        pltpu.make_async_copy(half_src(u, c), half_dst(u, c), loc.at[i]).wait()
        zb = block(u, y, z, x * (u.rows - u.most), u.most)
        send(i, z < 3, zb, zb, up_s.at[i, z], z_r.at[i, z], UP)
        send(i, z > 0, zb, zb, dn_s.at[i, z], z_r.at[i, z], DOWN)
        to_y(u, z)

    def hop(u, k):
        i = u.place
        ways = (
            (z >= k, z - k, (z >= k) & (z < 3), UP, up_s),
            (z + k <= 3, z + k, (z + k <= 3) & (z > 0), DOWN, dn_s),
        )
        for ok, j, more, dev, sems in ways:
            zb = block(u, y, j, x * (u.rows - u.most), u.most)

            def arrive(zb=zb, j=j):
                got(zb, z_r.at[i, j])
                to_y(u, j)
                b = block(u, y, j, x * u.most, u.rows - u.most)
                remote(b, b, x_s.at[i, 0], x_r.at[i, 0], X).start()

            when(ok, arrive)
            send(i, more, zb, zb, sems.at[i, j], z_r.at[i, j], dev)

    def cross(u):
        i = u.place
        got(across(u, 1 - y, x * (u.rows - u.via_y), u.via_y), y_r.at[i])
        b = across(u, 1 - y, x * u.via_y, u.rows - u.via_y)
        send(i, None, b, b, x_s.at[i, 1], x_r.at[i, 1], X)

    def last(u):
        i = u.place
        got(three(u, (1 - x) * u.most, u.rows - u.most), x_r.at[i, 0])
        got(across(u, 1 - y, (1 - x) * u.via_y, u.rows - u.via_y), x_r.at[i, 1])
        b = across(u, y, x * (u.rows - u.via_y), u.via_y)
        remote(b, b, y_s.at[i], y_r.at[i], Y).wait_send()
        b = three(u, x * u.most, u.rows - u.most)
        remote(b, b, x_s.at[i, 0], x_r.at[i, 0], X).wait_send()
        settle(i)

    mine = c == z // 2

    def rows_out(src, dst, slot):
        for i in (0, 1):
            zd = 2 * c + i
            d = dst.at[pl.ds(al(z * 112, 16), 112)]
            send("rows", zd != z, src.at[i], d, row_s.at[slot, i], row_r.at[slot, z], {"tp": zd})
            when(
                zd == z,
                lambda i=i, d=d: pltpu.make_async_copy(src.at[i], d, loc.at[count + slot]).start(),
            )

    def rows_in(dst, slot):
        def wait():
            for j in others:
                got(dst.at[pl.ds(al(j * 112, 16), 112)], row_r.at[slot, j])
            d = dst.at[pl.ds(al(z * 112, 16), 112)]
            pltpu.make_async_copy(d, d, loc.at[count + slot]).wait()

        when(mine, wait)
        send("rows", mine, dst, dst, row_s.at[slot, 2], row_r.at[slot, 4], C)

    def rows_have(dst, slot):
        when(c != z // 2, lambda: got(dst, row_r.at[slot, 4]))

    parts = [slice(t * 96, (t + 1) * 96 if t < 15 else frames) for t in range(16)]

    def enc_local(t):
        return pltpu.make_async_copy(
            enc.at[lax.rem(z, 2), parts[t]], memory.at[parts[t]], loc.at[count + 2 + t]
        )

    def enc_send(t):
        send(
            "rows", mine, enc.at[lax.rem(z, 2), parts[t]], memory.at[parts[t]], row_s.at[2, t], row_r.at[2, t], C
        )
        when(mine, lambda: enc_local(t).start())

    def enc_have():
        for t in range(16):
            when(mine, lambda: enc_local(t).wait())
            when(c != z // 2, lambda: got(memory.at[parts[t]], row_r.at[2, t]))

    me = 2 * y + c

    def ids_out():
        for k, dev in enumerate((C, Y, YC)):
            send("ids", None, ids, idbuf.at[me], ad_s.at[k], ad_r.at[k], dev)
        idbuf[pl.ds(me, 1)] = ids[...][None]

    def adapters_pick():
        for k, s in enumerate((2 * y + 1 - c, 2 * (1 - y) + c, 2 * (1 - y) + 1 - c)):
            got(idbuf.at[s], ad_r.at[k])
        held = lax.broadcasted_iota(jnp.int32, (128, 32), 1) + me * 32
        rank = lax.rem(lax.broadcasted_iota(jnp.int32, (128, 32), 0), 16)
        lines = [
            [jnp.broadcast_to(idbuf[2 * s + k // 2, k % 2 : k % 2 + 1, :32], (16, 32)) for k in range(4)]
            for s in range(2)
        ]
        wanted = jnp.concatenate([line for pair in lines for line in pair])
        target = held.astype(f32) - rank.astype(f32)
        picks = jnp.where(wanted * 16.0 == target, 1.0, 0.0).astype(bf16)
        here = []
        for s in range(2):
            line = lines[s][0]
            for k in (1, 2, 3):
                line = jnp.where(z == k, lines[s][k], line)
            here.append(line)
        picks_z = jnp.where(jnp.concatenate(here) * 16.0 == target[:32], 1.0, 0.0).astype(bf16)
        for h in range(2):
            cols = slice(h * 128, h * 128 + 128)
            wide = slice(h * 512, h * 512 + 512)
            given = [u_ai[m][:, cols] for m in range(6)] + [u_fi[:, wide]]
            given += [d_ao[m][:, cols] for m in range(2)] + [d_fo[:, wide]]
            cs[h] = nn(picks, jnp.concatenate(given, axis=1)).astype(bf16)
            if h == 0:
                given = [d_ai[m] for m in range(5)]
            else:
                given = [d_ai[5], d_fi[...], u_ao[0], u_ao[1], u_fo[...]]
            cw[h] = nn(picks_z, jnp.concatenate(given, axis=1)).astype(bf16)
        send("pick", None, cs.at[1 - c], rs, ad_s.at[3], ad_r.at[3], C)
        send("pick", None, cw.at[1 - c], rw, ad_s.at[4], ad_r.at[4], C)

    def adapters_y():
        got(rs, ad_r.at[3])
        got(rw, ad_r.at[4])
        rs[...] += cs[pl.ds(c, 1)][0]
        rw[...] += cw[pl.ds(c, 1)][0]
        send("pick", None, rs.at[pl.ds(al((1 - y) * 64, 64), 64)], ys, ad_s.at[5], ad_r.at[5], Y)
        send("pick", None, rw.at[pl.ds(al((1 - y) * 16, 16), 16)], yw, ad_s.at[6], ad_r.at[6], Y)

    def adapters_z():
        got(ys, ad_r.at[5])
        got(yw, ad_r.at[6])
        ys[...] += rs[pl.ds(al(y * 64, 64), 64)]
        fw[pl.ds(c, 1)] = (yw[...] + rw[pl.ds(al(y * 16, 16), 16)])[None]
        for k, j in enumerate(others):
            send("pick", None, ys.at[pl.ds(al(j * 16, 16), 16)], fz.at[z], ad_s.at[7 + k], ad_r.at[7 + z], {"tp": j})
        fz[pl.ds(z, 1)] = ys[pl.ds(al(z * 16, 16), 16)][None]
        send("pick", None, fw.at[c], fw.at[c], ad_s.at[11], ad_r.at[11], C)

    def adapters_have():
        for j in others:
            got(fz.at[j], ad_r.at[7 + j])
        got(fw.at[1 - c], ad_r.at[11])
        settle("pick")
        settle("ids")

    def whole(m):
        return fw[m // 5, :, (m % 5) * 1024 : (m % 5) * 1024 + 1024]

    def split(s):
        return jnp.concatenate([fz[k, :, s * 128 : s * 128 + 128] for k in range(4)], axis=1)

    def merge(u):
        m = u.index
        if u.tall:
            down_t = whole(min(m, 6)).T
            up_rows = split(m)
            for b in range(4):
                place = slice(m * 1024 + b * 256, m * 1024 + b * 256 + 256)
                ga[place] = (ga[place].astype(f32) + nn(down_t[b * 256 : b * 256 + 256], up_rows)).astype(bf16)
        else:
            down_t = split(10 + m).T
            up_rows = whole(7 + m if m < 2 else 9)
            for k in range(4):
                gb[m, k] = (gb[m, k].astype(f32) + nn(down_t[k * 128 : k * 128 + 128], up_rows)).astype(bf16)

    def wa(m):
        return ga[m * 1024 : (m + 1) * 1024]

    def wb(m):
        return gb[m].reshape(512, 1024)

    def part_out(e, slot):
        send(("part", e), None, outbox.at[slot], inbox.at[slot], ex_s.at[e], ex_r.at[e], C)

    def part_sum(e, slot):
        got(inbox.at[slot], ex_r.at[e])
        return outbox[slot] + inbox[slot]

    def norm_rows(side, source):
        unit, _ = normalize(source)
        normed[side] = (unit * gain[side] + shift[side]).astype(bf16)

    def start_rows():
        rows_have(rows, 0)
        norm_rows(0, rows[...].astype(f32))

    def project(m, source, out, length):
        def run():
            out[:length] = nn(source(), wa(m)).astype(bf16)
        return run

    def attention(side, first, number):
        q, k, v = ((q0, k0, v0), (q1, k1, v1))[side]
        length = (rows.shape[0], frames)[side]
        return lambda: attend_forward(q, k, v, mix.at[side], lse.at[side], length, side == 0, first, number)

    def part0():
        outbox[0] = nn(mix[0], wb(0))
        part_out(0, 0)

    def second_rows():
        hidden[0] = rows[...].astype(f32) + part_sum(0, 0)
        norm_rows(1, hidden[0])

    def fill():
        for out in (k1, v1):
            out[frames:] = jnp.zeros((out.shape[0] - frames, out.shape[1]), bf16)

    def part1():
        outbox[1] = nn(mix[1], wb(1))
        part_out(1, 1)

    def third_rows():
        hidden[1] = hidden[0] + part_sum(1, 1)
        norm_rows(2, hidden[1])
        rows_have(grads, 1)

    def feed_first():
        settle(("part", 0))
        settle(("part", 1))
        r_up[0] = rank_t(whole(6), normed[2])
        r_up[1] = rank_t(whole(9), grads[...])

    def chunk(j):
        def run():
            up, down = wa(6 + j), wb(2 + j)
            pre = nn(normed[2], up)
            cdf = 0.5 * (1.0 + lax.erf(pre * (2**-0.5)))
            active = (pre * cdf).astype(bf16)
            slope = cdf + pre * jnp.exp(-0.5 * pre * pre) * 0.3989422804014327
            grad = (nt(grads[...], down) * slope).astype(bf16)
            if j == 0:
                outbox[1] = nn(active, down)
                outbox[0] = nt(grad, up)
                r_in[...] = nt(split(6 + j), grad)
                t_out[...] = nt(split(12 + j), active)
            else:
                outbox[1] += nn(active, down)
                outbox[0] += nt(grad, up)
                r_in[...] += nt(split(6 + j), grad)
                t_out[...] += nt(split(12 + j), active)
            gsplit[6 + j] = nn(r_up[0], grad).astype(bf16)
            gsplit[12 + j] = nn(r_up[1], active).astype(bf16)
        return run

    tasks = {}

    def task(tick, fn):
        tasks.setdefault(tick, []).append(fn)

    task(1, adapters_pick)
    task(3, adapters_y)
    task(5, adapters_z)
    task(7, adapters_have)
    task(7, lambda: rows_in(rows, 0))
    task(8, start_rows)
    for u in units:
        task(2 * u.place + OFFS[4], functools.partial(merge, u))
    base = OFFS[4]
    task(base + 1, project(0, lambda: normed[0], q0, 448))
    task(base + 3, project(1, lambda: normed[0], k0, 448))
    task(base + 5, project(2, lambda: normed[0], v0, 448))
    task(base + 5, attention(0, 0, 2))
    task(base + 6, attention(0, 2, 2))
    task(base + 7, part0)
    task(base + 9, second_rows)
    task(base + 9, project(3, lambda: normed[1], q1, 448))
    task(base + 10, enc_have)
    task(base + 10, fill)
    task(base + 11, project(4, lambda: memory[...], k1, 1500))
    task(base + 12, project(5, lambda: memory[...], v1, 1500))
    task(base + 13, attention(1, 0, 2))
    task(base + 14, attention(1, 2, 2))
    task(base + 15, part1)
    task(base + 17, third_rows)
    task(base + 18, feed_first)
    task(12, lambda: rows_out(cot, grads, 1))
    task(22, lambda: rows_in(grads, 1))
    for j in range(4):
        task(base + 19 + 4 * j, chunk(j))

    ids_out()
    rows_out(tok, rows, 0)
    for u in units:
        core_exchange(u)
    for t in range(max(2 * count + base, max(tasks)) + 1):
        def at(offset):
            i, odd = divmod(t - offset, 2)
            return units[i] if not odd and 0 <= i < count else None

        if at(0):
            own(at(0))
        for k in (1, 2, 3):
            if at(OFFS[k - 1]):
                hop(at(OFFS[k - 1]), k)
        if at(OFFS[3]):
            cross(at(OFFS[3]))
        if at(OFFS[4]):
            last(at(OFFS[4]))
        if t < 16:
            enc_send(t)
        for fn in tasks.get(t, []):
            fn()

    def to_hbm(src, dst, slot):
        return pltpu.make_async_copy(src, dst, loc.at[count + 18 + slot])

    part_out(3, 0)
    gwhole[6] = nn(r_in[...].astype(bf16), normed[2]).astype(bf16)
    gwhole[9] = nn(t_out[...].astype(bf16), grads[...]).astype(bf16)
    g_now[...] = grads[...].astype(f32) + norm_back(hidden[1], gain[2], part_sum(3, 0))
    part_out(2, 1)
    settle("rows")
    grads[...] = g_now[...].astype(bf16)
    do[...] = nt(grads[...], wb(1)).astype(bf16)
    dk1, dv1 = ga.at[pl.ds(6144, 1536)], ga.at[pl.ds(7680, 1536)]
    attend_backward(q1, k1, v1, do, lse.at[1], dq, dk1, dv1, frames, False)
    settle(("part", 3))
    outbox[0] = nt(dq[...], wa(3))
    normed[2] = (hidden[1] + part_sum(2, 1)).astype(bf16)
    to_hbm(normed.at[2], result, 0).start()
    part_out(4, 0)

    def ranks(side, source, dk, dv):
        for i, (u, g) in enumerate(((normed.at[side], dq), (source, dk), (source, dv))):
            m = 3 * side + i
            held = g[: u.shape[0]]
            inner = rank_t(whole(m), u[...])
            back = rank_t(split(m), held)
            gsplit[m] = nn(inner, held).astype(bf16)
            gwhole[m] = nn(back, u[...]).astype(bf16)
        gsplit[10 + side] = nn(rank_t(whole(7 + side), grads[...]), mix[side]).astype(bf16)
        gwhole[7 + side] = nn(rank_t(split(10 + side), mix[side]), grads[...]).astype(bf16)

    def memory_half(h, place):
        rows_of = [pl.ds(al(m * 1024 + h * 512, 512), 512) for m in (4, 5)]
        return nt(dk1[place], ga[rows_of[0]]) + nt(dv1[place], ga[rows_of[1]])

    thirds = [slice(b * 512, b * 512 + 512) for b in range(3)]
    for place in thirds:
        k1[place] = memory_half(1 - c, place).astype(bf16)
    ranks(1, memory, dk1, dv1)
    g_now[...] += norm_back(hidden[0], gain[1], part_sum(4, 0))
    send("memory", None, k1, v1, ex_s.at[6], ex_r.at[6], C)
    grads[...] = g_now[...].astype(bf16)
    do[...] = nt(grads[...], wb(0)).astype(bf16)
    attend_backward(q0, k0, v0, do, lse.at[0], dq, dkv.at[0], dkv.at[1], rows.shape[0], True)
    settle(("part", 2))
    outbox[1] = nt(dq[...], wa(0))
    outbox[1] += nt(dkv[0], wa(1))
    outbox[1] += nt(dkv[1], wa(2))
    part_out(5, 1)
    got(v1, ex_r.at[6])
    settle("memory")
    for place in thirds:
        k1[place] = (memory_half(c, place) + v1[place].astype(f32)).astype(bf16)
    to_hbm(k1, g_memory, 1).start()
    ranks(0, normed.at[0], dkv.at[0], dkv.at[1])
    normed[1] = (g_now[...] + norm_back(rows[...].astype(f32), gain[0], part_sum(5, 1))).astype(bf16)
    to_hbm(normed.at[1], g_rows, 2).start()
    for src, dst, slot in ((normed.at[2], result, 0), (k1, g_memory, 1), (normed.at[1], g_rows, 2)):
        to_hbm(src, dst, slot).wait()
    for key in list(sent):
        settle(key)


def layer(tok, enc, cot, w_in, w_out, w_up, w_down, ids, gain, shift, *adapters):
    any_ = pl.BlockSpec(memory_space=pl.ANY)
    r, d = 448, tok.shape[2]
    frames = enc.shape[1]
    padded = -(-frames // 512) * 512
    dma = pltpu.SemaphoreType.DMA

    def vm(*shape, dtype=bf16):
        return pltpu.VMEM(shape, dtype)

    n = 16
    return pl.pallas_call(
        layer_kernel,
        out_shape=[sds((r, d), bf16), sds((r, d), bf16), sds((padded, d // 2), bf16), sds((16, 16, 512), bf16), sds((10, 16, d), bf16)],
        in_specs=[any_] * 7 + [VM] * 11,
        out_specs=[any_] * 3 + [VM] * 2,
        scratch_shapes=[
            vm(10 * d, 512), vm(6, 4, 128, d), vm(r, d), vm(r, d), vm(frames, d), vm(3, r, d),
            vm(r, 512), vm(r, 512), vm(r, 512), vm(2, r, 512), vm(r, 512), vm(padded, 512), vm(padded, 512),
            vm(2, 4, 2, r, dtype=f32), vm(2, r, d, dtype=f32), vm(r, d, dtype=f32), vm(r, 512), vm(r, 512), vm(2, r, 512),
            vm(2, r, d, dtype=f32), vm(2, r, d, dtype=f32),
            vm(4, 8, 128, dtype=f32), vm(2, 128, 2048), vm(2, 32, 5120), vm(128, 2048), vm(32, 5120), vm(64, 2048), vm(16, 5120),
            vm(4, 16, 2048), vm(2, 16, 5120), vm(16, r, dtype=f32), vm(16, r, dtype=f32), vm(2, 16, r),
            dma((n,)), dma((n,)), dma((n, 4)), dma((n, 4)), dma((n, 4)), dma((n,)), dma((n,)), dma((n, 2)), dma((n, 2)),
            dma((3, 16)), dma((3, 16)), dma((n + 21,)), dma((12,)), dma((12,)), dma((7,)), dma((7,)),
        ],
        compiler_params=pltpu.CompilerParams(
            collective_id=1, has_side_effects=True, vmem_limit_bytes=61 * 1024 * 1024
        ),
        name="layer",
    )(tok, enc, cot, w_in, w_out, w_up, w_down, ids, gain, shift, *adapters)


def swap_core(rows):
    return lax.ppermute(rows, "core", SWAP)


def core_sum(part):
    return part + swap_core(part)


def own_and_other(stacked):
    core = lax.axis_index("core")
    keep = lax.dynamic_index_in_dim(stacked, core, 0, keepdims=False)
    send = lax.dynamic_index_in_dim(stacked, 1 - core, 0, keepdims=False)
    return keep, swap_core(send)


def in_core_order(own, other):
    first = lax.axis_index("core") == 0
    return jnp.stack([jnp.where(first, own, other), jnp.where(first, other, own)])


def scatter_sh(stacked):
    n = lax.axis_size("sh")
    if n == 2:
        me = lax.axis_index("sh")
        keep = lax.dynamic_index_in_dim(stacked, me, 0, keepdims=False)
        send = lax.dynamic_index_in_dim(stacked, 1 - me, 0, keepdims=False)
        return keep + lax.ppermute(send, "sh", SWAP)
    return lax.psum_scatter(stacked, "sh", scatter_dimension=0, tiled=False)


def over_z(stacked):
    return lax.all_to_all(stacked, "tp", 0, 0, tiled=True)


def half_columns(rows):
    width = rows.shape[-1] // 2
    return lax.dynamic_slice_in_dim(rows, lax.axis_index("core") * width, width, rows.ndim - 1)


def rows_home(half):
    tp = lax.axis_size("tp")
    moved = over_z(half.reshape(tp, half.shape[0] // tp, half.shape[1]))
    own, other = own_and_other(moved.reshape(2, tp // 2, *moved.shape[1:]))
    both = in_core_order(own, other)
    return jnp.moveaxis(both, 0, 2).reshape(both.shape[1], both.shape[2], 2 * half.shape[1])


def rows_here(rows):
    tp = lax.axis_size("tp")
    both = in_core_order(rows, swap_core(rows)).reshape(4, *rows.shape[1:])
    moved = over_z(half_columns(both))
    moved = moved.reshape(tp * rows.shape[1], rows.shape[2] // 2)
    pair = in_core_order(moved, swap_core(moved))
    return jnp.concatenate([pair[0], pair[1]], axis=-1)


def gather_weights(w_attn_in, w_attn_out, w_up, w_down):
    def over_shard(block, axis):
        return lax.all_gather(block, ("sh", "core"), axis=axis, tiled=True)

    def over_tp(block, axis):
        return lax.all_gather(block, "tp", axis=axis, tiled=True)

    core = lax.axis_index("core")

    def half(block, axis):
        width = block.shape[axis] // 2
        return lax.dynamic_slice_in_dim(block, core * width, width, axis)

    w_in = over_tp(half(over_shard(w_attn_in.reshape(6, *w_attn_in.shape[3:]), 1), 2), 2)
    w_out = over_tp(half(over_shard(w_attn_out[0], 2), 1), 1)
    w_first = over_tp(half(over_shard(w_up[0], 0), 1), 1)
    w_second = over_tp(half(over_shard(w_down[0], 1), 0), 0)
    return w_in, w_out, w_first, w_second


def wide_parts(args):
    (
        tokens, encoded, cotangent, adapter_of, w_attn_in, w_attn_out, w_up, w_down, norm_gain, norm_shift,
        down_attn_in, up_attn_in, down_feed_in, up_feed_in, down_attn_out, up_attn_out, down_feed_out, up_feed_out,
    ) = args
    n, tp = lax.axis_size("sh"), lax.axis_size("tp")
    sh, core, z = lax.axis_index("sh"), lax.axis_index("core"), lax.axis_index("tp")
    width = w_attn_in.shape[3] * 2 * n
    held_rows = down_feed_in.shape[1]
    quarter = width // tp
    piece = quarter // 2

    ids = lax.all_gather(adapter_of, ("sh", "core"), tiled=True)

    row_ids = (sh * 2 + core) * held_rows + jnp.arange(held_rows)
    wanted = ids.reshape(n, tp)[:, :, None] * RANK + jnp.arange(RANK)
    picks = (wanted[..., None] == row_ids).astype(bf16)
    whole = jnp.concatenate(
        [
            down_attn_in.reshape(6, held_rows, width),
            down_feed_in,
            up_attn_out[0],
            up_feed_out,
        ]
    )
    def in_quarters(rows):
        return jnp.moveaxis(rows.reshape(held_rows, tp, quarter), 1, 0)

    split = jnp.concatenate(
        [
            up_attn_in.reshape(6, held_rows, quarter),
            in_quarters(up_feed_in[0]),
            down_attn_out[0],
            in_quarters(down_feed_out[0]),
        ]
    )
    picks_z = lax.dynamic_index_in_dim(picks, z, 1, keepdims=False)
    chosen_whole = jnp.einsum("srk,mkd->smrd", picks_z, whole, preferred_element_type=f32).astype(bf16)
    chosen_split = jnp.einsum("szrk,mkd->szmrd", picks, split, preferred_element_type=f32).astype(bf16)
    chosen_whole = core_sum(scatter_sh(chosen_whole))
    chosen_split = over_z(core_sum(scatter_sh(chosen_split)))

    def columns(first, count):
        mine = half_columns(chosen_split[:, first : first + count])
        return jnp.moveaxis(mine, 0, 2).reshape(count, RANK, tp * piece)

    def wide_columns(first):
        mine = lax.dynamic_slice_in_dim(chosen_split[:, first : first + tp], core * 2, 2, 1)
        return jnp.moveaxis(mine, 2, 0).reshape(RANK, tp * 2 * quarter)

    a_in, a_up, b_out, b_down = chosen_whole[:6], chosen_whole[6], chosen_whole[7:9], chosen_whole[9]
    b_in, b_up, a_out, a_down = columns(0, 6), wide_columns(6), columns(6 + tp, 2), wide_columns(8 + tp)

    w_in, w_out, w_first, w_second = gather_weights(w_attn_in, w_attn_out, w_up, w_down)
    taken = rows_here(tokens)
    upstream = rows_here(cotangent)
    mine = lax.dynamic_index_in_dim(encoded, z % 2, 0, keepdims=False)
    memory = jnp.where(core == z // 2, mine, swap_core(mine))

    def merge(weight, down_rows, up_rows):
        return (weight.astype(f32) + t_mm(down_rows, up_rows)).astype(bf16)

    w_in = [merge(w_in[i], a_in[i], b_in[i]) for i in range(6)]
    w_out = [merge(w_out[i], a_out[i], b_out[i]) for i in range(2)]
    w_first = merge(w_first, a_up, b_up)
    w_second = merge(w_second, a_down, b_down)

    gain, shift = norm_gain[0][:, None], norm_shift[0][:, None]
    frames = memory.shape[0]
    w_in = jnp.stack(w_in)
    normed0, q0, k0, v0, lse0, mix0, part = self_forward(taken, gain[0], shift[0], w_in[:3], w_out[0])
    k1, v1 = memory_project(memory, w_in[4:])
    hidden1, normed1, q1, lse1, mix1, part1 = cross_forward(
        taken, part, swap_core(part), gain[1], shift[1], w_in[3], k1, v1, w_out[1], frames
    )
    hidden2, part2, back, g_aup, g_bup, g_adown, g_bdown = feed(
        hidden1, part1, swap_core(part1), gain[2], shift[2], w_first, w_second, upstream, a_up, b_up, a_down, b_down
    )
    result = (hidden2 + core_sum(part2)).astype(bf16)
    grad, e1, dq1, dk1, dv1, back1 = cross_backward(
        hidden2, gain[2], upstream, back, swap_core(back), w_out[1], w_in[3], q1, k1, v1, lse1, frames
    )
    part = memory_backward(dk1, dv1, w_in[4:], frames)
    own, other = own_and_other(jnp.moveaxis(part.reshape(part.shape[0], 2, -1), 1, 0))
    memory_rows = (own.astype(f32) + other.astype(f32)).astype(bf16)
    grad, e0, dq0, dk0, dv0, back0 = self_backward(
        hidden1, gain[1], grad, back1, swap_core(back1), w_out[0], w_in[:3], q0, k0, v0, lse0
    )
    grad = final_norm(taken, gain[0], grad, back0, swap_core(back0))
    ranks1 = attention_ranks(normed1, memory, mix1, dq1, dk1, dv1, e1, a_in[3:], b_in[3:], a_out[1], b_out[1])
    ranks0 = attention_ranks(normed0, None, mix0, dq0, dk0, dv0, e0, a_in[:3], b_in[:3], a_out[0], b_out[0])
    feed_up = jnp.moveaxis(g_bup.reshape(RANK, tp, tp, piece), 2, 0).reshape(tp, RANK, tp * piece)
    feed_down = jnp.moveaxis(g_adown.reshape(RANK, tp, tp, piece), 2, 0).reshape(tp, RANK, tp * piece)
    out_split = jnp.stack([ranks0[2], ranks1[2]])
    out_whole = jnp.stack([ranks0[3], ranks1[3]])
    split_grads = jnp.concatenate([ranks0[1], ranks1[1], feed_up.astype(bf16), out_split, feed_down.astype(bf16)])
    whole_grads = jnp.concatenate(
        [ranks0[0], ranks1[0], g_aup.astype(bf16)[None], out_whole, g_bdown.astype(bf16)[None]]
    )
    here = ids.reshape(n, tp)[sh]
    return result, grad, memory_rows, split_grads, whole_grads, here


def narrow_parts(args):
    (
        tokens, encoded, cotangent, adapter_of, w_attn_in, w_attn_out, w_up, w_down, norm_gain, norm_shift,
        down_attn_in, up_attn_in, down_feed_in, up_feed_in, down_attn_out, up_attn_out, down_feed_out, up_feed_out,
    ) = args

    def six(rows):
        return rows.reshape(6, *rows.shape[3:])

    lines = jnp.pad(adapter_of.astype(f32), (0, 6))[:, None] * jnp.ones((1, 128), f32)
    outs = layer(
        tokens, encoded, cotangent, six(w_attn_in), w_attn_out[0], w_up[0], w_down[0], lines,
        norm_gain[0][:, None], norm_shift[0][:, None], six(down_attn_in), six(up_attn_in), down_feed_in[0],
        up_feed_in[0], down_attn_out[0], up_attn_out[0], down_feed_out[0], up_feed_out[0],
    )
    here = in_core_order(adapter_of, swap_core(adapter_of)).reshape(4)
    return (*outs[:2], outs[2][: encoded.shape[1]], *outs[3:], here)


def on_device(*args):
    n, tp = lax.axis_size("sh"), lax.axis_size("tp")
    held_rows, quarter = args[12].shape[1], args[11].shape[4]
    width, piece = quarter * tp, quarter // 2
    result, grad, memory_rows, split_grads, whole_grads, here = (narrow_parts if n == 2 else wide_parts)(args)
    activations = rows_home(half_columns(result))
    grad_encoded = rows_home(memory_rows).astype(f32)
    grad_tokens = rows_home(half_columns(grad)).astype(f32)
    compact = jnp.moveaxis(split_grads.reshape(-1, RANK, tp, piece), 2, 0)
    own, other = own_and_other(jnp.moveaxis(whole_grads.reshape(-1, RANK, tp, 2, piece), (3, 2), (0, 1)))
    compact = jnp.concatenate([compact, own + other], axis=1)
    compact = over_z(compact)
    rows = jnp.arange(2 * n * held_rows)
    place = (here[:, None] * RANK + jnp.arange(RANK))[None] == rows[:, None, None]
    dense = jnp.einsum("gkr,kmrp->gmp", place.astype(bf16), compact, preferred_element_type=f32)
    dense = dense.astype(bf16).reshape(n, 2, held_rows, *dense.shape[1:])
    dense = scatter_sh(dense)
    dense = dense + lax.ppermute(dense, "rep", SWAP)
    both = in_core_order(*own_and_other(dense))
    done = jnp.moveaxis(both, 0, 2)
    count = 8 + 2 * tp
    sums = done[:, :count].astype(f32)

    def narrow(first, number):
        block = sums[:, first : first + number].reshape(held_rows, number, quarter)
        return jnp.moveaxis(block, 1, 0)

    def wide_of(first):
        block = jnp.moveaxis(sums[:, first : first + tp], 2, 1)
        return block.reshape(held_rows, 2 * tp * piece)

    grad_up_attn_in = narrow(0, 6).reshape(1, 2, 3, held_rows, quarter)
    grad_up_feed_in = wide_of(6)[None]
    grad_down_attn_out = narrow(6 + tp, 2)[None]
    grad_down_feed_out = wide_of(8 + tp)[None]
    rest = done[:, count:].reshape(tp, held_rows // tp, 10, quarter)
    rest = jnp.moveaxis(over_z(rest), 0, 2)
    rest = jnp.moveaxis(rest.reshape(held_rows // tp, 10, width), 1, 0).astype(f32)
    return (
        activations,
        grad_tokens,
        grad_encoded,
        rest[:6].reshape(1, 2, 3, held_rows // tp, width),
        grad_up_attn_in,
        rest[6:7],
        grad_up_feed_in,
        grad_down_attn_out,
        rest[7:9][None],
        grad_down_feed_out,
        rest[9:10],
    )


def solution(mesh):
    rep, shard, tp = (mesh.shape[name] for name in ("rep", "shard", "tp"))
    fine = Mesh(mesh.devices.reshape(rep, shard // 2, 2, tp), ("rep", "sh", "core", "tp"))
    shard = ("sh", "core")
    clips = ("rep", "sh", "core")
    both = ("sh", "core", "tp")
    placed = (
        P(clips, "tp", None),
        P(clips, None, None),
        P(clips, "tp", None),
        P(clips),
        P(None, None, None, shard, "tp"),
        P(None, None, "tp", shard),
        P(None, shard, "tp"),
        P(None, "tp", shard),
        P(),
        P(),
        P(None, None, None, shard, None),
        P(None, None, None, shard, "tp"),
        P(None, shard, None),
        P(None, shard, "tp"),
        P(None, None, shard, "tp"),
        P(None, None, shard, None),
        P(None, shard, "tp"),
        P(None, shard, None),
    )
    return jax.shard_map(
        on_device,
        mesh=fine,
        in_specs=placed,
        out_specs=(
            P(clips, "tp", None),
            P(clips, "tp", None),
            P(clips, "tp", None),
            P(None, None, None, both, None),
            P(None, None, None, shard, "tp"),
            P(None, both, None),
            P(None, shard, "tp"),
            P(None, None, shard, "tp"),
            P(None, None, both, None),
            P(None, shard, "tp"),
            P(None, both, None),
        ),
        check_vma=False,
    )
```

time: 801 us -> 347 us (0.43)
  the two profiles are of different devices: /device:TPU:1 before, /device:TPU:0 now
where the time goes in v3:
time: 347 us; the launch traced here: 341 us
  Pallas kernels  218 us (63%)
  waiting for transfers between devices  64.8 us (19%)
  local copies, waits for them, and re-layouts  30 us (9%)
  starting transfers between devices  23.5 us (7%)
    pallas_call x1, Pallas kernels, layer(): pl.pallas_call(layer_kernel, out_shape=[sds((r, d), bf16), sds((r, d), bf...  218 us
    all_to_all x5, waiting for transfers between devices, over_z(): return lax.all_to_all(stacked, 'tp', 0, 0, tiled=True)  51.7 us
    all_to_all x5, starting transfers between devices, over_z(): return lax.all_to_all(stacked, 'tp', 0, 0, tiled=True)  20.8 us
    unnamed x14, local copies, waits for them, and re-layouts  11.5 us
    ppermute x1, waiting for transfers between devices, on_device(): dense = dense + lax.ppermute(dense, 'rep', SWAP)  10.8 us
  transfers between devices with their start and end apart: 13, of which 8 were waited for; matrix products, arithmetic and copies ran while one was open for 7% of the time, Pallas kernels for 0%

profile of v3, /device:TPU:0, one launch (start us, length us, event | category | flops | bytes accessed | tf_op | source)
XLA Modules:
  0.0 341.5 jit_solution(8866775052989459597)
XLA Ops:
  1.2 7.3 %copy.96.enc = bf16[2,1500,1024]{2,1,0:T(8,128)(2,1)} copy(bf16[2,1500,1024]{2,0,1:T(2,128)(2,1)} %param.19) | data formatting | bytes 12288000 | tf_op args[1]
  9.2 218.1 %layer.1 = (bf16[448,1024]{1,0:T(8,128)(2,1)}, bf16[448,1024]{1,0:T(8,128)(2,1)}, bf16[1536,512]{1,0:T(8,128)(2,1)}, bf16[16,16,512]{2,1,0:T(8,128)(2,1)}, bf16[10,16,1024]{2,1,0:T(8,128)(2,1)}) custom-call(bf16[2,112,1024]{2,1,0:T(8,128)(2,1)} %tok.1, bf16[2,1500,1024]{2,1,0:T(8,128)(2,1)} %copy.96.enc, bf16[2,112,1024]{2,1,0:T(8,128)(2,1)} %cot.1, ...), custom_call_target="tpu_custom_call" | custom-call | tf_op jit(solution)/shard_map/layer/pallas_call | solution.py:774
  227.3 1.9 constant_dynamic-slice_fusion.6
  229.2 7.0 %all-to-all-start = ((bf16[4,112,512]{2,1,0:T(8,128)(2,1)}), bf16[4,112,512]{2,1,0:T(8,128)(2,1)S(1)}, u32[]{:S(2)}, u32[]{:S(2)}) async-start(bf16[4,112,512]{2,1,0:T(8,128)(2,1)} %bitcast.14), calls=%async_computation | async-start | bytes 917504 | tf_op jit(solution)/shard_map/all_to_all | solution.py:827
  238.1 1.0 collective-permute-done.4
  239.9 10.5 %all-to-all-done = bf16[4,112,512]{2,1,0:T(8,128)(2,1)S(1)} async-done(((bf16[4,112,512]{2,1,0:T(8,128)(2,1)}), bf16[4,112,512]{2,1,0:T(8,128)(2,1)S(1)}, u32[]{:S(2)}, u32[]{:S(2)}) %all-to-all-start) | async-done | bytes 458784 | tf_op jit(solution)/shard_map/all_to_all | solution.py:827
  250.4 3.5 %all-to-all-start.3 = ((bf16[4,26,16,128]{3,2,1,0:T(8,128)(2,1)}), bf16[4,26,16,128]{3,2,1,0:T(8,128)(2,1)S(1)}, u32[]{:S(2)}, u32[]{:S(2)}) async-start(bf16[4,26,16,128]{3,2,1,0:T(8,128)(2,1)} %pad_maximum_fusion), calls=%async_computation.3 | async-start | bytes 851968 | tf_op jit(solution)/shard_map/all_to_all | solution.py:827
  254.9 11.7 %all-to-all-done.3 = bf16[4,26,16,128]{3,2,1,0:T(8,128)(2,1)S(1)} async-done(((bf16[4,26,16,128]{3,2,1,0:T(8,128)(2,1)}), bf16[4,26,16,128]{3,2,1,0:T(8,128)(2,1)S(1)}, u32[]{:S(2)}, u32[]{:S(2)}) %all-to-all-start.3) | async-done | bytes 426016 | tf_op jit(solution)/shard_map/all_to_all | solution.py:827
  266.6 3.5 %all-to-all-start.1 = ((bf16[4,112,512]{2,1,0:T(8,128)(2,1)}), bf16[4,112,512]{2,1,0:T(8,128)(2,1)S(1)}, u32[]{:S(2)}, u32[]{:S(2)}) async-start(bf16[4,112,512]{2,1,0:T(8,128)(2,1)} %bitcast.21), calls=%async_computation.1 | async-start | bytes 917504 | tf_op jit(solution)/shard_map/all_to_all | solution.py:827
  271.4 1.1 collective-permute-start.5
  272.6 1.5 reshape.122
  274.9 7.8 %all-to-all-done.1 = bf16[4,112,512]{2,1,0:T(8,128)(2,1)S(1)} async-done(((bf16[4,112,512]{2,1,0:T(8,128)(2,1)}), bf16[4,112,512]{2,1,0:T(8,128)(2,1)S(1)}, u32[]{:S(2)}, u32[]{:S(2)}) %all-to-all-start.1) | async-done | bytes 458784 | tf_op jit(solution)/shard_map/all_to_all | solution.py:827
  282.7 3.6 %all-to-all-start.2 = ((bf16[4,375,512]{2,1,0:T(8,128)(2,1)}), bf16[4,375,512]{2,1,0:T(8,128)(2,1)S(1)}, u32[]{:S(2)}, u32[]{:S(2)}) async-start(bf16[4,375,512]{2,1,0:T(8,128)(2,1)} %reshape.122), calls=%async_computation.2 | async-start | bytes 3080192 | tf_op jit(solution)/shard_map/all_to_all | solution.py:827
  286.6 1.3 collective-permute-done.1
  287.9 10.8 %collective-permute-done.6 = bf16[2,32,26,128]{3,1,2,0:T(8,128)(2,1)S(1)} collective-permute-done((bf16[2,32,26,128]{3,1,2,0:T(8,128)(2,1)S(1)}, bf16[2,32,26,128]{3,1,2,0:T(8,128)(2,1)S(1)}, u32[]{:S(2)}, u32[]{:S(2)}) %collective-permute-start.6) | collective-permute-done | bytes 426016 | tf_op jit(solution)/shard_map/ppermute | solution.py:1011
  299.0 0.8 copy.123
  299.8 1.0 copy.124
  302.7 19.2 %all-to-all-done.2 = bf16[4,375,512]{2,1,0:T(8,128)(2,1)S(1)} async-done(((bf16[4,375,512]{2,1,0:T(8,128)(2,1)}), bf16[4,375,512]{2,1,0:T(8,128)(2,1)S(1)}, u32[]{:S(2)}, u32[]{:S(2)}) %all-to-all-start.2) | async-done | bytes 1536032 | tf_op jit(solution)/shard_map/all_to_all | solution.py:827
  321.9 3.3 all-to-all-start.4
  325.4 1.5 copy.142
  329.1 2.5 all-to-all-done.4
  333.7 1.8 convert_bitcast_fusion
  335.5 2.4 copy.102
  337.9 3.3 copy.116
  (69 shorter events, 14.0 us)
Async XLA Ops:
  0.6 7.8 %collective-permute-start.3 = (s32[2]{0:T(128)}, s32[2]{0:T(128)S(1)}, u32[]{:S(2)}, u32[]{:S(2)}) collective-permute-start(s32[2]{0:T(128)} %param.21), channel_id=1, source_target_pairs={{0,4},{4,0},{1,5},{5,1},{2,6},{6,2},{3,7},{7,3},{8,12},{12,8},{9,1... | collective-permute-start | bytes 32 | tf_op jit(solution)/shard_map/ppermute | solution.py:797
  1.2 7.3 %copy-start.4 = (s32[2]{0:T(128)S(1)}, s32[2]{0:T(128)}, u32[]{:S(2)}) copy-start(s32[2]{0:T(128)} %param.21) | copy-start | bytes 28
  227.3 8.9 %copy-start.1 = (bf16[10,16,1024]{2,1,0:T(8,128)(2,1)S(1)}, bf16[10,16,1024]{2,1,0:T(8,128)(2,1)}, u32[]{:S(2)}) copy-start(bf16[10,16,1024]{2,1,0:T(8,128)(2,1)} %get-tuple-element.20) | copy-start | bytes 983044
  229.2 8.9 %copy-start.2 = (bf16[16,16,512]{2,1,0:T(8,128)(2,1)S(1)}, bf16[16,16,512]{2,1,0:T(8,128)(2,1)}, u32[]{:S(2)}) copy-start(bf16[16,16,512]{2,1,0:T(8,128)(2,1)} %get-tuple-element.19) | copy-start | bytes 786436
  229.2 21.3 %all-to-all-start = ((bf16[4,112,512]{2,1,0:T(8,128)(2,1)}), bf16[4,112,512]{2,1,0:T(8,128)(2,1)S(1)}, u32[]{:S(2)}, u32[]{:S(2)}) async-start(bf16[4,112,512]{2,1,0:T(8,128)(2,1)} %bitcast.14), calls=%async_computation | async-start | bytes 917504 | tf_op jit(solution)/shard_map/all_to_all | solution.py:827
  237.2 16.8 %copy-start.3 = (bf16[448,1024]{1,0:T(8,128)(2,1)S(1)}, bf16[448,1024]{1,0:T(8,128)(2,1)}, u32[]{:S(2)}) copy-start(bf16[448,1024]{1,0:T(8,128)(2,1)} %get-tuple-element.17) | copy-start | bytes 2752516
  237.2 1.8 collective-permute-start.4
  250.4 16.1 %all-to-all-start.3 = ((bf16[4,26,16,128]{3,2,1,0:T(8,128)(2,1)}), bf16[4,26,16,128]{3,2,1,0:T(8,128)(2,1)S(1)}, u32[]{:S(2)}, u32[]{:S(2)}) async-start(bf16[4,26,16,128]{3,2,1,0:T(8,128)(2,1)} %pad_maximum_fusion), calls=%async_computation.3 | async-start | bytes 851968 | tf_op jit(solution)/shard_map/all_to_all | solution.py:827
  266.6 16.1 %all-to-all-start.1 = ((bf16[4,112,512]{2,1,0:T(8,128)(2,1)}), bf16[4,112,512]{2,1,0:T(8,128)(2,1)S(1)}, u32[]{:S(2)}, u32[]{:S(2)}) async-start(bf16[4,112,512]{2,1,0:T(8,128)(2,1)} %bitcast.21), calls=%async_computation.1 | async-start | bytes 917504 | tf_op jit(solution)/shard_map/all_to_all | solution.py:827
  270.6 1.9 copy-start
  271.4 14.9 %collective-permute-start.5 = (bf16[2,32,26,128]{3,1,2,0:T(8,128)(2,1)}, bf16[2,32,26,128]{3,1,2,0:T(8,128)(2,1)S(1)}, u32[]{:S(2)}, u32[]{:S(2)}) collective-permute-start(bf16[2,32,26,128]{3,1,2,0:T(8,128)(2,1)} %bitcast.156), channel_id=1, source_target_pairs={{0,8},{8,0},{1,9},{9,1},{2,10},{10,2},{3,11},{11,3},{4,12},{12,4},... | collective-permute-start | bytes 1277960 | tf_op jit(solution)/shard_map/ppermute | solution.py:822
  274.8 11.7 %collective-permute-start = (bf16[2,112,512]{2,1,0:T(8,128)(2,1)}, bf16[2,112,512]{2,1,0:T(8,128)(2,1)S(1)}, u32[]{:S(2)}, u32[]{:S(2)}) collective-permute-start(bf16[2,112,512]{2,1,0:T(8,128)(2,1)} %dynamic-slice_bitcast_fusion.1), channel_id=1, source_target_pairs={{0,4},{4,0},{1,5},{5,1},{2,6},{6,2},{3,7},{7,3},{8,12},{12,8},{9,1... | collective-permute-start | bytes 688136 | tf_op jit(solution)/shard_map/ppermute | solution.py:797
  282.7 39.3 %all-to-all-start.2 = ((bf16[4,375,512]{2,1,0:T(8,128)(2,1)}), bf16[4,375,512]{2,1,0:T(8,128)(2,1)S(1)}, u32[]{:S(2)}, u32[]{:S(2)}) async-start(bf16[4,375,512]{2,1,0:T(8,128)(2,1)} %reshape.122), calls=%async_computation.2 | async-start | bytes 3080192 | tf_op jit(solution)/shard_map/all_to_all | solution.py:827
  286.3 1.6 collective-permute-start.1
  286.4 12.3 %collective-permute-start.6 = (bf16[2,32,26,128]{3,1,2,0:T(8,128)(2,1)S(1)}, bf16[2,32,26,128]{3,1,2,0:T(8,128)(2,1)S(1)}, u32[]{:S(2)}, u32[]{:S(2)}) collective-permute-start(bf16[2,32,26,128]{3,1,2,0:T(8,128)(2,1)S(1)} %fusion.2), channel_id=1, source_target_pairs={{0,16},{16,0},{1,17},{17,1},{2,18},{18,2},{3,19},{19,3},{4,20},{20... | collective-permute-start | bytes 1277960 | tf_op jit(solution)/shard_map/ppermute | solution.py:1011
  298.8 2.0 collective-permute-start.7
  321.9 9.6 %all-to-all-start.4 = ((bf16[4,8,10,256]{3,1,2,0:T(8,128)(2,1)}), bf16[4,8,10,256]{3,1,2,0:T(8,128)(2,1)S(1)}, u32[]{:S(2)}, u32[]{:S(2)}) async-start(bf16[4,8,10,256]{3,1,2,0:T(8,128)(2,1)} %copy.110), calls=%async_computation.4 | async-start | bytes 327680 | tf_op jit(solution)/shard_map/all_to_all | solution.py:827
  326.8 6.7 %collective-permute-start.2 = (bf16[2,375,512]{2,0,1:T(2,128)(2,1)}, bf16[2,375,512]{2,0,1:T(2,128)(2,1)S(1)}, u32[]{:S(2)}, u32[]{:S(2)}) collective-permute-start(bf16[2,375,512]{2,0,1:T(2,128)(2,1)} %bitcast.155), channel_id=1, source_target_pairs={{0,4},{4,0},{1,5},{5,1},{2,6},{6,2},{3,7},{7,3},{8,12},{12,8},{9,1... | collective-permute-start | bytes 2304008 | tf_op jit(solution)/shard_map/ppermute | solution.py:797

commit v4 on v3

--- a/solution.py
+++ b/solution.py
@@ -65,20 +65,22 @@
     return pl.ds(pl.multiple_of(p * 128, 128), 128)
 
 
-def scores_t(keys, queries, frames, causal):
+def scores_t(keys, queries, frames, causal, groups=1):
     s = nt(keys, queries) * SCALE
     if causal:
         key = lax.broadcasted_iota(jnp.int32, s.shape, 0)
         query = lax.broadcasted_iota(jnp.int32, s.shape, 1)
         s = jnp.where(query >= key, s, HIDE)
     elif frames < s.shape[0]:
-        full = frames // 128 * 128
-        key = full + lax.broadcasted_iota(jnp.int32, (s.shape[0] - full, s.shape[1]), 0)
-        s = jnp.concatenate([s[:full], jnp.where(key < frames, s[full:], HIDE)])
+        step, used = s.shape[0] // groups, frames // groups
+        kept = used // 16 * 16
+        key = kept + lax.broadcasted_iota(jnp.int32, (step - kept, s.shape[1]), 0)
+        blocks = [s[g * step : (g + 1) * step] for g in range(groups)]
+        s = jnp.concatenate([part for b in blocks for part in (b[:kept], jnp.where(key < used, b[kept:], HIDE))])
     return s
 
 
-def attend_forward(q, k, v, mix, lse, frames, causal, start=0, number=None):
+def attend_forward(q, k, v, mix, lse, frames, causal, start=0, number=None, groups=1):
     def pair(p, carry):
         lanes = pair_lanes(p)
         qp, kp = q[:, lanes], k[:, lanes]
@@ -86,7 +88,7 @@
         first = lax.broadcasted_iota(jnp.int32, qp.shape, 1) < HD
         outs, logs = [], []
         for h in (0, 1):
-            s = scores_t(kp, jnp.where(first == (h == 0), qp, 0), frames, causal)
+            s = scores_t(kp, jnp.where(first == (h == 0), qp, 0), frames, causal, groups)
             top = jnp.max(s, axis=0, keepdims=True)
             e = jnp.exp(s - top)
             total = jnp.sum(e, axis=0, keepdims=True)
@@ -100,7 +102,7 @@
     lax.fori_loop(start, start + (number or q.shape[1] // 128), pair, 0)
 
 
-def attend_backward(q, k, v, do, lse, dq, dk, dv, frames, causal):
+def attend_backward(q, k, v, do, lse, dq, dk, dv, frames, causal, start=0, number=None, groups=1):
     def pair(p, carry):
         lanes = pair_lanes(p)
         qp, kp, vp, dop = q[:, lanes], k[:, lanes], v[:, lanes], do[:, lanes]
@@ -110,7 +112,7 @@
         dqs, dks, dvs = [], [], []
         for h in (0, 1):
             mine = first == (h == 0)
-            s = scores_t(kp, jnp.where(mine, qp, 0), frames, causal)
+            s = scores_t(kp, jnp.where(mine, qp, 0), frames, causal, groups)
             probs = jnp.exp(s - logs[h : h + 1])
             dvs.append(nn(probs.astype(bf16), dop))
             dp = nt(vp, jnp.where(mine, dop, 0))
@@ -124,7 +126,7 @@
         dq[:, lanes] = (jnp.concatenate(dqs).T * SCALE).astype(bf16)
         return carry
 
-    lax.fori_loop(0, q.shape[1] // 128, pair, 0)
+    lax.fori_loop(start, start + (number or q.shape[1] // 128), pair, 0)
 
 
 def params():
@@ -308,14 +310,16 @@
 def layer_kernel(
     tok, enc, cot, w_in, w_out, w_up, w_down, ids, gain, shift,
     d_ai, u_ai, d_fi, u_fi, d_ao, u_ao, d_fo, u_fo,
-    result, g_rows, g_memory, gsplit, gwhole,
-    ga, gb, rows, grads, memory, normed, q0, k0, v0, mix, q1, k1, v1, lse, hidden, g_now, do, dq, dkv,
-    outbox, inbox, idbuf, cs, cw, rs, rw, ys, yw, fz, fw, r_in, t_out, r_up,
-    core_s, core_r, up_s, dn_s, z_r, y_s, y_r, x_s, x_r, row_s, row_r, loc, ad_s, ad_r, ex_s, ex_r,
+    acts, g_tok, g_enc, split_sum, whole_sum,
+    ga, gb, rows, grads, memory, normed, q0, k0, v0, mix, q1, k1, v1, lse, hidden, g_now, dd, dkv,
+    outbox, inbox, idbuf, rs, rw, ys, yw, ys_own, yw_own, fz, fw, r_in, t_out, r_up, gsplit, gwhole, wz,
+    rwb0, rwb1, rwb2, czs0, czs1, czs2, czw0, czw1, czw2, sb0, sb1, sb2, yb0, yb1, yb2, xb0, xb1, xb2, cb0, cb1, cb2,
+    core_s, core_r, up_s, dn_s, z_r, y_s, y_r, x_s, x_r, row_s, row_r, loc, ad_s, ad_r, ex_s, ex_r, b_s, b_r, home_s, home_r,
 ):
     units = make_units()
     count = len(units)
-    frames = enc.shape[1]
+    frames, groups = 1500 * enc.shape[1] // 1536, 4
+    do, dq = dd.at[0], dd.at[1]
     x, y, c, z = (lax.axis_index(a) for a in ("rep", "sh", "core", "tp"))
     al = pl.multiple_of
     sent = {}
@@ -345,9 +349,9 @@
         remote(dst, dst, r, r, X).wait_recv()
 
     bar = pltpu.get_barrier_semaphore()
-    for dev in [X, Y, C, YC] + [{"tp": j} for j in others]:
+    for dev in [X, Y, C, YC] + [{"tp": j} for j in others] + [{"tp": j, "core": 1 - c} for j in others]:
         pl.semaphore_signal(bar, inc=1, device_id=dev, device_id_type=MESH)
-    pl.semaphore_wait(bar, 7)
+    pl.semaphore_wait(bar, 10)
 
     def block(u, yy, zz, first, size):
         if u.tall:
@@ -456,7 +460,7 @@
     def rows_have(dst, slot):
         when(c != z // 2, lambda: got(dst, row_r.at[slot, 4]))
 
-    parts = [slice(t * 96, (t + 1) * 96 if t < 15 else frames) for t in range(16)]
+    parts = [slice(t * 96, (t + 1) * 96) for t in range(16)]
 
     def enc_local(t):
         return pltpu.make_async_copy(
@@ -465,7 +469,7 @@
 
     def enc_send(t):
         send(
-            "rows", mine, enc.at[lax.rem(z, 2), parts[t]], memory.at[parts[t]], row_s.at[2, t], row_r.at[2, t], C
+            "enc", mine, enc.at[lax.rem(z, 2), parts[t]], memory.at[parts[t]], row_s.at[2, t], row_r.at[2, t], C
         )
         when(mine, lambda: enc_local(t).start())
 
@@ -505,28 +509,38 @@
             wide = slice(h * 512, h * 512 + 512)
             given = [u_ai[m][:, cols] for m in range(6)] + [u_fi[:, wide]]
             given += [d_ao[m][:, cols] for m in range(2)] + [d_fo[:, wide]]
-            cs[h] = nn(picks, jnp.concatenate(given, axis=1)).astype(bf16)
+            for b in range(4):
+                block_of = jnp.concatenate(given, axis=1)[:, b * 512 : b * 512 + 512]
+                dkv[h, b * 128 : b * 128 + 128] = nn(picks, block_of).astype(bf16)
             if h == 0:
                 given = [d_ai[m] for m in range(5)]
             else:
-                given = [d_ai[5], d_fi[...], u_ao[0], u_ao[1], u_fo[...]]
-            cw[h] = nn(picks_z, jnp.concatenate(given, axis=1)).astype(bf16)
-        send("pick", None, cs.at[1 - c], rs, ad_s.at[3], ad_r.at[3], C)
-        send("pick", None, cw.at[1 - c], rw, ad_s.at[4], ad_r.at[4], C)
+                given = [d_ai[5], d_fi, u_ao[0], u_ao[1], u_fo]
+            for b in range(10):
+                block_of = given[b // 2][:, b % 2 * 512 : b % 2 * 512 + 512]
+                dd[h, b * 32 : b * 32 + 32] = nn(picks_z, block_of).astype(bf16)
+        send("pick", None, dkv.at[1 - c], rs, ad_s.at[3], ad_r.at[3], C)
+        send("pick", None, dd.at[1 - c, 0:320], rw, ad_s.at[4], ad_r.at[4], C)
 
     def adapters_y():
         got(rs, ad_r.at[3])
         got(rw, ad_r.at[4])
-        rs[...] += cs[pl.ds(c, 1)][0]
-        rw[...] += cw[pl.ds(c, 1)][0]
-        send("pick", None, rs.at[pl.ds(al((1 - y) * 64, 64), 64)], ys, ad_s.at[5], ad_r.at[5], Y)
-        send("pick", None, rw.at[pl.ds(al((1 - y) * 16, 16), 16)], yw, ad_s.at[6], ad_r.at[6], Y)
+        rs[...] += dkv[pl.ds(c, 1)][0]
+        rw[...] += dd[pl.ds(c, 1), 0:320][0]
+        for b in range(4):
+            for k in range(2):
+                ys_own[k, :, b * 512 : b * 512 + 512] = rs[b * 128 + k * 64 : b * 128 + k * 64 + 64]
+        for b in range(10):
+            for k in range(2):
+                yw_own[k, :, b * 512 : b * 512 + 512] = rw[b * 32 + k * 16 : b * 32 + k * 16 + 16]
+        send("pick", None, ys_own.at[1 - y], ys, ad_s.at[5], ad_r.at[5], Y)
+        send("pick", None, yw_own.at[1 - y], yw, ad_s.at[6], ad_r.at[6], Y)
 
     def adapters_z():
         got(ys, ad_r.at[5])
         got(yw, ad_r.at[6])
-        ys[...] += rs[pl.ds(al(y * 64, 64), 64)]
-        fw[pl.ds(c, 1)] = (yw[...] + rw[pl.ds(al(y * 16, 16), 16)])[None]
+        ys[...] += ys_own[pl.ds(y, 1)][0]
+        fw[pl.ds(c, 1)] = (yw[...] + yw_own[pl.ds(y, 1)][0])[None]
         for k, j in enumerate(others):
             send("pick", None, ys.at[pl.ds(al(j * 16, 16), 16)], fz.at[z], ad_s.at[7 + k], ad_r.at[7 + z], {"tp": j})
         fz[pl.ds(z, 1)] = ys[pl.ds(al(z * 16, 16), 16)][None]
@@ -588,7 +602,7 @@
     def attention(side, first, number):
         q, k, v = ((q0, k0, v0), (q1, k1, v1))[side]
         length = (rows.shape[0], frames)[side]
-        return lambda: attend_forward(q, k, v, mix.at[side], lse.at[side], length, side == 0, first, number)
+        return lambda: attend_forward(q, k, v, mix.at[side], lse.at[side], length, side == 0, first, number, groups)
 
     def part0():
         outbox[0] = nn(mix[0], wb(0))
@@ -597,10 +611,6 @@
     def second_rows():
         hidden[0] = rows[...].astype(f32) + part_sum(0, 0)
         norm_rows(1, hidden[0])
-
-    def fill():
-        for out in (k1, v1):
-            out[frames:] = jnp.zeros((out.shape[0] - frames, out.shape[1]), bf16)
 
     def part1():
         outbox[1] = nn(mix[1], wb(1))
@@ -635,8 +645,8 @@
                 outbox[0] += nt(grad, up)
                 r_in[...] += nt(split(6 + j), grad)
                 t_out[...] += nt(split(12 + j), active)
-            gsplit[6 + j] = nn(r_up[0], grad).astype(bf16)
-            gsplit[12 + j] = nn(r_up[1], active).astype(bf16)
+            gsplit[j] = nn(r_up[0], grad).astype(bf16)
+            gsplit[4 + j] = nn(r_up[1], active).astype(bf16)
         return run
 
     tasks = {}
@@ -662,9 +672,8 @@
     task(base + 9, second_rows)
     task(base + 9, project(3, lambda: normed[1], q1, 448))
     task(base + 10, enc_have)
-    task(base + 10, fill)
-    task(base + 11, project(4, lambda: memory[...], k1, 1500))
-    task(base + 12, project(5, lambda: memory[...], v1, 1500))
+    task(base + 11, project(4, lambda: memory[...], k1, 1536))
+    task(base + 12, project(5, lambda: memory[...], v1, 1536))
     task(base + 13, attention(1, 0, 2))
     task(base + 14, attention(1, 2, 2))
     task(base + 15, part1)
@@ -698,64 +707,233 @@
         for fn in tasks.get(t, []):
             fn()
 
-    def to_hbm(src, dst, slot):
-        return pltpu.make_async_copy(src, dst, loc.at[count + 18 + slot])
-
+    boxes = list(
+        zip(
+            (rwb0, rwb1, rwb2), (czs0, czs1, czs2), (czw0, czw1, czw2), (sb0, sb1, sb2), (yb0, yb1, yb2),
+            (xb0, xb1, xb2), (cb0, cb1, cb2), ((0, 8, 0, 1), (8, 4, 2, 2), (12, 4, 6, 2)), strict=True,
+        )
+    )
+
+    def home_core(b):
+        rwb, first, half = boxes[b][0], boxes[b][7][2], boxes[b][7][3]
+        send(("home", b), None, gwhole.at[pl.ds(first + (1 - c) * half, half)], rwb, b_s.at[b, 0], b_r.at[b, 0], C)
+
+    def home_z(b):
+        rwb, czs, czw = boxes[b][:3]
+        s0, ns, first, half = boxes[b][7]
+        got(rwb, b_r.at[b, 0])
+        rwb[...] += gwhole[pl.ds(first + c * half, half)]
+
+        def cuts(j):
+            return gsplit.at[s0 : s0 + ns, :, pl.ds(al(j * 128, 128), 128)], rwb.at[:, :, pl.ds(al(j * 256, 256), 256)]
+
+        for k, j in enumerate(others):
+            one, two = cuts(j)
+            send(("home", b), None, one, czs.at[z], b_s.at[b, 1 + k], b_r.at[b, 1 + z], {"tp": j})
+            send(("home", b), None, two, czw.at[z], b_s.at[b, 5 + k], b_r.at[b, 5 + z], {"tp": j})
+        one, two = cuts(z)
+        czs[pl.ds(z, 1)] = one[...][None]
+        czw[pl.ds(z, 1)] = two[...][None]
+
+    def dense_rows(b, to):
+        czs, czw, (_, ns, _, half) = boxes[b][1], boxes[b][2], boxes[b][7]
+        stack = jnp.concatenate(
+            [jnp.concatenate([czs[k, s] for s in range(ns)] + [czw[k, w] for w in range(half)], axis=1) for k in range(4)]
+        )
+        row = lax.broadcasted_iota(jnp.int32, (64, 64), 0)
+        col = lax.broadcasted_iota(jnp.int32, (64, 64), 1)
+        clip = col // 16
+        chosen = jnp.zeros((64, 64), f32)
+        for k in range(4):
+            line = idbuf[pl.ds(2 * y + k // 2, 1), k % 2 : k % 2 + 1, :64][0]
+            chosen = jnp.where(clip == k, jnp.broadcast_to(line, (64, 64)), chosen)
+        target = (row + 64 * to - lax.rem(col, 16)).astype(f32)
+        return nn(jnp.where(chosen * 16.0 == target, 1.0, 0.0).astype(bf16), stack)
+
+    def home_y(b):
+        _, czs, czw, sb, yb = boxes[b][:5]
+        for j in others:
+            got(czs.at[j], b_r.at[b, 1 + j])
+            got(czw.at[j], b_r.at[b, 5 + j])
+        sb[...] = dense_rows(b, 1 - y).astype(bf16)
+        send(("home", b), None, sb, yb, b_s.at[b, 9], b_r.at[b, 9], Y)
+
+    def home_x(b):
+        yb, xb = boxes[b][4:6]
+        got(yb, b_r.at[b, 9])
+        yb[...] = (dense_rows(b, y) + yb[...].astype(f32)).astype(bf16)
+        send(("home", b), None, yb, xb, b_s.at[b, 10], b_r.at[b, 10], X)
+
+    def home_rows(b):
+        yb, xb, cb = boxes[b][4:7]
+        got(xb, b_r.at[b, 10])
+        xb[...] += yb[...]
+        send(("home", b), None, xb.at[pl.ds(al((1 - c) * 32, 32), 32)], cb, b_s.at[b, 11], b_r.at[b, 11], C)
+
+    def home_last(b):
+        xb, cb = boxes[b][5:7]
+        s0, ns, first, half = boxes[b][7]
+        got(cb, b_r.at[b, 11])
+        here, there = xb[pl.ds(al(c * 32, 32), 32)].astype(f32), cb[...].astype(f32)
+        low, high = jnp.where(c == 0, here, there), jnp.where(c == 0, there, here)
+        for s in range(ns):
+            lanes = slice(s * 128, s * 128 + 128)
+            split_sum[s0 + s] = jnp.concatenate([low[:, lanes], high[:, lanes]], axis=1)
+        for w in range(half):
+            lanes = slice(ns * 128 + w * 256, ns * 128 + w * 256 + 256)
+            for q in range(4):
+                wz[q, first + w] = low[q * 8 : q * 8 + 8, lanes]
+                wz[q, first + half + w] = high[q * 8 : q * 8 + 8, lanes]
+        slots = pl.ds(first, 2 * half)
+        for k, j in enumerate(others):
+            send(("home", b), None, wz.at[j, slots], whole_sum.at[z, slots], b_s.at[b, 12 + k], b_r.at[b, 12 + z], {"tp": j})
+        pltpu.make_async_copy(wz.at[z, slots], whole_sum.at[z, slots], loc.at[count + 18 + b]).start()
+
+    def home_done(b):
+        first, half = boxes[b][7][2:]
+        slots = pl.ds(first, 2 * half)
+        for j in others:
+            got(whole_sum.at[j, slots], b_r.at[b, 12 + j])
+        pltpu.make_async_copy(wz.at[z, slots], whole_sum.at[z, slots], loc.at[count + 18 + b]).wait()
+
+    def rows_back(src, dst, slot):
+        def go():
+            for k, j in enumerate(others):
+                part = src.at[pl.ds(al(j * 112, 16), 112)]
+                remote(part, dst.at[lax.rem(z, 2)], home_s.at[slot, k], home_r.at[slot, z], {"tp": j}).start()
+            own_part(src, dst, slot).start()
+
+        when(mine, go)
+
+    def own_part(src, dst, slot):
+        part = src.at[pl.ds(al(z * 112, 16), 112)]
+        return pltpu.make_async_copy(part, dst.at[lax.rem(z, 2)], loc.at[count + 21 + slot])
+
+    def rows_back_done(src, dst, slot):
+        def go():
+            for k, j in enumerate(others):
+                part = src.at[pl.ds(al(j * 112, 16), 112)]
+                remote(part, part, home_s.at[slot, k], home_r.at[slot, z], {"tp": j}).wait_send()
+            own_part(src, dst, slot).wait()
+
+        when(mine, go)
+        for i in (0, 1):
+            source = 2 * c + i
+            when(source != z, lambda: got(dst.at[i], home_r.at[slot, source]))
+
+    def enc_dst(quarter_of):
+        return g_enc.at[lax.rem(z, 2), :, pl.ds(al(c * 512, 512), 512)]
+
+    def enc_copy(j):
+        part = k1.at[pl.ds(al(j * 384, 128), 384)]
+        owner = z // 2
+        sems = home_s.at[2, j], home_r.at[2 + c, z]
+        return part, owner, sems
+
+    def enc_back(j):
+        part, owner, (s, r) = enc_copy(j)
+        when((j != z) | (c != owner), lambda: remote(part, enc_dst(j), s, r, {"tp": j, "core": owner}).start())
+        when((j == z) & (c == owner), lambda: pltpu.make_async_copy(part, enc_dst(j), loc.at[count + 23]).start())
+
+    def enc_back_done():
+        for j in range(4):
+            part, owner, (s, r) = enc_copy(j)
+            when((j != z) | (c != owner), lambda: remote(part, enc_dst(j), s, r, {"tp": j, "core": owner}).wait_send())
+            when((j == z) & (c == owner), lambda: pltpu.make_async_copy(part, enc_dst(j), loc.at[count + 23]).wait())
+        for i in (0, 1):
+            for other in (0, 1):
+                source = 2 * c + i
+                when(
+                    (source != z) | (c != other),
+                    lambda: got(g_enc.at[i, :, other * 512 : other * 512 + 512], home_r.at[2 + other, source]),
+                )
+
+    def rank_pair(side, i, u, g):
+        s0, w0 = (12, 6) if side == 0 else (8, 2)
+        m = 3 * side + i
+        inner = rank_t(whole(m), u[...])
+        back = rank_t(split(m), g[...])
+        gsplit[s0 + i] = nn(inner, g[...]).astype(bf16)
+        gwhole[w0 + i] = nn(back, u[...]).astype(bf16)
+
+    def rank_out(side):
+        s0, w0 = (12, 6) if side == 0 else (8, 2)
+        gsplit[s0 + 3] = nn(rank_t(whole(7 + side), grads[...]), mix[side]).astype(bf16)
+        gwhole[w0 + 3] = nn(rank_t(split(10 + side), mix[side]), grads[...]).astype(bf16)
+
+    def memory_half(h, place):
+        rows_of = [pl.ds(al(m * 1024 + h * 512, 512), 512) for m in (4, 5)]
+        return nt(dk1[place], ga[rows_of[0]]) + nt(dv1[place], ga[rows_of[1]])
+
+    quarters = [slice(q * 384, q * 384 + 384) for q in range(4)]
+    dk1, dv1 = ga.at[pl.ds(6144, 1536)], ga.at[pl.ds(7680, 1536)]
+    dk0, dv0 = dkv.at[0, 0:448], dkv.at[1, 0:448]
     part_out(3, 0)
-    gwhole[6] = nn(r_in[...].astype(bf16), normed[2]).astype(bf16)
-    gwhole[9] = nn(t_out[...].astype(bf16), grads[...]).astype(bf16)
+    gwhole[0] = nn(r_in[...].astype(bf16), normed[2]).astype(bf16)
+    gwhole[1] = nn(t_out[...].astype(bf16), grads[...]).astype(bf16)
+    home_core(0)
     g_now[...] = grads[...].astype(f32) + norm_back(hidden[1], gain[2], part_sum(3, 0))
     part_out(2, 1)
     settle("rows")
     grads[...] = g_now[...].astype(bf16)
     do[...] = nt(grads[...], wb(1)).astype(bf16)
-    dk1, dv1 = ga.at[pl.ds(6144, 1536)], ga.at[pl.ds(7680, 1536)]
-    attend_backward(q1, k1, v1, do, lse.at[1], dq, dk1, dv1, frames, False)
+    home_z(0)
+    attend_backward(q1, k1, v1, do, lse.at[1], dq, dk1, dv1, frames, False, 0, 2, groups)
+    normed[2] = (hidden[1] + part_sum(2, 1)).astype(bf16)
+    rows_back(normed.at[2], acts, 0)
+    rank_out(1)
+    home_y(0)
+    attend_backward(q1, k1, v1, do, lse.at[1], dq, dk1, dv1, frames, False, 2, 2, groups)
     settle(("part", 3))
     outbox[0] = nt(dq[...], wa(3))
-    normed[2] = (hidden[1] + part_sum(2, 1)).astype(bf16)
-    to_hbm(normed.at[2], result, 0).start()
     part_out(4, 0)
-
-    def ranks(side, source, dk, dv):
-        for i, (u, g) in enumerate(((normed.at[side], dq), (source, dk), (source, dv))):
-            m = 3 * side + i
-            held = g[: u.shape[0]]
-            inner = rank_t(whole(m), u[...])
-            back = rank_t(split(m), held)
-            gsplit[m] = nn(inner, held).astype(bf16)
-            gwhole[m] = nn(back, u[...]).astype(bf16)
-        gsplit[10 + side] = nn(rank_t(whole(7 + side), grads[...]), mix[side]).astype(bf16)
-        gwhole[7 + side] = nn(rank_t(split(10 + side), mix[side]), grads[...]).astype(bf16)
-
-    def memory_half(h, place):
-        rows_of = [pl.ds(al(m * 1024 + h * 512, 512), 512) for m in (4, 5)]
-        return nt(dk1[place], ga[rows_of[0]]) + nt(dv1[place], ga[rows_of[1]])
-
-    thirds = [slice(b * 512, b * 512 + 512) for b in range(3)]
-    for place in thirds:
+    for place in quarters:
         k1[place] = memory_half(1 - c, place).astype(bf16)
-    ranks(1, memory, dk1, dv1)
-    g_now[...] += norm_back(hidden[0], gain[1], part_sum(4, 0))
+    home_x(0)
+    grad_part = part_sum(4, 0)
     send("memory", None, k1, v1, ex_s.at[6], ex_r.at[6], C)
+    g_now[...] += norm_back(hidden[0], gain[1], grad_part)
     grads[...] = g_now[...].astype(bf16)
     do[...] = nt(grads[...], wb(0)).astype(bf16)
-    attend_backward(q0, k0, v0, do, lse.at[0], dq, dkv.at[0], dkv.at[1], rows.shape[0], True)
+    got(v1, ex_r.at[6])
+    settle("memory")
+    for q, place in enumerate(quarters):
+        k1[place] = (memory_half(c, place) + v1[place].astype(f32)).astype(bf16)
+        enc_back(q)
+    rank_pair(1, 0, normed.at[1], dq)
+    home_rows(0)
+    attend_backward(q0, k0, v0, do, lse.at[0], dq, dk0, dv0, rows.shape[0], True)
     settle(("part", 2))
     outbox[1] = nt(dq[...], wa(0))
-    outbox[1] += nt(dkv[0], wa(1))
-    outbox[1] += nt(dkv[1], wa(2))
+    outbox[1] += nt(dk0[...], wa(1))
+    outbox[1] += nt(dv0[...], wa(2))
     part_out(5, 1)
-    got(v1, ex_r.at[6])
-    settle("memory")
-    for place in thirds:
-        k1[place] = (memory_half(c, place) + v1[place].astype(f32)).astype(bf16)
-    to_hbm(k1, g_memory, 1).start()
-    ranks(0, normed.at[0], dkv.at[0], dkv.at[1])
-    normed[1] = (g_now[...] + norm_back(rows[...].astype(f32), gain[0], part_sum(5, 1))).astype(bf16)
-    to_hbm(normed.at[1], g_rows, 2).start()
-    for src, dst, slot in ((normed.at[2], result, 0), (k1, g_memory, 1), (normed.at[1], g_rows, 2)):
-        to_hbm(src, dst, slot).wait()
+    home_last(0)
+    rank_pair(0, 0, normed.at[0], dq)
+    rank_pair(0, 1, normed.at[0], dk0)
+    rank_pair(0, 2, normed.at[0], dv0)
+    rank_out(0)
+    home_core(2)
+    normed[0] = (g_now[...] + norm_back(rows[...].astype(f32), gain[0], part_sum(5, 1))).astype(bf16)
+    rows_back(normed.at[0], g_tok, 1)
+    home_z(2)
+    rank_pair(1, 1, memory, dk1)
+    rank_pair(1, 2, memory, dv1)
+    home_core(1)
+    home_y(2)
+    home_z(1)
+    home_x(2)
+    home_y(1)
+    home_rows(2)
+    home_x(1)
+    home_last(2)
+    home_rows(1)
+    home_last(1)
+    for b in range(3):
+        home_done(b)
+    rows_back_done(normed.at[2], acts, 0)
+    rows_back_done(normed.at[0], g_tok, 1)
+    enc_back_done()
     for key in list(sent):
         settle(key)
 
@@ -763,31 +941,40 @@
 def layer(tok, enc, cot, w_in, w_out, w_up, w_down, ids, gain, shift, *adapters):
     any_ = pl.BlockSpec(memory_space=pl.ANY)
     r, d = 448, tok.shape[2]
-    frames = enc.shape[1]
-    padded = -(-frames // 512) * 512
+    padded = enc.shape[1]
     dma = pltpu.SemaphoreType.DMA
 
     def vm(*shape, dtype=bf16):
         return pltpu.VMEM(shape, dtype)
 
     n = 16
+    halves = (1, 2, 2)
+    splits = (8, 4, 4)
+    widths = [s * 128 + w * 256 for s, w in zip(splits, halves, strict=True)]
     return pl.pallas_call(
         layer_kernel,
-        out_shape=[sds((r, d), bf16), sds((r, d), bf16), sds((padded, d // 2), bf16), sds((16, 16, 512), bf16), sds((10, 16, d), bf16)],
+        out_shape=[
+            sds((2, r // 4, d), bf16), sds((2, r // 4, d), bf16), sds((2, padded // 4, d), bf16),
+            sds((16, 32, 256), f32), sds((4, 10, 8, 256), f32),
+        ],
         in_specs=[any_] * 7 + [VM] * 11,
-        out_specs=[any_] * 3 + [VM] * 2,
+        out_specs=[any_] * 3 + [VM, any_],
         scratch_shapes=[
-            vm(10 * d, 512), vm(6, 4, 128, d), vm(r, d), vm(r, d), vm(frames, d), vm(3, r, d),
+            vm(10 * d, 512), vm(6, 4, 128, d), vm(r, d), vm(r, d), vm(padded, d), vm(3, r, d),
             vm(r, 512), vm(r, 512), vm(r, 512), vm(2, r, 512), vm(r, 512), vm(padded, 512), vm(padded, 512),
-            vm(2, 4, 2, r, dtype=f32), vm(2, r, d, dtype=f32), vm(r, d, dtype=f32), vm(r, 512), vm(r, 512), vm(2, r, 512),
+            vm(2, 4, 2, r, dtype=f32), vm(2, r, d, dtype=f32), vm(r, d, dtype=f32), vm(2, r, 512), vm(2, 512, 512),
             vm(2, r, d, dtype=f32), vm(2, r, d, dtype=f32),
-            vm(4, 8, 128, dtype=f32), vm(2, 128, 2048), vm(2, 32, 5120), vm(128, 2048), vm(32, 5120), vm(64, 2048), vm(16, 5120),
+            vm(4, 8, 128, dtype=f32), vm(512, 512), vm(320, 512), vm(64, 2048), vm(16, 5120), vm(2, 64, 2048), vm(2, 16, 5120),
             vm(4, 16, 2048), vm(2, 16, 5120), vm(16, r, dtype=f32), vm(16, r, dtype=f32), vm(2, 16, r),
+            vm(16, 16, 512), vm(10, 16, d), vm(4, 10, 8, 256, dtype=f32),
+            *[vm(w, 16, d) for w in halves], *[vm(4, s, 16, 128) for s in splits], *[vm(4, w, 16, 256) for w in halves],
+            *[vm(64, w) for w in widths], *[vm(64, w) for w in widths], *[vm(64, w) for w in widths], *[vm(32, w) for w in widths],
             dma((n,)), dma((n,)), dma((n, 4)), dma((n, 4)), dma((n, 4)), dma((n,)), dma((n,)), dma((n, 2)), dma((n, 2)),
-            dma((3, 16)), dma((3, 16)), dma((n + 21,)), dma((12,)), dma((12,)), dma((7,)), dma((7,)),
+            dma((3, 16)), dma((3, 16)), dma((n + 24,)), dma((12,)), dma((12,)), dma((7,)), dma((7,)),
+            dma((3, 16)), dma((3, 16)), dma((4, 4)), dma((4, 4)),
         ],
         compiler_params=pltpu.CompilerParams(
-            collective_id=1, has_side_effects=True, vmem_limit_bytes=61 * 1024 * 1024
+            collective_id=1, has_side_effects=True, vmem_limit_bytes=int(62.5 * 1024 * 1024)
         ),
         name="layer",
     )(tok, enc, cot, w_in, w_out, w_up, w_down, ids, gain, shift, *adapters)
@@ -982,20 +1169,45 @@
         return rows.reshape(6, *rows.shape[3:])
 
     lines = jnp.pad(adapter_of.astype(f32), (0, 6))[:, None] * jnp.ones((1, 128), f32)
-    outs = layer(
-        tokens, encoded, cotangent, six(w_attn_in), w_attn_out[0], w_up[0], w_down[0], lines,
+    _, frames, d = encoded.shape
+    step = frames // 4
+    spaced = jnp.pad(encoded.reshape(2, 4, step, d), ((0, 0), (0, 0), (0, 384 - step), (0, 0)))
+    spaced = spaced.reshape(2, 1536, d)
+    acts, g_tok, g_enc, split_sum, whole_sum = layer(
+        tokens, spaced, cotangent, six(w_attn_in), w_attn_out[0], w_up[0], w_down[0], lines,
         norm_gain[0][:, None], norm_shift[0][:, None], six(down_attn_in), six(up_attn_in), down_feed_in[0],
         up_feed_in[0], down_attn_out[0], up_attn_out[0], down_feed_out[0], up_feed_out[0],
     )
-    here = in_core_order(adapter_of, swap_core(adapter_of)).reshape(4)
-    return (*outs[:2], outs[2][: encoded.shape[1]], *outs[3:], here)
+    held = split_sum.shape[1]
+
+    def wide_of(first):
+        block = split_sum[first : first + 4].reshape(4, held, 2, 128)
+        return jnp.moveaxis(block, 0, 2).reshape(1, held, 1024)
+
+    whole = jnp.moveaxis(whole_sum, 0, 2).reshape(10, whole_sum.shape[2], d)
+    cross_side, self_side = split_sum[8:12], split_sum[12:16]
+    return (
+        acts,
+        g_tok.astype(f32),
+        g_enc[:, :step].astype(f32),
+        jnp.stack([whole[6:9], whole[2:5]])[None],
+        jnp.stack([self_side[:3], cross_side[:3]])[None],
+        whole[0:1],
+        wide_of(0),
+        jnp.stack([self_side[3], cross_side[3]])[None],
+        jnp.stack([whole[9], whole[5]])[None],
+        wide_of(4),
+        whole[1:2],
+    )
 
 
 def on_device(*args):
+    if lax.axis_size("sh") == 2:
+        return narrow_parts(args)
     n, tp = lax.axis_size("sh"), lax.axis_size("tp")
     held_rows, quarter = args[12].shape[1], args[11].shape[4]
     width, piece = quarter * tp, quarter // 2
-    result, grad, memory_rows, split_grads, whole_grads, here = (narrow_parts if n == 2 else wide_parts)(args)
+    result, grad, memory_rows, split_grads, whole_grads, here = wide_parts(args)
     activations = rows_home(half_columns(result))
     grad_encoded = rows_home(memory_rows).astype(f32)
     grad_tokens = rows_home(half_columns(grad)).astype(f32)

time: 347 us -> 307 us (0.88)
  the two profiles are of different devices: /device:TPU:0 before, /device:TPU:1 now
where the time goes in v4:
time: 307 us; the launch traced here: 301 us
  Pallas kernels  276 us (90%)
  local copies, waits for them, and re-layouts  19.9 us (6%)
  other arithmetic  4.04 us (1%)
    pallas_call x1, Pallas kernels, layer(): pl.pallas_call(layer_kernel, out_shape=[sds((2, r // 4, d), bf16), sds((2...  276 us

profile of v4, /device:TPU:1, one launch (start us, length us, event | category | flops | bytes accessed | tf_op | source)
XLA Modules:
  0.0 300.7 jit_solution(149378696352777003)
XLA Ops:
  0.6 4.7 %copy.33 = bf16[2,4,375,1024]{3,2,1,0:T(8,128)(2,1)S(1)} copy(bf16[2,4,375,1024]{3,0,2,1:T(2,128)(2,1)} %bitcast.36) | data formatting | bytes 12288000 | tf_op jit(solution)/shard_map/reshape | solution.py:1174
  5.4 3.4 %pad.8 = bf16[2,4,384,1024]{3,2,1,0:T(8,128)(2,1)} pad(bf16[2,4,375,1024]{3,2,1,0:T(8,128)(2,1)S(1)} %copy.33, bf16[]{:T(256)} %constant.3.clone.1), padding=0_0x0_0x0_9x0_0 | pad | bytes 12435458 | tf_op jit(solution)/shard_map/jit(_pad)/pad | solution.py:1174
  8.8 0.7 mul.2.ids
  9.5 275.6 %layer.1 = (bf16[2,112,1024]{2,1,0:T(8,128)(2,1)}, bf16[2,112,1024]{2,1,0:T(8,128)(2,1)}, bf16[2,384,1024]{2,1,0:T(8,128)(2,1)}, f32[16,32,256]{2,1,0:T(8,128)}, f32[4,10,8,256]{3,2,1,0:T(8,128)}) custom-call(bf16[2,112,1024]{2,1,0:T(8,128)(2,1)} %tok.1, bf16[2,1536,1024]{2,1,0:T(8,128)(2,1)} %bitcast.35, bf16[2,112,1024]{2,1,0:T(8,128)(2,1)} %cot.1, ...), custom_call_target="tpu_custom_call" | custom-call | tf_op jit(solution)/shard_map/layer/pallas_call | solution.py:954
  285.1 1.6 fusion.2
  286.7 0.6 maximum_bitcast_fusion.3
  287.3 0.8 fusion.1
  288.1 0.6 maximum_bitcast_fusion.2
  288.7 1.0 slice_bitcast_fusion.1
  289.7 0.7 maximum_bitcast_fusion.1
  290.4 1.0 fusion.3
  291.4 0.1 stack.24
  291.5 0.1 stack.25
  291.6 0.7 maximum_bitcast_fusion
  292.3 0.1 reshape.64
  292.3 0.1 copy.36
  292.4 0.7 reshape.65
  293.2 0.1 reshape.66
  293.2 0.1 copy.37
  293.3 0.7 reshape.67
  294.0 0.4 slice_convert_fusion
  294.4 4.0 %copy.38 = f32[2,375,1024]{2,0,1:T(2,128)} copy(f32[2,375,1024]{2,1,0:T(8,128)S(1)} %slice_convert_fusion) | data formatting | bytes 6144000
  298.4 1.0 convert_element_type.14
  299.5 0.8 copy.40
  (15 shorter events, 0.1 us)
Async XLA Ops:
  5.4 3.5 %copy-start.4 = (s32[2]{0:T(128)S(1)}, s32[2]{0:T(128)}, u32[]{:S(2)}) copy-start(s32[2]{0:T(128)} %param.21) | copy-start | bytes 28
  285.1 7.2 %copy-start.1 = (f32[16,32,256]{2,1,0:T(8,128)S(1)}, f32[16,32,256]{2,1,0:T(8,128)}, u32[]{:S(2)}) copy-start(f32[16,32,256]{2,1,0:T(8,128)} %get-tuple-element.20) | copy-start | bytes 1572868
  285.1 8.9 %copy-start = (bf16[2,384,1024]{2,1,0:T(8,128)(2,1)S(1)}, bf16[2,384,1024]{2,1,0:T(8,128)(2,1)}, u32[]{:S(2)}) copy-start(bf16[2,384,1024]{2,1,0:T(8,128)(2,1)} %get-tuple-element.18) | copy-start | bytes 4718596
  294.4 4.0 %copy-start.3 = (bf16[2,112,1024]{2,1,0:T(8,128)(2,1)S(1)}, bf16[2,112,1024]{2,1,0:T(8,128)(2,1)}, u32[]{:S(2)}) copy-start(bf16[2,112,1024]{2,1,0:T(8,128)(2,1)} %get-tuple-element.17) | copy-start | bytes 1376260
  294.4 5.0 %copy-start.2 = (bf16[2,112,1024]{2,1,0:T(8,128)(2,1)S(1)}, bf16[2,112,1024]{2,1,0:T(8,128)(2,1)}, u32[]{:S(2)}) copy-start(bf16[2,112,1024]{2,1,0:T(8,128)(2,1)} %get-tuple-element.66) | copy-start | bytes 1376260
